TPU v7x, 512 devices: a whole 4x8x8 slice. The times are simulated.
512 devices in a mesh: sec: 32 (over y, x), ch: 16 (over z, core).
Axes of the slice: x: 4, y: 8, z: 8, core: 2. Of those that a mesh axis runs over, the one named last changes fastest.
Arguments:
- start_amps: bfloat16 [6, 1024, 2048], P(None, 'ch'), may hold values from -6 to 6
- energies: float32 [6], replicated, may hold values from 0.5 to 2
- thresholds: bfloat16 [32, 1024], P('sec', 'ch'), may hold values from -3 to -1
- intersection: bfloat16 [32, 1024, 1024], P('sec', 'ch'), may hold values from -0.2 to 1
Outputs:
- boundary_amps: bfloat16 [32, 6, 1024, 2048], P('sec', None, 'ch')
All inputs are finite; a program needn't handle non-finite values.
Results may differ from a plain program's by a relative error of at most 0.04.
Values may be sent and summed in bfloat16 or wider, within the bound.
No kernel may reach another device: no remote copies, remote signals or barrier semaphores. Data moves between devices by JAX's collectives and lax.ppermute only.
A program may use at most 64 MiB of HBM per device.

v0:
```python
import math

import jax
import jax.numpy as jnp
from jax import lax
from jax.sharding import PartitionSpec as P


def side_by_side(arrays, axis, dim, along):
    widths = [math.prod(a.shape[along:]) for a in arrays]
    both = jnp.concatenate(
        [a.reshape(*a.shape[:along], w) for a, w in zip(arrays, widths)], axis=along
    )
    out = lax.all_gather(both, axis, axis=dim, tiled=True)
    tiles = jnp.split(out, [sum(widths[:k]) for k in range(1, len(widths))], axis=along)
    return tuple((b.reshape(*out.shape[:along], *a.shape[along:]) for a, b in zip(arrays, tiles)))


def passed_along(value, axis, steps):
    count = lax.axis_size(axis)
    leading, last = (max(0, -steps), min(count, count - steps))
    return lax.ppermute(value, axis, [(source, source + steps) for source in range(leading, last)])


def per_device(start_amps, energies, thresholds, intersection):
    sectors = lax.axis_size("sec")
    sector_index = lax.axis_index("sec")
    groups = lax.axis_size("ch")
    energy_count = energies.shape[0]
    step_count = sectors + energy_count - 1
    row_count = intersection.shape[1]
    width_cols = start_amps.shape[2]
    half_cols = width_cols // 2
    col_width = half_cols // groups
    intersection_whole, thresholds_whole = side_by_side((intersection, thresholds), "ch", 1, 2)
    basis_change = intersection_whole[0]
    channel_thresholds = thresholds_whole[0].astype(jnp.float32)
    channel_count = basis_change.shape[0]
    paired = start_amps.reshape(energy_count, row_count, 2, half_cols)
    start_cols = lax.all_to_all(paired, "ch", split_axis=3, concat_axis=1, tiled=True)
    stored_init = jnp.zeros((energy_count, channel_count, 2, col_width), jnp.bfloat16)

    def multiply(flat):
        return jnp.dot(basis_change, flat, preferred_element_type=jnp.float32).astype(jnp.bfloat16)

    def skipped(flat):
        return jnp.zeros((channel_count, 2 * col_width), jnp.bfloat16)

    def step(step_index, state_pair):
        outgoing, stored = state_pair
        incoming = passed_along(outgoing, "sec", 1)
        energy_raw = step_index - sector_index
        active = (energy_raw >= 0) & (energy_raw < energy_count)
        energy_slot = jnp.clip(energy_raw, 0, energy_count - 1)
        initial = lax.dynamic_index_in_dim(start_cols, energy_slot, 0, keepdims=False)
        source = jnp.where(sector_index == 0, initial, incoming).astype(jnp.float32)
        wavenumber = jnp.sqrt(energies[energy_slot] - channel_thresholds)[:, None]
        values_part = source[:, 0, :]
        slopes_part = source[:, 1, :]
        cosine = jnp.cos(wavenumber)
        sine_term = jnp.sin(wavenumber)
        new_values = cosine * values_part + sine_term / wavenumber * slopes_part
        new_slopes = -wavenumber * sine_term * values_part + cosine * slopes_part
        rotated = jnp.stack([new_values, new_slopes], axis=1).astype(jnp.bfloat16)
        flat = rotated.reshape(channel_count, 2 * col_width)
        fresh = lax.cond(active, multiply, skipped, flat)
        fresh = fresh.reshape(channel_count, 2, col_width)
        previous = lax.dynamic_index_in_dim(stored, energy_slot, 0, keepdims=False)
        kept = jnp.where(active, fresh, previous)
        stored = lax.dynamic_update_index_in_dim(stored, kept, energy_slot, 0)
        return (fresh, stored)

    outgoing_init = jnp.zeros((channel_count, 2, col_width), jnp.bfloat16)
    final_pair = lax.fori_loop(0, step_count, step, (outgoing_init, stored_init))
    returned = lax.all_to_all(final_pair[1], "ch", split_axis=1, concat_axis=3, tiled=True)
    return returned.reshape(energy_count, row_count, width_cols)[None]


def solution(mesh):
    in_specs = (P(None, "ch", None), P(), P("sec", "ch"), P("sec", "ch", None))
    out_specs = P("sec", None, "ch", None)
    return jax.shard_map(
        per_device, mesh=mesh, in_specs=in_specs, out_specs=out_specs, check_vma=False
    )
```

profile of v0, /device:TPU:33, one launch (start us, length us, event | category | flops | bytes accessed | tf_op | source)
XLA Modules:
  0.0 773.9 jit_solution(15608727686123887330)
XLA Ops:
  12.7 7.8 %copy.21 = bf16[6,64,2,1024]{1,2,0,3:T(2,128)(2,1)S(1)} copy(bf16[6,64,2,1024]{3,2,1,0:T(2,128)(2,1)} %reshape.109) | data formatting | bytes 3145728 | tf_op jit(solution)/shard_map/reshape | solution.py:39
  23.8 11.0 %all-to-all-start = ((bf16[16,2,24576]{2,1,0:T(2,128)(2,1)}), bf16[16,2,24576]{2,1,0:T(2,128)(2,1)}, u32[]{:S(2)}, u32[]{:S(2)}) async-start(bf16[16,2,24576]{2,1,0:T(2,128)(2,1)} %reshape.112), calls=%async_computation | async-start | bytes 3145728 | tf_op jit(solution)/shard_map/all_to_all | solution.py:40
  34.8 45.2 %all-to-all-done = bf16[16,2,24576]{2,1,0:T(2,128)(2,1)} async-done(((bf16[16,2,24576]{2,1,0:T(2,128)(2,1)}), bf16[16,2,24576]{2,1,0:T(2,128)(2,1)}, u32[]{:S(2)}, u32[]{:S(2)}) %all-to-all-start) | async-done | bytes 1572896 | tf_op jit(solution)/shard_map/all_to_all | solution.py:40
  97.7 559.2 %while.16 = (s32[]{:T(128)}, bf16[1024,2,64]{0,2,1:T(8,128)(2,1)}, bf16[6,1024,2,64]{1,3,2,0:T(8,128)(2,1)}, s32[]{:T(128)}, f32[6]{0:T(128)S(1)}, /*index=5*/f3...) while((s32[]{:T(128)}, bf16[1024,2,64]{0,2,1:T(8,128)(2,1)}, ...), condition=%wide.region_3.4_spmd, body=%wide.region_0.3_spmd.sunk | while | flops 269619200 | bytes 7368989 | solution.py:74
  102.1 8.2 %collective-permute-done = bf16[1024,2,64]{0,2,1:T(8,128)(2,1)S(1)} collective-permute-done((bf16[1024,2,64]{0,2,1:T(8,128)(2,1)}, bf16[1024,2,64]{0,2,1:T(8,128)(2,1)S(1)}, u32[]{:S(2)}, u32[]{:S(2)}) %collective-permute-start) | collective-permute-done | bytes 262176 | tf_op jit(solution)/shard_map/while/body/eval_jaxpr/ppermute | solution.py:22
  117.2 8.6 %collective-permute-done = bf16[1024,2,64]{0,2,1:T(8,128)(2,1)S(1)} collective-permute-done((bf16[1024,2,64]{0,2,1:T(8,128)(2,1)}, bf16[1024,2,64]{0,2,1:T(8,128)(2,1)S(1)}, u32[]{:S(2)}, u32[]{:S(2)}) %collective-permute-start) | collective-permute-done | bytes 262176 | tf_op jit(solution)/shard_map/while/body/eval_jaxpr/ppermute | solution.py:22
  132.5 7.4 collective-permute-done
  146.8 7.4 collective-permute-done
  161.0 7.4 collective-permute-done
  175.3 7.4 collective-permute-done
  189.5 7.4 collective-permute-done
  203.7 7.4 collective-permute-done
  218.0 7.4 collective-permute-done
  246.5 7.4 collective-permute-done
  260.7 8.0 %collective-permute-done = bf16[1024,2,64]{0,2,1:T(8,128)(2,1)S(1)} collective-permute-done((bf16[1024,2,64]{0,2,1:T(8,128)(2,1)}, bf16[1024,2,64]{0,2,1:T(8,128)(2,1)S(1)}, u32[]{:S(2)}, u32[]{:S(2)}) %collective-permute-start) | collective-permute-done | bytes 262176 | tf_op jit(solution)/shard_map/while/body/eval_jaxpr/ppermute | solution.py:22
  275.5 9.1 %collective-permute-done = bf16[1024,2,64]{0,2,1:T(8,128)(2,1)S(1)} collective-permute-done((bf16[1024,2,64]{0,2,1:T(8,128)(2,1)}, bf16[1024,2,64]{0,2,1:T(8,128)(2,1)S(1)}, u32[]{:S(2)}, u32[]{:S(2)}) %collective-permute-start) | collective-permute-done | bytes 262176 | tf_op jit(solution)/shard_map/while/body/eval_jaxpr/ppermute | solution.py:22
  291.5 10.5 %collective-permute-done = bf16[1024,2,64]{0,2,1:T(8,128)(2,1)S(1)} collective-permute-done((bf16[1024,2,64]{0,2,1:T(8,128)(2,1)}, bf16[1024,2,64]{0,2,1:T(8,128)(2,1)S(1)}, u32[]{:S(2)}, u32[]{:S(2)}) %collective-permute-start) | collective-permute-done | bytes 262176 | tf_op jit(solution)/shard_map/while/body/eval_jaxpr/ppermute | solution.py:22
  308.8 9.7 %collective-permute-done = bf16[1024,2,64]{0,2,1:T(8,128)(2,1)S(1)} collective-permute-done((bf16[1024,2,64]{0,2,1:T(8,128)(2,1)}, bf16[1024,2,64]{0,2,1:T(8,128)(2,1)S(1)}, u32[]{:S(2)}, u32[]{:S(2)}) %collective-permute-start) | collective-permute-done | bytes 262176 | tf_op jit(solution)/shard_map/while/body/eval_jaxpr/ppermute | solution.py:22
  325.3 8.8 %collective-permute-done = bf16[1024,2,64]{0,2,1:T(8,128)(2,1)S(1)} collective-permute-done((bf16[1024,2,64]{0,2,1:T(8,128)(2,1)}, bf16[1024,2,64]{0,2,1:T(8,128)(2,1)S(1)}, u32[]{:S(2)}, u32[]{:S(2)}) %collective-permute-start) | collective-permute-done | bytes 262176 | tf_op jit(solution)/shard_map/while/body/eval_jaxpr/ppermute | solution.py:22
  340.9 7.8 %collective-permute-done = bf16[1024,2,64]{0,2,1:T(8,128)(2,1)S(1)} collective-permute-done((bf16[1024,2,64]{0,2,1:T(8,128)(2,1)}, bf16[1024,2,64]{0,2,1:T(8,128)(2,1)S(1)}, u32[]{:S(2)}, u32[]{:S(2)}) %collective-permute-start) | collective-permute-done | bytes 262176 | tf_op jit(solution)/shard_map/while/body/eval_jaxpr/ppermute | solution.py:22
  357.3 8.6 %collective-permute-done = bf16[1024,2,64]{0,2,1:T(8,128)(2,1)S(1)} collective-permute-done((bf16[1024,2,64]{0,2,1:T(8,128)(2,1)}, bf16[1024,2,64]{0,2,1:T(8,128)(2,1)S(1)}, u32[]{:S(2)}, u32[]{:S(2)}) %collective-permute-start) | collective-permute-done | bytes 262176 | tf_op jit(solution)/shard_map/while/body/eval_jaxpr/ppermute | solution.py:22
  374.4 7.4 collective-permute-done
  390.4 7.4 collective-permute-done
  406.3 7.4 collective-permute-done
  422.3 7.4 collective-permute-done
  438.3 7.4 collective-permute-done
  495.2 8.6 %collective-permute-done = bf16[1024,2,64]{0,2,1:T(8,128)(2,1)S(1)} collective-permute-done((bf16[1024,2,64]{0,2,1:T(8,128)(2,1)}, bf16[1024,2,64]{0,2,1:T(8,128)(2,1)S(1)}, u32[]{:S(2)}, u32[]{:S(2)}) %collective-permute-start) | collective-permute-done | bytes 262176 | tf_op jit(solution)/shard_map/while/body/eval_jaxpr/ppermute | solution.py:22
  510.6 9.7 %collective-permute-done = bf16[1024,2,64]{0,2,1:T(8,128)(2,1)S(1)} collective-permute-done((bf16[1024,2,64]{0,2,1:T(8,128)(2,1)}, bf16[1024,2,64]{0,2,1:T(8,128)(2,1)S(1)}, u32[]{:S(2)}, u32[]{:S(2)}) %collective-permute-start) | collective-permute-done | bytes 262176 | tf_op jit(solution)/shard_map/while/body/eval_jaxpr/ppermute | solution.py:22
  527.1 10.0 %collective-permute-done = bf16[1024,2,64]{0,2,1:T(8,128)(2,1)S(1)} collective-permute-done((bf16[1024,2,64]{0,2,1:T(8,128)(2,1)}, bf16[1024,2,64]{0,2,1:T(8,128)(2,1)S(1)}, u32[]{:S(2)}, u32[]{:S(2)}) %collective-permute-start) | collective-permute-done | bytes 262176 | tf_op jit(solution)/shard_map/while/body/eval_jaxpr/ppermute | solution.py:22
  543.8 9.1 %collective-permute-done = bf16[1024,2,64]{0,2,1:T(8,128)(2,1)S(1)} collective-permute-done((bf16[1024,2,64]{0,2,1:T(8,128)(2,1)}, bf16[1024,2,64]{0,2,1:T(8,128)(2,1)S(1)}, u32[]{:S(2)}, u32[]{:S(2)}) %collective-permute-start) | collective-permute-done | bytes 262176 | tf_op jit(solution)/shard_map/while/body/eval_jaxpr/ppermute | solution.py:22
  559.7 8.1 %collective-permute-done = bf16[1024,2,64]{0,2,1:T(8,128)(2,1)S(1)} collective-permute-done((bf16[1024,2,64]{0,2,1:T(8,128)(2,1)}, bf16[1024,2,64]{0,2,1:T(8,128)(2,1)S(1)}, u32[]{:S(2)}, u32[]{:S(2)}) %collective-permute-start) | collective-permute-done | bytes 262176 | tf_op jit(solution)/shard_map/while/body/eval_jaxpr/ppermute | solution.py:22
  667.3 85.1 %all_to_all.33 = bf16[16,2,24576]{2,1,0:T(2,128)(2,1)} all-to-all(bf16[16,2,24576]{2,1,0:T(2,128)(2,1)} %reshape.114), channel_id=1, replica_groups=mesh['sec'=32,'ch'=16] {'ch'}, dimensions={0} | all-to-all | bytes 3145728 | tf_op jit(solution)/shard_map/all_to_all | solution.py:75
  (401 shorter events, 426.1 us)
Async XLA Ops:
  6.5 86.2 %all-gather.2.cloned.1.call-start = ((), (), s32[]{:S(2)}) async-start(), calls=%async_computation.2 | async-start | bytes 2506752 | tf_op jit(solution)/shard_map/all_gather | solution.py:14
  23.8 56.2 %all-to-all-start = ((bf16[16,2,24576]{2,1,0:T(2,128)(2,1)}), bf16[16,2,24576]{2,1,0:T(2,128)(2,1)}, u32[]{:S(2)}, u32[]{:S(2)}) async-start(bf16[16,2,24576]{2,1,0:T(2,128)(2,1)} %reshape.112), calls=%async_computation | async-start | bytes 3145728 | tf_op jit(solution)/shard_map/all_to_all | solution.py:40
  97.7 12.7 %collective-permute-start = (bf16[1024,2,64]{0,2,1:T(8,128)(2,1)}, bf16[1024,2,64]{0,2,1:T(8,128)(2,1)S(1)}, u32[]{:S(2)}, u32[]{:S(2)}) collective-permute-start(bf16[1024,2,64]{0,2,1:T(8,128)(2,1)} %get-tuple-element.316), channel_id=1, source_target_pairs={{0,16},{16,32},{32,48},{48,64},{64,80},{80,96},{96,112},{112,128},... | collective-permute-start | bytes 786440 | tf_op jit(solution)/shard_map/while/body/eval_jaxpr/ppermute | solution.py:22
  114.0 11.8 %collective-permute-start = (bf16[1024,2,64]{0,2,1:T(8,128)(2,1)}, bf16[1024,2,64]{0,2,1:T(8,128)(2,1)S(1)}, u32[]{:S(2)}, u32[]{:S(2)}) collective-permute-start(bf16[1024,2,64]{0,2,1:T(8,128)(2,1)} %get-tuple-element.316), channel_id=1, source_target_pairs={{0,16},{16,32},{32,48},{48,64},{64,80},{80,96},{96,112},{112,128},... | collective-permute-start | bytes 786440 | tf_op jit(solution)/shard_map/while/body/eval_jaxpr/ppermute | solution.py:22
  129.3 10.6 %collective-permute-start = (bf16[1024,2,64]{0,2,1:T(8,128)(2,1)}, bf16[1024,2,64]{0,2,1:T(8,128)(2,1)S(1)}, u32[]{:S(2)}, u32[]{:S(2)}) collective-permute-start(bf16[1024,2,64]{0,2,1:T(8,128)(2,1)} %get-tuple-element.316), channel_id=1, source_target_pairs={{0,16},{16,32},{32,48},{48,64},{64,80},{80,96},{96,112},{112,128},... | collective-permute-start | bytes 786440 | tf_op jit(solution)/shard_map/while/body/eval_jaxpr/ppermute | solution.py:22
  143.6 10.6 %collective-permute-start = (bf16[1024,2,64]{0,2,1:T(8,128)(2,1)}, bf16[1024,2,64]{0,2,1:T(8,128)(2,1)S(1)}, u32[]{:S(2)}, u32[]{:S(2)}) collective-permute-start(bf16[1024,2,64]{0,2,1:T(8,128)(2,1)} %get-tuple-element.316), channel_id=1, source_target_pairs={{0,16},{16,32},{32,48},{48,64},{64,80},{80,96},{96,112},{112,128},... | collective-permute-start | bytes 786440 | tf_op jit(solution)/shard_map/while/body/eval_jaxpr/ppermute | solution.py:22
  157.8 10.6 %collective-permute-start = (bf16[1024,2,64]{0,2,1:T(8,128)(2,1)}, bf16[1024,2,64]{0,2,1:T(8,128)(2,1)S(1)}, u32[]{:S(2)}, u32[]{:S(2)}) collective-permute-start(bf16[1024,2,64]{0,2,1:T(8,128)(2,1)} %get-tuple-element.316), channel_id=1, source_target_pairs={{0,16},{16,32},{32,48},{48,64},{64,80},{80,96},{96,112},{112,128},... | collective-permute-start | bytes 786440 | tf_op jit(solution)/shard_map/while/body/eval_jaxpr/ppermute | solution.py:22
  172.1 10.6 %collective-permute-start = (bf16[1024,2,64]{0,2,1:T(8,128)(2,1)}, bf16[1024,2,64]{0,2,1:T(8,128)(2,1)S(1)}, u32[]{:S(2)}, u32[]{:S(2)}) collective-permute-start(bf16[1024,2,64]{0,2,1:T(8,128)(2,1)} %get-tuple-element.316), channel_id=1, source_target_pairs={{0,16},{16,32},{32,48},{48,64},{64,80},{80,96},{96,112},{112,128},... | collective-permute-start | bytes 786440 | tf_op jit(solution)/shard_map/while/body/eval_jaxpr/ppermute | solution.py:22
  186.3 10.6 %collective-permute-start = (bf16[1024,2,64]{0,2,1:T(8,128)(2,1)}, bf16[1024,2,64]{0,2,1:T(8,128)(2,1)S(1)}, u32[]{:S(2)}, u32[]{:S(2)}) collective-permute-start(bf16[1024,2,64]{0,2,1:T(8,128)(2,1)} %get-tuple-element.316), channel_id=1, source_target_pairs={{0,16},{16,32},{32,48},{48,64},{64,80},{80,96},{96,112},{112,128},... | collective-permute-start | bytes 786440 | tf_op jit(solution)/shard_map/while/body/eval_jaxpr/ppermute | solution.py:22
  200.5 10.6 %collective-permute-start = (bf16[1024,2,64]{0,2,1:T(8,128)(2,1)}, bf16[1024,2,64]{0,2,1:T(8,128)(2,1)S(1)}, u32[]{:S(2)}, u32[]{:S(2)}) collective-permute-start(bf16[1024,2,64]{0,2,1:T(8,128)(2,1)} %get-tuple-element.316), channel_id=1, source_target_pairs={{0,16},{16,32},{32,48},{48,64},{64,80},{80,96},{96,112},{112,128},... | collective-permute-start | bytes 786440 | tf_op jit(solution)/shard_map/while/body/eval_jaxpr/ppermute | solution.py:22
  214.8 10.6 %collective-permute-start = (bf16[1024,2,64]{0,2,1:T(8,128)(2,1)}, bf16[1024,2,64]{0,2,1:T(8,128)(2,1)S(1)}, u32[]{:S(2)}, u32[]{:S(2)}) collective-permute-start(bf16[1024,2,64]{0,2,1:T(8,128)(2,1)} %get-tuple-element.316), channel_id=1, source_target_pairs={{0,16},{16,32},{32,48},{48,64},{64,80},{80,96},{96,112},{112,128},... | collective-permute-start | bytes 786440 | tf_op jit(solution)/shard_map/while/body/eval_jaxpr/ppermute | solution.py:22
  229.0 10.6 %collective-permute-start = (bf16[1024,2,64]{0,2,1:T(8,128)(2,1)}, bf16[1024,2,64]{0,2,1:T(8,128)(2,1)S(1)}, u32[]{:S(2)}, u32[]{:S(2)}) collective-permute-start(bf16[1024,2,64]{0,2,1:T(8,128)(2,1)} %get-tuple-element.316), channel_id=1, source_target_pairs={{0,16},{16,32},{32,48},{48,64},{64,80},{80,96},{96,112},{112,128},... | collective-permute-start | bytes 786440 | tf_op jit(solution)/shard_map/while/body/eval_jaxpr/ppermute | solution.py:22
  243.3 10.6 %collective-permute-start = (bf16[1024,2,64]{0,2,1:T(8,128)(2,1)}, bf16[1024,2,64]{0,2,1:T(8,128)(2,1)S(1)}, u32[]{:S(2)}, u32[]{:S(2)}) collective-permute-start(bf16[1024,2,64]{0,2,1:T(8,128)(2,1)} %get-tuple-element.316), channel_id=1, source_target_pairs={{0,16},{16,32},{32,48},{48,64},{64,80},{80,96},{96,112},{112,128},... | collective-permute-start | bytes 786440 | tf_op jit(solution)/shard_map/while/body/eval_jaxpr/ppermute | solution.py:22
  257.5 11.2 %collective-permute-start = (bf16[1024,2,64]{0,2,1:T(8,128)(2,1)}, bf16[1024,2,64]{0,2,1:T(8,128)(2,1)S(1)}, u32[]{:S(2)}, u32[]{:S(2)}) collective-permute-start(bf16[1024,2,64]{0,2,1:T(8,128)(2,1)} %get-tuple-element.316), channel_id=1, source_target_pairs={{0,16},{16,32},{32,48},{48,64},{64,80},{80,96},{96,112},{112,128},... | collective-permute-start | bytes 786440 | tf_op jit(solution)/shard_map/while/body/eval_jaxpr/ppermute | solution.py:22
  272.3 12.3 %collective-permute-start = (bf16[1024,2,64]{0,2,1:T(8,128)(2,1)}, bf16[1024,2,64]{0,2,1:T(8,128)(2,1)S(1)}, u32[]{:S(2)}, u32[]{:S(2)}) collective-permute-start(bf16[1024,2,64]{0,2,1:T(8,128)(2,1)} %get-tuple-element.316), channel_id=1, source_target_pairs={{0,16},{16,32},{32,48},{48,64},{64,80},{80,96},{96,112},{112,128},... | collective-permute-start | bytes 786440 | tf_op jit(solution)/shard_map/while/body/eval_jaxpr/ppermute | solution.py:22
  288.3 13.7 %collective-permute-start = (bf16[1024,2,64]{0,2,1:T(8,128)(2,1)}, bf16[1024,2,64]{0,2,1:T(8,128)(2,1)S(1)}, u32[]{:S(2)}, u32[]{:S(2)}) collective-permute-start(bf16[1024,2,64]{0,2,1:T(8,128)(2,1)} %get-tuple-element.316), channel_id=1, source_target_pairs={{0,16},{16,32},{32,48},{48,64},{64,80},{80,96},{96,112},{112,128},... | collective-permute-start | bytes 786440 | tf_op jit(solution)/shard_map/while/body/eval_jaxpr/ppermute | solution.py:22
  305.6 12.9 %collective-permute-start = (bf16[1024,2,64]{0,2,1:T(8,128)(2,1)}, bf16[1024,2,64]{0,2,1:T(8,128)(2,1)S(1)}, u32[]{:S(2)}, u32[]{:S(2)}) collective-permute-start(bf16[1024,2,64]{0,2,1:T(8,128)(2,1)} %get-tuple-element.316), channel_id=1, source_target_pairs={{0,16},{16,32},{32,48},{48,64},{64,80},{80,96},{96,112},{112,128},... | collective-permute-start | bytes 786440 | tf_op jit(solution)/shard_map/while/body/eval_jaxpr/ppermute | solution.py:22
  322.1 12.0 %collective-permute-start = (bf16[1024,2,64]{0,2,1:T(8,128)(2,1)}, bf16[1024,2,64]{0,2,1:T(8,128)(2,1)S(1)}, u32[]{:S(2)}, u32[]{:S(2)}) collective-permute-start(bf16[1024,2,64]{0,2,1:T(8,128)(2,1)} %get-tuple-element.316), channel_id=1, source_target_pairs={{0,16},{16,32},{32,48},{48,64},{64,80},{80,96},{96,112},{112,128},... | collective-permute-start | bytes 786440 | tf_op jit(solution)/shard_map/while/body/eval_jaxpr/ppermute | solution.py:22
  337.7 11.1 %collective-permute-start = (bf16[1024,2,64]{0,2,1:T(8,128)(2,1)}, bf16[1024,2,64]{0,2,1:T(8,128)(2,1)S(1)}, u32[]{:S(2)}, u32[]{:S(2)}) collective-permute-start(bf16[1024,2,64]{0,2,1:T(8,128)(2,1)} %get-tuple-element.316), channel_id=1, source_target_pairs={{0,16},{16,32},{32,48},{48,64},{64,80},{80,96},{96,112},{112,128},... | collective-permute-start | bytes 786440 | tf_op jit(solution)/shard_map/while/body/eval_jaxpr/ppermute | solution.py:22
  354.1 11.8 %collective-permute-start = (bf16[1024,2,64]{0,2,1:T(8,128)(2,1)}, bf16[1024,2,64]{0,2,1:T(8,128)(2,1)S(1)}, u32[]{:S(2)}, u32[]{:S(2)}) collective-permute-start(bf16[1024,2,64]{0,2,1:T(8,128)(2,1)} %get-tuple-element.316), channel_id=1, source_target_pairs={{0,16},{16,32},{32,48},{48,64},{64,80},{80,96},{96,112},{112,128},... | collective-permute-start | bytes 786440 | tf_op jit(solution)/shard_map/while/body/eval_jaxpr/ppermute | solution.py:22
  371.2 10.6 %collective-permute-start = (bf16[1024,2,64]{0,2,1:T(8,128)(2,1)}, bf16[1024,2,64]{0,2,1:T(8,128)(2,1)S(1)}, u32[]{:S(2)}, u32[]{:S(2)}) collective-permute-start(bf16[1024,2,64]{0,2,1:T(8,128)(2,1)} %get-tuple-element.316), channel_id=1, source_target_pairs={{0,16},{16,32},{32,48},{48,64},{64,80},{80,96},{96,112},{112,128},... | collective-permute-start | bytes 786440 | tf_op jit(solution)/shard_map/while/body/eval_jaxpr/ppermute | solution.py:22
  387.2 10.6 %collective-permute-start = (bf16[1024,2,64]{0,2,1:T(8,128)(2,1)}, bf16[1024,2,64]{0,2,1:T(8,128)(2,1)S(1)}, u32[]{:S(2)}, u32[]{:S(2)}) collective-permute-start(bf16[1024,2,64]{0,2,1:T(8,128)(2,1)} %get-tuple-element.316), channel_id=1, source_target_pairs={{0,16},{16,32},{32,48},{48,64},{64,80},{80,96},{96,112},{112,128},... | collective-permute-start | bytes 786440 | tf_op jit(solution)/shard_map/while/body/eval_jaxpr/ppermute | solution.py:22
  403.1 10.6 %collective-permute-start = (bf16[1024,2,64]{0,2,1:T(8,128)(2,1)}, bf16[1024,2,64]{0,2,1:T(8,128)(2,1)S(1)}, u32[]{:S(2)}, u32[]{:S(2)}) collective-permute-start(bf16[1024,2,64]{0,2,1:T(8,128)(2,1)} %get-tuple-element.316), channel_id=1, source_target_pairs={{0,16},{16,32},{32,48},{48,64},{64,80},{80,96},{96,112},{112,128},... | collective-permute-start | bytes 786440 | tf_op jit(solution)/shard_map/while/body/eval_jaxpr/ppermute | solution.py:22
  463.5 10.6 %collective-permute-start = (bf16[1024,2,64]{0,2,1:T(8,128)(2,1)}, bf16[1024,2,64]{0,2,1:T(8,128)(2,1)S(1)}, u32[]{:S(2)}, u32[]{:S(2)}) collective-permute-start(bf16[1024,2,64]{0,2,1:T(8,128)(2,1)} %get-tuple-element.316), channel_id=1, source_target_pairs={{0,16},{16,32},{32,48},{48,64},{64,80},{80,96},{96,112},{112,128},... | collective-permute-start | bytes 786440 | tf_op jit(solution)/shard_map/while/body/eval_jaxpr/ppermute | solution.py:22
  492.0 11.8 %collective-permute-start = (bf16[1024,2,64]{0,2,1:T(8,128)(2,1)}, bf16[1024,2,64]{0,2,1:T(8,128)(2,1)S(1)}, u32[]{:S(2)}, u32[]{:S(2)}) collective-permute-start(bf16[1024,2,64]{0,2,1:T(8,128)(2,1)} %get-tuple-element.316), channel_id=1, source_target_pairs={{0,16},{16,32},{32,48},{48,64},{64,80},{80,96},{96,112},{112,128},... | collective-permute-start | bytes 786440 | tf_op jit(solution)/shard_map/while/body/eval_jaxpr/ppermute | solution.py:22
  507.4 12.9 %collective-permute-start = (bf16[1024,2,64]{0,2,1:T(8,128)(2,1)}, bf16[1024,2,64]{0,2,1:T(8,128)(2,1)S(1)}, u32[]{:S(2)}, u32[]{:S(2)}) collective-permute-start(bf16[1024,2,64]{0,2,1:T(8,128)(2,1)} %get-tuple-element.316), channel_id=1, source_target_pairs={{0,16},{16,32},{32,48},{48,64},{64,80},{80,96},{96,112},{112,128},... | collective-permute-start | bytes 786440 | tf_op jit(solution)/shard_map/while/body/eval_jaxpr/ppermute | solution.py:22
  523.9 13.2 %collective-permute-start = (bf16[1024,2,64]{0,2,1:T(8,128)(2,1)}, bf16[1024,2,64]{0,2,1:T(8,128)(2,1)S(1)}, u32[]{:S(2)}, u32[]{:S(2)}) collective-permute-start(bf16[1024,2,64]{0,2,1:T(8,128)(2,1)} %get-tuple-element.316), channel_id=1, source_target_pairs={{0,16},{16,32},{32,48},{48,64},{64,80},{80,96},{96,112},{112,128},... | collective-permute-start | bytes 786440 | tf_op jit(solution)/shard_map/while/body/eval_jaxpr/ppermute | solution.py:22
  540.6 12.3 %collective-permute-start = (bf16[1024,2,64]{0,2,1:T(8,128)(2,1)}, bf16[1024,2,64]{0,2,1:T(8,128)(2,1)S(1)}, u32[]{:S(2)}, u32[]{:S(2)}) collective-permute-start(bf16[1024,2,64]{0,2,1:T(8,128)(2,1)} %get-tuple-element.316), channel_id=1, source_target_pairs={{0,16},{16,32},{32,48},{48,64},{64,80},{80,96},{96,112},{112,128},... | collective-permute-start | bytes 786440 | tf_op jit(solution)/shard_map/while/body/eval_jaxpr/ppermute | solution.py:22
  556.5 11.3 %collective-permute-start = (bf16[1024,2,64]{0,2,1:T(8,128)(2,1)}, bf16[1024,2,64]{0,2,1:T(8,128)(2,1)S(1)}, u32[]{:S(2)}, u32[]{:S(2)}) collective-permute-start(bf16[1024,2,64]{0,2,1:T(8,128)(2,1)} %get-tuple-element.316), channel_id=1, source_target_pairs={{0,16},{16,32},{32,48},{48,64},{64,80},{80,96},{96,112},{112,128},... | collective-permute-start | bytes 786440 | tf_op jit(solution)/shard_map/while/body/eval_jaxpr/ppermute | solution.py:22
  571.5 10.6 %collective-permute-start = (bf16[1024,2,64]{0,2,1:T(8,128)(2,1)}, bf16[1024,2,64]{0,2,1:T(8,128)(2,1)S(1)}, u32[]{:S(2)}, u32[]{:S(2)}) collective-permute-start(bf16[1024,2,64]{0,2,1:T(8,128)(2,1)} %get-tuple-element.316), channel_id=1, source_target_pairs={{0,16},{16,32},{32,48},{48,64},{64,80},{80,96},{96,112},{112,128},... | collective-permute-start | bytes 786440 | tf_op jit(solution)/shard_map/while/body/eval_jaxpr/ppermute | solution.py:22
  599.9 10.6 %collective-permute-start = (bf16[1024,2,64]{0,2,1:T(8,128)(2,1)}, bf16[1024,2,64]{0,2,1:T(8,128)(2,1)S(1)}, u32[]{:S(2)}, u32[]{:S(2)}) collective-permute-start(bf16[1024,2,64]{0,2,1:T(8,128)(2,1)} %get-tuple-element.316), channel_id=1, source_target_pairs={{0,16},{16,32},{32,48},{48,64},{64,80},{80,96},{96,112},{112,128},... | collective-permute-start | bytes 786440 | tf_op jit(solution)/shard_map/while/body/eval_jaxpr/ppermute | solution.py:22
  614.2 10.6 %collective-permute-start = (bf16[1024,2,64]{0,2,1:T(8,128)(2,1)}, bf16[1024,2,64]{0,2,1:T(8,128)(2,1)S(1)}, u32[]{:S(2)}, u32[]{:S(2)}) collective-permute-start(bf16[1024,2,64]{0,2,1:T(8,128)(2,1)} %get-tuple-element.316), channel_id=1, source_target_pairs={{0,16},{16,32},{32,48},{48,64},{64,80},{80,96},{96,112},{112,128},... | collective-permute-start | bytes 786440 | tf_op jit(solution)/shard_map/while/body/eval_jaxpr/ppermute | solution.py:22
  (8 other events, 77.6 us)
Sparse Core Ops, SparseCore 0:
  9.5 65.6 all-gather.1
where the time goes:
time: 779 us; the launch traced here: 774 us
  waiting for transfers between devices  341 us (44%)
  other arithmetic  131 us (17%)
  local copies, waits for them, and re-layouts  108 us (14%)
  blocking collectives  85.1 us (11%)
  starting transfers between devices  82.8 us (11%)
  between operations  13.4 us (2%)
  matrix products  9.19 us (1%)
    ppermute x37, waiting for transfers between devices, passed_along(): lax.ppermute(value, axis, [(source, source + steps) for source in range(l...  296 us
    all_to_all x1, blocking collectives, per_device(): lax.all_to_all(final_pair[1], 'ch', split_axis=1, concat_axis=3, tiled=True)  85.1 us
    ppermute x37, starting transfers between devices, passed_along(): lax.ppermute(value, axis, [(source, source + steps) for source in range(l...  71.8 us
    dynamic_update_slice x37, other arithmetic, step(): stored = lax.dynamic_update_index_in_dim(stored, kept, energy_slot, 0)  63.8 us
    all_to_all x1, waiting for transfers between devices, per_device(): lax.all_to_all(paired, 'ch', split_axis=3, concat_axis=1, tiled=True)  45.2 us
    convert_element_type x37, other arithmetic, step(): source = jnp.where(sector_index == 0, initial, incoming).astype(jnp.float32)  36.6 us
    div x37, other arithmetic, step(): new_values = cosine * values_part + sine_term / wavenumber * slopes_part  24.7 us
    reshape x62, local copies, waits for them, and re-layouts, step(): fresh = fresh.reshape(channel_count, 2, col_width)  23.2 us
  transfers between devices with their start and end apart: 39, of which 38 were waited for; matrix products, arithmetic and copies ran while one was open for 9% of the time, Pallas kernels for 0%

commit v1 on v0

v1 whole, which is shorter than its diff:
```python
import jax
import jax.numpy as jnp
from jax import lax
from jax.experimental import pallas as pl
from jax.experimental.pallas import tpu as pltpu
from jax.sharding import Mesh
from jax.sharding import PartitionSpec as P

AXES = ("y", "x", "z", "core")
SIZES = (8, 4, 8, 2)
CH_AXES = ("z", "core")
PLANE = ("x", "z", "core")
VMEM = 56 * 1024 * 1024


def spread_kernel(x_ref, v_ref, p_ref, out_ref):
    both = jnp.concatenate([v_ref[0], p_ref[0]], axis=0).astype(jnp.float32)
    turned = both.T.astype(jnp.bfloat16)
    groups, _, per, lanes = out_ref.shape
    out_ref[...] = turned.reshape(groups, 1, per, lanes)


def spread(x_index, start):
    energies, rows, width = start.shape
    cols = width // 8
    per = cols // 16
    return pl.pallas_call(
        spread_kernel,
        grid_spec=pltpu.PrefetchScalarGridSpec(
            num_scalar_prefetch=1,
            grid=(energies,),
            in_specs=[
                pl.BlockSpec((1, rows, cols), lambda e, x: (e, 0, x[0])),
                pl.BlockSpec((1, rows, cols), lambda e, x: (e, 0, 4 + x[0])),
            ],
            out_specs=pl.BlockSpec((16, 1, per, 2 * rows), lambda e, x: (0, e, 0, 0)),
        ),
        out_shape=jax.ShapeDtypeStruct((16, energies, per, 2 * rows), start.dtype),
        name="spread",
    )(x_index, start, start)


def join_kernel(in_ref, out_ref):
    rows = in_ref.shape[1]
    low = lax.broadcasted_iota(jnp.int32, (rows, 128), 1) < 64
    for z in range(8):
        one = in_ref[2 * z].astype(jnp.float32)
        two = in_ref[2 * z + 1].astype(jnp.float32)
        lanes = pl.ds(128 * z, 128)
        out_ref[0, :, lanes] = jnp.where(low, one, pltpu.roll(two, 64, 1)).astype(out_ref.dtype)
        out_ref[1, :, lanes] = jnp.where(low, pltpu.roll(one, 64, 1), two).astype(out_ref.dtype)


def join(pieces):
    rows = pieces.shape[1]
    return pl.pallas_call(
        join_kernel,
        out_shape=jax.ShapeDtypeStruct((2, rows, 1024), pieces.dtype),
        name="join",
    )(pieces)


def stage_kernel(active, state_ref, basis_ref, coef_ref, kept_ref, next_ref, out_ref, now, rot):
    del active, kept_ref
    s = pl.program_id(0)
    energies = coef_ref.shape[2]
    rows = state_ref.shape[1]
    per = rows // energies

    @pl.when(s == 0)
    def _():
        now[pl.ds(0, rows)] = state_ref[0]
        now[pl.ds(rows, rows)] = state_ref[1]

    for e in range(energies):
        cosine = coef_ref[0, 0, pl.ds(e, 1), :]
        ratio = coef_ref[0, 1, pl.ds(e, 1), :]
        product = coef_ref[0, 2, pl.ds(e, 1), :]
        values = now[pl.ds(per * e, per), :].astype(jnp.float32)
        slopes = now[pl.ds(rows + per * e, per), :].astype(jnp.float32)
        rot[pl.ds(per * e, per), :] = (cosine * values + ratio * slopes).astype(rot.dtype)
        rot[pl.ds(rows + per * e, per), :] = (cosine * slopes - product * values).astype(rot.dtype)
    fresh = lax.dot_general(
        rot[...], basis_ref[0], (((1,), (1,)), ((), ())), preferred_element_type=jnp.float32
    )
    rounded = fresh.astype(now.dtype)
    now[...] = rounded
    low = lax.broadcasted_iota(jnp.int32, (rows, 128), 1) < 64
    for z in range(8):
        lanes = slice(128 * z, 128 * z + 128)
        values = fresh[:rows, lanes]
        slopes = fresh[rows:, lanes]
        out_ref[0, 2 * z] = jnp.where(low, values, pltpu.roll(slopes, 64, 1)).astype(out_ref.dtype)
        out_ref[0, 2 * z + 1] = jnp.where(low, pltpu.roll(values, 64, 1), slopes).astype(out_ref.dtype)

    @pl.when(s == pl.num_programs(0) - 1)
    def _():
        next_ref[0] = rounded[:rows]
        next_ref[1] = rounded[rows:]


def stage(active, state, basis, coefs, kept):
    sectors, channels, _ = basis.shape
    rows = state.shape[1]
    return pl.pallas_call(
        stage_kernel,
        grid_spec=pltpu.PrefetchScalarGridSpec(
            num_scalar_prefetch=1,
            grid=(sectors,),
            in_specs=[
                pl.BlockSpec(state.shape, lambda s, a: (0, 0, 0)),
                pl.BlockSpec((1, channels, channels), lambda s, a: (s, 0, 0)),
                pl.BlockSpec((1,) + coefs.shape[1:], lambda s, a: (s, 0, 0, 0)),
                pl.BlockSpec(memory_space=pl.ANY),
            ],
            out_specs=[
                pl.BlockSpec(state.shape, lambda s, a: (0, 0, 0)),
                pl.BlockSpec((1, 16, rows, 128), lambda s, a: (jnp.where(a[0] == 1, s, sectors), 0, 0, 0)),
            ],
            scratch_shapes=[
                pltpu.VMEM((2 * rows, channels), state.dtype),
                pltpu.VMEM((2 * rows, channels), state.dtype),
            ],
        ),
        out_shape=[
            jax.ShapeDtypeStruct(state.shape, state.dtype),
            jax.ShapeDtypeStruct(kept.shape, kept.dtype),
        ],
        input_output_aliases={4: 1},
        compiler_params=pltpu.CompilerParams(vmem_limit_bytes=VMEM),
        name="stage",
    )(active, state, basis, coefs, kept)


def finish_kernel(in_ref, out_ref):
    groups, _, per, lanes = in_ref.shape
    turned = in_ref[...].reshape(groups * per, lanes).astype(jnp.float32).T.astype(out_ref.dtype)
    half = lanes // 2
    cols = groups * per
    out_ref[0, :, pl.ds(0, cols)] = turned[:half]
    out_ref[0, :, pl.ds(cols, cols)] = turned[half:]


def finish(pieces):
    groups, energies, per, lanes = pieces.shape
    return pl.pallas_call(
        finish_kernel,
        grid=(energies,),
        in_specs=[pl.BlockSpec((groups, 1, per, lanes), lambda e: (0, e, 0, 0))],
        out_specs=pl.BlockSpec((1, lanes // 2, 2 * groups * per), lambda e: (e, 0, 0)),
        out_shape=jax.ShapeDtypeStruct((energies, lanes // 2, 2 * groups * per), pieces.dtype),
        compiler_params=pltpu.CompilerParams(vmem_limit_bytes=VMEM),
        name="finish",
    )(pieces)


def per_device(start_amps, energies, thresholds, intersection):
    planes = lax.axis_size("y")
    y_index = lax.axis_index("y")
    x_index = lax.axis_index("x").astype(jnp.int32).reshape(1)
    count = energies.shape[0]
    channels = intersection.shape[2]
    basis = lax.all_gather(intersection[0], PLANE, tiled=True).reshape(4, channels, channels)
    limits = lax.all_gather(thresholds[0], PLANE, tiled=True).reshape(4, 1, channels)
    wave = jnp.sqrt(energies[None, :, None] - limits.astype(jnp.float32))
    sine = jnp.sin(wave)
    coefs = jnp.stack([jnp.cos(wave), sine / wave, wave * sine], axis=1)

    blocks = spread(x_index, start_amps)
    per, lanes = blocks.shape[2:]
    rows = count * per
    state = join(lax.all_to_all(blocks.reshape(16, rows, lanes), CH_AXES, 0, 0))
    kept = jnp.zeros((5, 16, rows, lanes), jnp.bfloat16)
    for step in range(planes):
        if step:
            state = lax.ppermute(state, "y", [(k, k + 1) for k in range(planes - 1)])
        active = (y_index == step).astype(jnp.int32).reshape(1)
        state, kept = stage(active, state, basis, coefs, kept)
    back = lax.all_to_all(kept[:4].reshape(64, rows, lanes), PLANE, 0, 0)
    return finish(back.reshape(64, count, per, lanes))[None]


def solution(mesh):
    fine = Mesh(mesh.devices.reshape(SIZES), AXES)
    sec, ch = ("y", "x"), CH_AXES
    in_specs = (P(None, ch, None), P(), P(sec, ch), P(sec, ch, None))
    out_specs = P(sec, None, ch, None)
    return jax.shard_map(
        per_device, mesh=fine, in_specs=in_specs, out_specs=out_specs, check_vma=False
    )
```

time: 779 us -> 372 us (0.48)
  the two profiles are of different devices: /device:TPU:33 before, /device:TPU:39 now
where the time goes in v1:
time: 372 us; the launch traced here: 371 us
  blocking collectives  193 us (52%)
  Pallas kernels  68.6 us (18%)
  waiting for transfers between devices  58.5 us (16%)
  starting transfers between devices  24.7 us (7%)
  between operations  14.2 us (4%)
  local copies, waits for them, and re-layouts  10.7 us (3%)
    unnamed x1, blocking collectives  110 us
    all_to_all x1, blocking collectives, per_device(): back = lax.all_to_all(kept[:4].reshape(64, rows, lanes), PLANE, 0, 0)  83.5 us
    pallas_call x8, Pallas kernels, stage(): pl.pallas_call(stage_kernel, grid_spec=pltpu.PrefetchScalarGridSpec(num_s...  57.9 us
    ppermute x7, waiting for transfers between devices, per_device(): state = lax.ppermute(state, 'y', [(k, k + 1) for k in range(planes - 1)])  57.8 us
    ppermute x7, starting transfers between devices, per_device(): state = lax.ppermute(state, 'y', [(k, k + 1) for k in range(planes - 1)])  13.7 us
    all_to_all x1, starting transfers between devices, per_device(): state = join(lax.all_to_all(blocks.reshape(16, rows, lanes), CH_AXES, 0, 0))  11 us
    unnamed x23, local copies, waits for them, and re-layouts  7.51 us
  transfers between devices with their start and end apart: 9, of which 7 were waited for; matrix products, arithmetic and copies ran while one was open for 1% of the time, Pallas kernels for 2%

profile of v1, /device:TPU:39, one launch (start us, length us, event | category | flops | bytes accessed | tf_op | source)
XLA Modules:
  0.0 371.2 jit_solution(13420576054140280719)
XLA Ops:
  7.3 4.0 %spread.1 = bf16[16,6,16,128]{3,2,1,0:T(8,128)(2,1)} custom-call(s32[1]{0:T(128)} %bitcast.8.x_ref, bf16[6,64,2048]{2,1,0:T(8,128)(2,1)} %p_ref.1, bf16[6,64,2048]{2,1,0:T(8,128)(2,1)} %p_ref.1), custom_call_target="tpu_custom_call" | custom-call | tf_op jit(solution)/shard_map/spread/pallas_call | solution.py:27
  11.2 11.0 %all-to-all-start = ((bf16[16,96,128]{2,1,0:T(8,128)(2,1)}), bf16[16,96,128]{2,1,0:T(8,128)(2,1)S(1)}, u32[]{:S(2)}, u32[]{:S(2)}) async-start(bf16[16,96,128]{2,1,0:T(8,128)(2,1)} %bitcast.26), calls=%async_computation | async-start | bytes 786432 | tf_op jit(solution)/shard_map/all_to_all | solution.py:172
  22.3 1.3 dynamic-slice
  24.4 109.6 %all-reduce = bf16[4096]{0:T(1024)(128)(2,1)S(1)} all-reduce(bf16[4096]{0:T(1024)(128)(2,1)S(1)} %dynamic-update-slice), channel_id=3, replica_groups=mesh['y'=8,'x'=4,'z'=8,'core'=2] {'x','z','core'}, use_global_device_ids=true, to_apply=%add | all-reduce | flops 4096 | bytes 16384
  134.7 0.8 pad_maximum_fusion.coef_ref
  136.2 1.9 join.1.state_ref
  138.1 1.7 broadcast_in_dim.7.kept_ref
  139.8 7.2 %stage.8 = (bf16[2,96,1024]{2,1,0:T(8,128)(2,1)}, bf16[5,16,96,128]{3,2,1,0:T(8,128)(2,1)}) custom-call(s32[1]{0:T(128)} %bitcast.7.active, bf16[2,96,1024]{2,1,0:T(8,128)(2,1)} %join.1.state_ref, bf16[4,1024,1024]{2,1,0:T(8,128)(2,1)} %bitcast.16, f32[4,3,6,1024]{3,2,1,0:T(8,128)} %pad_maximum_fusion.coef_ref, ...), custom_call_target="tpu_custom_call", output_to_operand_aliasing={{1}: (4, {})} | custom-call | tf_op jit(solution)/shard_map/stage/pallas_call | solution.py:105
  147.0 2.2 collective-permute-start
  149.3 9.2 %collective-permute-done.state_ref = bf16[2,96,1024]{2,1,0:T(8,128)(2,1)S(1)} collective-permute-done((bf16[2,96,1024]{2,1,0:T(8,128)(2,1)}, bf16[2,96,1024]{2,1,0:T(8,128)(2,1)S(1)}, u32[]{:S(2)}, u32[]{:S(2)}) %collective-permute-start) | collective-permute-done | bytes 393248 | tf_op jit(solution)/shard_map/ppermute | solution.py:176
  159.2 7.2 %stage.9 = (bf16[2,96,1024]{2,1,0:T(8,128)(2,1)}, bf16[5,16,96,128]{3,2,1,0:T(8,128)(2,1)}) custom-call(s32[1]{0:T(128)} %bitcast.6.active, bf16[2,96,1024]{2,1,0:T(8,128)(2,1)} %copy-done.2, bf16[4,1024,1024]{2,1,0:T(8,128)(2,1)} %bitcast.17, f32[4,3,6,1024]{3,2,1,0:T(8,128)} %pad_maximum_fusion.coef_ref, ...), custom_call_target="tpu_custom_call", output_to_operand_aliasing={{1}: (4, {})} | custom-call | tf_op jit(solution)/shard_map/stage/pallas_call | solution.py:105
  166.4 1.9 collective-permute-start.1
  168.3 8.6 %collective-permute-done.1.state_ref = bf16[2,96,1024]{2,1,0:T(8,128)(2,1)S(1)} collective-permute-done((bf16[2,96,1024]{2,1,0:T(8,128)(2,1)}, bf16[2,96,1024]{2,1,0:T(8,128)(2,1)S(1)}, u32[]{:S(2)}, u32[]{:S(2)}) %collective-permute-start.1) | collective-permute-done | bytes 393248 | tf_op jit(solution)/shard_map/ppermute | solution.py:176
  177.7 7.2 %stage.10 = (bf16[2,96,1024]{2,1,0:T(8,128)(2,1)}, bf16[5,16,96,128]{3,2,1,0:T(8,128)(2,1)}) custom-call(s32[1]{0:T(128)} %bitcast.5.active, bf16[2,96,1024]{2,1,0:T(8,128)(2,1)} %copy-done.3, bf16[4,1024,1024]{2,1,0:T(8,128)(2,1)} %bitcast.18, f32[4,3,6,1024]{3,2,1,0:T(8,128)} %pad_maximum_fusion.coef_ref, ...), custom_call_target="tpu_custom_call", output_to_operand_aliasing={{1}: (4, {})} | custom-call | tf_op jit(solution)/shard_map/stage/pallas_call | solution.py:105
  184.9 1.9 collective-permute-start.2
  186.8 8.0 %collective-permute-done.2.state_ref = bf16[2,96,1024]{2,1,0:T(8,128)(2,1)S(1)} collective-permute-done((bf16[2,96,1024]{2,1,0:T(8,128)(2,1)}, bf16[2,96,1024]{2,1,0:T(8,128)(2,1)S(1)}, u32[]{:S(2)}, u32[]{:S(2)}) %collective-permute-start.2) | collective-permute-done | bytes 393248 | tf_op jit(solution)/shard_map/ppermute | solution.py:176
  195.6 7.2 %stage.11 = (bf16[2,96,1024]{2,1,0:T(8,128)(2,1)}, bf16[5,16,96,128]{3,2,1,0:T(8,128)(2,1)}) custom-call(s32[1]{0:T(128)} %bitcast.4.active, bf16[2,96,1024]{2,1,0:T(8,128)(2,1)} %copy-done.4, bf16[4,1024,1024]{2,1,0:T(8,128)(2,1)} %bitcast.19, f32[4,3,6,1024]{3,2,1,0:T(8,128)} %pad_maximum_fusion.coef_ref, ...), custom_call_target="tpu_custom_call", output_to_operand_aliasing={{1}: (4, {})} | custom-call | tf_op jit(solution)/shard_map/stage/pallas_call | solution.py:105
  202.8 1.9 collective-permute-start.3
  204.7 8.0 %collective-permute-done.3.state_ref = bf16[2,96,1024]{2,1,0:T(8,128)(2,1)S(1)} collective-permute-done((bf16[2,96,1024]{2,1,0:T(8,128)(2,1)}, bf16[2,96,1024]{2,1,0:T(8,128)(2,1)S(1)}, u32[]{:S(2)}, u32[]{:S(2)}) %collective-permute-start.3) | collective-permute-done | bytes 393248 | tf_op jit(solution)/shard_map/ppermute | solution.py:176
  213.4 7.3 %stage.12 = (bf16[2,96,1024]{2,1,0:T(8,128)(2,1)}, bf16[5,16,96,128]{3,2,1,0:T(8,128)(2,1)}) custom-call(s32[1]{0:T(128)} %bitcast.3.active, bf16[2,96,1024]{2,1,0:T(8,128)(2,1)} %copy-done.5, bf16[4,1024,1024]{2,1,0:T(8,128)(2,1)} %bitcast.20, f32[4,3,6,1024]{3,2,1,0:T(8,128)} %pad_maximum_fusion.coef_ref, ...), custom_call_target="tpu_custom_call", output_to_operand_aliasing={{1}: (4, {})} | custom-call | tf_op jit(solution)/shard_map/stage/pallas_call | solution.py:105
  220.8 1.9 collective-permute-start.4
  222.7 8.0 %collective-permute-done.4.state_ref = bf16[2,96,1024]{2,1,0:T(8,128)(2,1)S(1)} collective-permute-done((bf16[2,96,1024]{2,1,0:T(8,128)(2,1)}, bf16[2,96,1024]{2,1,0:T(8,128)(2,1)S(1)}, u32[]{:S(2)}, u32[]{:S(2)}) %collective-permute-start.4) | collective-permute-done | bytes 393248 | tf_op jit(solution)/shard_map/ppermute | solution.py:176
  231.5 7.2 %stage.13 = (bf16[2,96,1024]{2,1,0:T(8,128)(2,1)}, bf16[5,16,96,128]{3,2,1,0:T(8,128)(2,1)}) custom-call(s32[1]{0:T(128)} %bitcast.2.active, bf16[2,96,1024]{2,1,0:T(8,128)(2,1)} %copy-done.6, bf16[4,1024,1024]{2,1,0:T(8,128)(2,1)} %bitcast.21, f32[4,3,6,1024]{3,2,1,0:T(8,128)} %pad_maximum_fusion.coef_ref, ...), custom_call_target="tpu_custom_call", output_to_operand_aliasing={{1}: (4, {})} | custom-call | tf_op jit(solution)/shard_map/stage/pallas_call | solution.py:105
  238.7 1.9 collective-permute-start.5
  240.6 8.0 %collective-permute-done.5.state_ref = bf16[2,96,1024]{2,1,0:T(8,128)(2,1)S(1)} collective-permute-done((bf16[2,96,1024]{2,1,0:T(8,128)(2,1)}, bf16[2,96,1024]{2,1,0:T(8,128)(2,1)S(1)}, u32[]{:S(2)}, u32[]{:S(2)}) %collective-permute-start.5) | collective-permute-done | bytes 393248 | tf_op jit(solution)/shard_map/ppermute | solution.py:176
  249.4 7.2 %stage.14 = (bf16[2,96,1024]{2,1,0:T(8,128)(2,1)}, bf16[5,16,96,128]{3,2,1,0:T(8,128)(2,1)}) custom-call(s32[1]{0:T(128)} %bitcast.1.active, bf16[2,96,1024]{2,1,0:T(8,128)(2,1)} %copy-done.7, bf16[4,1024,1024]{2,1,0:T(8,128)(2,1)} %bitcast.22, f32[4,3,6,1024]{3,2,1,0:T(8,128)} %pad_maximum_fusion.coef_ref, ...), custom_call_target="tpu_custom_call", output_to_operand_aliasing={{1}: (4, {})} | custom-call | tf_op jit(solution)/shard_map/stage/pallas_call | solution.py:105
  256.6 1.9 collective-permute-start.6
  258.5 8.0 %collective-permute-done.6.state_ref = bf16[2,96,1024]{2,1,0:T(8,128)(2,1)S(1)} collective-permute-done((bf16[2,96,1024]{2,1,0:T(8,128)(2,1)}, bf16[2,96,1024]{2,1,0:T(8,128)(2,1)S(1)}, u32[]{:S(2)}, u32[]{:S(2)}) %collective-permute-start.6) | collective-permute-done | bytes 393248 | tf_op jit(solution)/shard_map/ppermute | solution.py:176
  267.3 7.2 %stage.15 = (bf16[2,96,1024]{2,1,0:T(8,128)(2,1)}, bf16[5,16,96,128]{3,2,1,0:T(8,128)(2,1)}) custom-call(s32[1]{0:T(128)} %bitcast.active, bf16[2,96,1024]{2,1,0:T(8,128)(2,1)} %copy-done.1, bf16[4,1024,1024]{2,1,0:T(8,128)(2,1)} %bitcast.23, f32[4,3,6,1024]{3,2,1,0:T(8,128)} %pad_maximum_fusion.coef_ref, ...), custom_call_target="tpu_custom_call", output_to_operand_aliasing={{1}: (4, {})} | custom-call | tf_op jit(solution)/shard_map/stage/pallas_call | solution.py:105
  274.5 1.5 slice.3
  276.0 83.5 %all_to_all.10 = bf16[64,96,128]{2,1,0:T(8,128)(2,1)} all-to-all(bf16[64,96,128]{2,1,0:T(8,128)(2,1)S(1)} %bitcast.24), channel_id=1, replica_groups=mesh['y'=8,'x'=4,'z'=8,'core'=2] {'x','z','core'}, dimensions={0} | all-to-all | bytes 3145728 | tf_op jit(solution)/shard_map/all_to_all | solution.py:179
  359.5 4.9 %finish.1 = bf16[6,64,2048]{2,1,0:T(8,128)(2,1)} custom-call(bf16[64,6,16,128]{3,2,1,0:T(8,128)(2,1)} %bitcast.25), custom_call_target="tpu_custom_call" | custom-call | tf_op jit(solution)/shard_map/finish/pallas_call | solution.py:146
  (28 shorter events, 7.5 us)
Async XLA Ops:
  6.5 131.6 %all-gather.4.cloned.1.call-start = ((), (), s32[]{:S(2)}) async-start(), calls=%async_computation.2 | async-start | bytes 8519680 | tf_op jit(solution)/shard_map/all_gather | solution.py:163
  7.3 16.9 %copy-start.9 = (bf16[1,64]{1,0:T(2,128)(2,1)S(1)}, bf16[1,64]{1,0:T(2,128)(2,1)}, u32[]{:S(2)}) copy-start(bf16[1,64]{1,0:T(2,128)(2,1)} %param.6) | copy-start | bytes 388
  7.3 126.8 %copy-start.8 = (f32[6]{0:T(128)S(1)}, f32[6]{0:T(128)}, u32[]{:S(2)}) copy-start(f32[6]{0:T(128)} %param.5) | copy-start | bytes 76
  11.2 124.2 %all-to-all-start = ((bf16[16,96,128]{2,1,0:T(8,128)(2,1)}), bf16[16,96,128]{2,1,0:T(8,128)(2,1)S(1)}, u32[]{:S(2)}, u32[]{:S(2)}) async-start(bf16[16,96,128]{2,1,0:T(8,128)(2,1)} %bitcast.26), calls=%async_computation | async-start | bytes 786432 | tf_op jit(solution)/shard_map/all_to_all | solution.py:172
  135.5 0.7 copy-start
  147.0 11.4 %collective-permute-start = (bf16[2,96,1024]{2,1,0:T(8,128)(2,1)}, bf16[2,96,1024]{2,1,0:T(8,128)(2,1)S(1)}, u32[]{:S(2)}, u32[]{:S(2)}) collective-permute-start(bf16[2,96,1024]{2,1,0:T(8,128)(2,1)} %get-tuple-element.20), channel_id=1, source_target_pairs={{0,64},{64,128},{128,192},{192,256},{256,320},{320,384},{384,448},... | collective-permute-start | bytes 1179656 | tf_op jit(solution)/shard_map/ppermute | solution.py:176
  158.5 0.7 copy-start.2
  166.4 10.5 %collective-permute-start.1 = (bf16[2,96,1024]{2,1,0:T(8,128)(2,1)}, bf16[2,96,1024]{2,1,0:T(8,128)(2,1)S(1)}, u32[]{:S(2)}, u32[]{:S(2)}) collective-permute-start(bf16[2,96,1024]{2,1,0:T(8,128)(2,1)} %get-tuple-element.22), channel_id=1, source_target_pairs={{0,64},{64,128},{128,192},{192,256},{256,320},{320,384},{384,448},... | collective-permute-start | bytes 1179656 | tf_op jit(solution)/shard_map/ppermute | solution.py:176
  176.9 0.7 copy-start.3
  184.9 9.9 %collective-permute-start.2 = (bf16[2,96,1024]{2,1,0:T(8,128)(2,1)}, bf16[2,96,1024]{2,1,0:T(8,128)(2,1)S(1)}, u32[]{:S(2)}, u32[]{:S(2)}) collective-permute-start(bf16[2,96,1024]{2,1,0:T(8,128)(2,1)} %get-tuple-element.24), channel_id=1, source_target_pairs={{0,64},{64,128},{128,192},{192,256},{256,320},{320,384},{384,448},... | collective-permute-start | bytes 1179656 | tf_op jit(solution)/shard_map/ppermute | solution.py:176
  194.8 0.7 copy-start.4
  202.8 9.9 %collective-permute-start.3 = (bf16[2,96,1024]{2,1,0:T(8,128)(2,1)}, bf16[2,96,1024]{2,1,0:T(8,128)(2,1)S(1)}, u32[]{:S(2)}, u32[]{:S(2)}) collective-permute-start(bf16[2,96,1024]{2,1,0:T(8,128)(2,1)} %get-tuple-element.26), channel_id=1, source_target_pairs={{0,64},{64,128},{128,192},{192,256},{256,320},{320,384},{384,448},... | collective-permute-start | bytes 1179656 | tf_op jit(solution)/shard_map/ppermute | solution.py:176
  212.7 0.7 copy-start.5
  220.8 9.9 %collective-permute-start.4 = (bf16[2,96,1024]{2,1,0:T(8,128)(2,1)}, bf16[2,96,1024]{2,1,0:T(8,128)(2,1)S(1)}, u32[]{:S(2)}, u32[]{:S(2)}) collective-permute-start(bf16[2,96,1024]{2,1,0:T(8,128)(2,1)} %get-tuple-element.28), channel_id=1, source_target_pairs={{0,64},{64,128},{128,192},{192,256},{256,320},{320,384},{384,448},... | collective-permute-start | bytes 1179656 | tf_op jit(solution)/shard_map/ppermute | solution.py:176
  230.7 0.7 copy-start.6
  238.7 9.9 %collective-permute-start.5 = (bf16[2,96,1024]{2,1,0:T(8,128)(2,1)}, bf16[2,96,1024]{2,1,0:T(8,128)(2,1)S(1)}, u32[]{:S(2)}, u32[]{:S(2)}) collective-permute-start(bf16[2,96,1024]{2,1,0:T(8,128)(2,1)} %get-tuple-element.30), channel_id=1, source_target_pairs={{0,64},{64,128},{128,192},{192,256},{256,320},{320,384},{384,448},... | collective-permute-start | bytes 1179656 | tf_op jit(solution)/shard_map/ppermute | solution.py:176
  248.6 0.7 copy-start.7
  256.6 9.9 %collective-permute-start.6 = (bf16[2,96,1024]{2,1,0:T(8,128)(2,1)}, bf16[2,96,1024]{2,1,0:T(8,128)(2,1)S(1)}, u32[]{:S(2)}, u32[]{:S(2)}) collective-permute-start(bf16[2,96,1024]{2,1,0:T(8,128)(2,1)} %get-tuple-element.32), channel_id=1, source_target_pairs={{0,64},{64,128},{128,192},{192,256},{256,320},{320,384},{384,448},... | collective-permute-start | bytes 1179656 | tf_op jit(solution)/shard_map/ppermute | solution.py:176
  266.5 0.7 copy-start.1
Sparse Core Ops, SparseCore 0:
  10.7 92.6 all-gather.3

commit v2 on v1

--- a/solution.py
+++ b/solution.py
@@ -10,17 +10,23 @@
 SIZES = (8, 4, 8, 2)
 CH_AXES = ("z", "core")
 PLANE = ("x", "z", "core")
-VMEM = 56 * 1024 * 1024
-
-
-def spread_kernel(x_ref, v_ref, p_ref, out_ref):
+VMEM = 16 * 1024 * 1024
+
+
+def spread_kernel(x_ref, v_ref, p_ref, limit_ref, out_ref):
+    e = pl.program_id(0)
     both = jnp.concatenate([v_ref[0], p_ref[0]], axis=0).astype(jnp.float32)
     turned = both.T.astype(jnp.bfloat16)
     groups, _, per, lanes = out_ref.shape
     out_ref[...] = turned.reshape(groups, 1, per, lanes)
 
-
-def spread(x_index, start):
+    @pl.when(e == pl.num_programs(0) - 1)
+    def _():
+        for k in range(groups):
+            out_ref[k, 0] = limit_ref[...]
+
+
+def spread(x_index, start, limits):
     energies, rows, width = start.shape
     cols = width // 8
     per = cols // 16
@@ -28,31 +34,31 @@
         spread_kernel,
         grid_spec=pltpu.PrefetchScalarGridSpec(
             num_scalar_prefetch=1,
-            grid=(energies,),
+            grid=(energies + 1,),
             in_specs=[
-                pl.BlockSpec((1, rows, cols), lambda e, x: (e, 0, x[0])),
-                pl.BlockSpec((1, rows, cols), lambda e, x: (e, 0, 4 + x[0])),
+                pl.BlockSpec((1, rows, cols), lambda e, x: (jnp.minimum(e, energies - 1), 0, x[0])),
+                pl.BlockSpec((1, rows, cols), lambda e, x: (jnp.minimum(e, energies - 1), 0, 4 + x[0])),
+                pl.BlockSpec(limits.shape, lambda e, x: (0, 0)),
             ],
             out_specs=pl.BlockSpec((16, 1, per, 2 * rows), lambda e, x: (0, e, 0, 0)),
         ),
-        out_shape=jax.ShapeDtypeStruct((16, energies, per, 2 * rows), start.dtype),
+        out_shape=jax.ShapeDtypeStruct((16, energies + 1, per, 2 * rows), start.dtype),
         name="spread",
-    )(x_index, start, start)
+    )(x_index, start, start, limits)
 
 
 def join_kernel(in_ref, out_ref):
-    rows = in_ref.shape[1]
+    rows = out_ref.shape[1]
     low = lax.broadcasted_iota(jnp.int32, (rows, 128), 1) < 64
     for z in range(8):
-        one = in_ref[2 * z].astype(jnp.float32)
-        two = in_ref[2 * z + 1].astype(jnp.float32)
+        one = in_ref[2 * z, pl.ds(0, rows)].astype(jnp.float32)
+        two = in_ref[2 * z + 1, pl.ds(0, rows)].astype(jnp.float32)
         lanes = pl.ds(128 * z, 128)
         out_ref[0, :, lanes] = jnp.where(low, one, pltpu.roll(two, 64, 1)).astype(out_ref.dtype)
         out_ref[1, :, lanes] = jnp.where(low, pltpu.roll(one, 64, 1), two).astype(out_ref.dtype)
 
 
-def join(pieces):
-    rows = pieces.shape[1]
+def join(pieces, rows):
     return pl.pallas_call(
         join_kernel,
         out_shape=jax.ShapeDtypeStruct((2, rows, 1024), pieces.dtype),
@@ -80,8 +86,12 @@
         slopes = now[pl.ds(rows + per * e, per), :].astype(jnp.float32)
         rot[pl.ds(per * e, per), :] = (cosine * values + ratio * slopes).astype(rot.dtype)
         rot[pl.ds(rows + per * e, per), :] = (cosine * slopes - product * values).astype(rot.dtype)
+    channels = now.shape[1]
     fresh = lax.dot_general(
-        rot[...], basis_ref[0], (((1,), (1,)), ((), ())), preferred_element_type=jnp.float32
+        rot[...],
+        basis_ref[...].reshape(channels, channels),
+        (((1,), (1,)), ((), ())),
+        preferred_element_type=jnp.float32,
     )
     rounded = fresh.astype(now.dtype)
     now[...] = rounded
@@ -100,7 +110,7 @@
 
 
 def stage(active, state, basis, coefs, kept):
-    sectors, channels, _ = basis.shape
+    groups, sectors, share, channels = basis.shape
     rows = state.shape[1]
     return pl.pallas_call(
         stage_kernel,
@@ -109,7 +119,7 @@
             grid=(sectors,),
             in_specs=[
                 pl.BlockSpec(state.shape, lambda s, a: (0, 0, 0)),
-                pl.BlockSpec((1, channels, channels), lambda s, a: (s, 0, 0)),
+                pl.BlockSpec((groups, 1, share, channels), lambda s, a: (0, s, 0, 0)),
                 pl.BlockSpec((1,) + coefs.shape[1:], lambda s, a: (s, 0, 0, 0)),
                 pl.BlockSpec(memory_space=pl.ANY),
             ],
@@ -149,7 +159,6 @@
         in_specs=[pl.BlockSpec((groups, 1, per, lanes), lambda e: (0, e, 0, 0))],
         out_specs=pl.BlockSpec((1, lanes // 2, 2 * groups * per), lambda e: (e, 0, 0)),
         out_shape=jax.ShapeDtypeStruct((energies, lanes // 2, 2 * groups * per), pieces.dtype),
-        compiler_params=pltpu.CompilerParams(vmem_limit_bytes=VMEM),
         name="finish",
     )(pieces)
 
@@ -160,16 +169,21 @@
     x_index = lax.axis_index("x").astype(jnp.int32).reshape(1)
     count = energies.shape[0]
     channels = intersection.shape[2]
-    basis = lax.all_gather(intersection[0], PLANE, tiled=True).reshape(4, channels, channels)
-    limits = lax.all_gather(thresholds[0], PLANE, tiled=True).reshape(4, 1, channels)
+    share = intersection.shape[1]
+    extra = jnp.pad(thresholds, ((0, 7), (0, channels - share)))
+    ring = lax.all_gather(jnp.concatenate([intersection[0], extra]), "x")
+    basis = lax.all_gather(ring[:, :share], CH_AXES)
+    limits = jnp.pad(ring[:, share, :share].reshape(2, 2 * share), ((0, 14), (0, 0)))
+
+    blocks = spread(x_index, start_amps, limits)
+    per, lanes = blocks.shape[2:]
+    rows = count * per
+    blocks = lax.all_to_all(blocks.reshape(16, rows + per, lanes), CH_AXES, 0, 0)
+    state = join(blocks, rows)
+    limits = blocks[:, rows : rows + 2].reshape(16, 4, share).swapaxes(0, 1).reshape(4, 1, channels)
     wave = jnp.sqrt(energies[None, :, None] - limits.astype(jnp.float32))
     sine = jnp.sin(wave)
     coefs = jnp.stack([jnp.cos(wave), sine / wave, wave * sine], axis=1)
-
-    blocks = spread(x_index, start_amps)
-    per, lanes = blocks.shape[2:]
-    rows = count * per
-    state = join(lax.all_to_all(blocks.reshape(16, rows, lanes), CH_AXES, 0, 0))
     kept = jnp.zeros((5, 16, rows, lanes), jnp.bfloat16)
     for step in range(planes):
         if step:

time: 372 us -> 301 us (0.81)
  blocking collectives: 193 us -> 64.5 us
  waiting for transfers between devices: 58.5 us -> 116 us
  Pallas kernels: 68.6 us -> 46.7 us
  local copies, waits for them, and re-layouts: 10.7 us -> 29.8 us
    unnamed x1 -> x0, blocking collectives: 110 us -> none
    all_gather x1, waiting for transfers between devices: 0.01 us -> 32.4 us  [per_device(): basis = lax.all_gather(ring[:, :share], CH_AXES)]
    all_to_all x1, blocking collectives: 83.5 us -> 54.5 us  [per_device(): back = lax.all_to_all(kept[:4].reshape(64, rows, lanes), PLANE, 0, 0)]
    pallas_call x8, Pallas kernels: 57.9 us -> 35.7 us  [stage(): pl.pallas_call(stage_kernel, grid_spec=pltpu.PrefetchScalarGridSpec(num_s...]
    unnamed x23 -> x22, local copies, waits for them, and re-layouts: 7.51 us -> 27.7 us
    all_to_all x1, waiting for transfers between devices: 0.01 us -> 19.2 us  [per_device(): lax.all_to_all(blocks.reshape(16, rows + per, lanes), CH_AXES, 0, 0)]
    all_gather x0 -> x1, blocking collectives: none -> 10 us  [per_device(): ring = lax.all_gather(jnp.concatenate([intersection[0], extra]), 'x')]
    ppermute x7, waiting for transfers between devices: 57.8 us -> 63.9 us  [per_device(): state = lax.ppermute(state, 'y', [(k, k + 1) for k in range(planes - 1)])]
  transfers between devices with their start and end apart: 9 -> 9, of which waited for: 7 -> 9; matrix products, arithmetic and copies ran while one was open for 1% -> 1% of each run, Pallas kernels for 2% -> 2%
where the time goes in v2:
time: 301 us; the launch traced here: 300 us
  waiting for transfers between devices  116 us (39%)
  blocking collectives  64.5 us (21%)
  Pallas kernels  46.7 us (16%)
  local copies, waits for them, and re-layouts  29.8 us (10%)
  starting transfers between devices  28.4 us (9%)
  between operations  13.6 us (5%)
    ppermute x7, waiting for transfers between devices, per_device(): state = lax.ppermute(state, 'y', [(k, k + 1) for k in range(planes - 1)])  63.9 us
    all_to_all x1, blocking collectives, per_device(): back = lax.all_to_all(kept[:4].reshape(64, rows, lanes), PLANE, 0, 0)  54.5 us
    pallas_call x8, Pallas kernels, stage(): pl.pallas_call(stage_kernel, grid_spec=pltpu.PrefetchScalarGridSpec(num_s...  35.7 us
    all_gather x1, waiting for transfers between devices, per_device(): basis = lax.all_gather(ring[:, :share], CH_AXES)  32.4 us
    unnamed x22, local copies, waits for them, and re-layouts  27.7 us
    all_to_all x1, waiting for transfers between devices, per_device(): lax.all_to_all(blocks.reshape(16, rows + per, lanes), CH_AXES, 0, 0)  19.2 us
    all_to_all x1, starting transfers between devices, per_device(): lax.all_to_all(blocks.reshape(16, rows + per, lanes), CH_AXES, 0, 0)  14.6 us
    ppermute x7, starting transfers between devices, per_device(): state = lax.ppermute(state, 'y', [(k, k + 1) for k in range(planes - 1)])  13.8 us
  transfers between devices with their start and end apart: 9, of which 9 were waited for; matrix products, arithmetic and copies ran while one was open for 1% of the time, Pallas kernels for 2%

profile of v2, /device:TPU:39, one launch (start us, length us, event | category | flops | bytes accessed | tf_op | source)
XLA Modules:
  0.0 300.2 jit_solution(3448790155863701103)
XLA Ops:
  7.5 10.0 %all-gather = bf16[288,1024]{1,0:T(8,128)(2,1)S(1)} all-gather(bf16[72,1024]{1,0:T(8,128)(2,1)S(1)} %fusion.1), channel_id=2, replica_groups=mesh['y'=8,'x'=4,'z'=8,'core'=2] {'x'}, dimensions={0}, use_global_device_ids=true | all-gather | bytes 737280 | tf_op jit(solution)/shard_map/all_gather | solution.py:174
  19.1 4.1 %spread.1 = bf16[16,7,16,128]{3,2,1,0:T(8,128)(2,1)} custom-call(s32[1]{0:T(128)} %bitcast.8.x_ref, bf16[6,64,2048]{2,1,0:T(8,128)(2,1)} %p_ref.1, bf16[6,64,2048]{2,1,0:T(8,128)(2,1)} %p_ref.1, bf16[16,128]{1,0:T(8,128)(2,1)} %pad.9.limit_ref), custom_call_target="tpu_custom_call" | custom-call | tf_op jit(solution)/shard_map/spread/pallas_call | solution.py:33
  23.2 14.6 %all-to-all-start = ((bf16[16,112,128]{2,1,0:T(8,128)(2,1)}), bf16[16,112,128]{2,1,0:T(8,128)(2,1)S(1)}, u32[]{:S(2)}, u32[]{:S(2)}) async-start(bf16[16,112,128]{2,1,0:T(8,128)(2,1)} %bitcast.29), calls=%async_computation | async-start | bytes 917504 | tf_op jit(solution)/shard_map/all_to_all | solution.py:181
  37.8 19.2 %all-to-all-done.in_ref = bf16[16,112,128]{2,1,0:T(8,128)(2,1)S(1)} async-done(((bf16[16,112,128]{2,1,0:T(8,128)(2,1)}), bf16[16,112,128]{2,1,0:T(8,128)(2,1)S(1)}, u32[]{:S(2)}, u32[]{:S(2)}) %all-to-all-start) | async-done | bytes 458784 | tf_op jit(solution)/shard_map/all_to_all | solution.py:181
  57.8 2.0 join.1.state_ref
  60.4 32.4 %all-gather.4.cloned.1.call-done = bf16[64,64,1024]{2,1,0:T(8,128)(2,1)} async-done(((bf16[4,64,1024]{2,1,0:T(8,128)(2,1)}), bf16[64,64,1024]{2,1,0:T(8,128)(2,1)}) %all-gather.4.cloned.1.call-update) | async-done | bytes 8388624 | tf_op jit(solution)/shard_map/all_gather | solution.py:175
  93.2 3.4 %copy-done = bf16[64,64,1024]{2,1,0:T(8,128)(2,1)S(1)} copy-done((bf16[64,64,1024]{2,1,0:T(8,128)(2,1)S(1)}, bf16[64,64,1024]{2,1,0:T(8,128)(2,1)}, u32[]{:S(2)}) %copy-start) | copy-done | bytes 8388632
  96.5 4.4 %stage.8 = (bf16[2,96,1024]{2,1,0:T(8,128)(2,1)S(1)}, bf16[5,16,96,128]{3,2,1,0:T(8,128)(2,1)S(1)}) custom-call(s32[1]{0:T(128)} %bitcast.7.active, bf16[2,96,1024]{2,1,0:T(8,128)(2,1)S(1)} %copy-done.8, bf16[16,4,64,1024]{3,2,1,0:T(8,128)(2,1)S(1)} %bitcast.17, f32[4,3,6,1024]{3,2,1,0:T(8,128)S(1)} %pad_maximum_fusion.coef_ref, ...), custom_call_target="tpu_custom_call", output_to_operand_aliasing={{1}: (4, {})} | custom-call | tf_op jit(solution)/shard_map/stage/pallas_call | solution.py:115
  100.9 2.3 collective-permute-start
  103.2 11.2 %collective-permute-done.state_ref = bf16[2,96,1024]{2,1,0:T(8,128)(2,1)S(1)} collective-permute-done((bf16[2,96,1024]{2,1,0:T(8,128)(2,1)S(1)}, bf16[2,96,1024]{2,1,0:T(8,128)(2,1)S(1)}, u32[]{:S(2)}, u32[]{:S(2)}) %collective-permute-start) | collective-permute-done | bytes 393248 | tf_op jit(solution)/shard_map/ppermute | solution.py:190
  114.5 3.4 %copy-done.1 = bf16[64,64,1024]{2,1,0:T(8,128)(2,1)S(1)} copy-done((bf16[64,64,1024]{2,1,0:T(8,128)(2,1)S(1)}, bf16[64,64,1024]{2,1,0:T(8,128)(2,1)}, u32[]{:S(2)}) %copy-start.1) | copy-done | bytes 8388632
  117.9 4.4 %stage.9 = (bf16[2,96,1024]{2,1,0:T(8,128)(2,1)S(1)}, bf16[5,16,96,128]{3,2,1,0:T(8,128)(2,1)S(1)}) custom-call(s32[1]{0:T(128)} %bitcast.6.active, bf16[2,96,1024]{2,1,0:T(8,128)(2,1)S(1)} %collective-permute-done.state_ref, bf16[16,4,64,1024]{3,2,1,0:T(8,128)(2,1)S(1)} %bitcast.18, ...), custom_call_target="tpu_custom_call", output_to_operand_aliasing={{1}: (4, {})} | custom-call | tf_op jit(solution)/shard_map/stage/pallas_call | solution.py:115
  124.2 10.7 %collective-permute-done.1.state_ref = bf16[2,96,1024]{2,1,0:T(8,128)(2,1)S(1)} collective-permute-done((bf16[2,96,1024]{2,1,0:T(8,128)(2,1)S(1)}, bf16[2,96,1024]{2,1,0:T(8,128)(2,1)S(1)}, u32[]{:S(2)}, u32[]{:S(2)}) %collective-permute-start.1) | collective-permute-done | bytes 393248 | tf_op jit(solution)/shard_map/ppermute | solution.py:190
  134.9 3.4 %copy-done.2 = bf16[64,64,1024]{2,1,0:T(8,128)(2,1)S(1)} copy-done((bf16[64,64,1024]{2,1,0:T(8,128)(2,1)S(1)}, bf16[64,64,1024]{2,1,0:T(8,128)(2,1)}, u32[]{:S(2)}) %copy-start.2) | copy-done | bytes 8388632
  138.3 4.4 %stage.10 = (bf16[2,96,1024]{2,1,0:T(8,128)(2,1)S(1)}, bf16[5,16,96,128]{3,2,1,0:T(8,128)(2,1)S(1)}) custom-call(s32[1]{0:T(128)} %bitcast.5.active, bf16[2,96,1024]{2,1,0:T(8,128)(2,1)S(1)} %collective-permute-done.1.state_ref, bf16[16,4,64,1024]{3,2,1,0:T(8,128)(2,1)S(1)} %bitcast.19, ...), custom_call_target="tpu_custom_call", output_to_operand_aliasing={{1}: (4, {})} | custom-call | tf_op jit(solution)/shard_map/stage/pallas_call | solution.py:115
  144.6 9.8 %collective-permute-done.2.state_ref = bf16[2,96,1024]{2,1,0:T(8,128)(2,1)S(1)} collective-permute-done((bf16[2,96,1024]{2,1,0:T(8,128)(2,1)S(1)}, bf16[2,96,1024]{2,1,0:T(8,128)(2,1)S(1)}, u32[]{:S(2)}, u32[]{:S(2)}) %collective-permute-start.2) | collective-permute-done | bytes 393248 | tf_op jit(solution)/shard_map/ppermute | solution.py:190
  154.4 3.4 %copy-done.3 = bf16[64,64,1024]{2,1,0:T(8,128)(2,1)S(1)} copy-done((bf16[64,64,1024]{2,1,0:T(8,128)(2,1)S(1)}, bf16[64,64,1024]{2,1,0:T(8,128)(2,1)}, u32[]{:S(2)}) %copy-start.3) | copy-done | bytes 8388632
  157.7 4.4 %stage.11 = (bf16[2,96,1024]{2,1,0:T(8,128)(2,1)S(1)}, bf16[5,16,96,128]{3,2,1,0:T(8,128)(2,1)S(1)}) custom-call(s32[1]{0:T(128)} %bitcast.4.active, bf16[2,96,1024]{2,1,0:T(8,128)(2,1)S(1)} %collective-permute-done.2.state_ref, bf16[16,4,64,1024]{3,2,1,0:T(8,128)(2,1)S(1)} %bitcast.20, ...), custom_call_target="tpu_custom_call", output_to_operand_aliasing={{1}: (4, {})} | custom-call | tf_op jit(solution)/shard_map/stage/pallas_call | solution.py:115
  164.0 8.8 %collective-permute-done.3.state_ref = bf16[2,96,1024]{2,1,0:T(8,128)(2,1)S(1)} collective-permute-done((bf16[2,96,1024]{2,1,0:T(8,128)(2,1)S(1)}, bf16[2,96,1024]{2,1,0:T(8,128)(2,1)S(1)}, u32[]{:S(2)}, u32[]{:S(2)}) %collective-permute-start.3) | collective-permute-done | bytes 393248 | tf_op jit(solution)/shard_map/ppermute | solution.py:190
  172.9 3.4 %copy-done.4 = bf16[64,64,1024]{2,1,0:T(8,128)(2,1)S(1)} copy-done((bf16[64,64,1024]{2,1,0:T(8,128)(2,1)S(1)}, bf16[64,64,1024]{2,1,0:T(8,128)(2,1)}, u32[]{:S(2)}) %copy-start.4) | copy-done | bytes 8388632
  176.3 4.4 %stage.12 = (bf16[2,96,1024]{2,1,0:T(8,128)(2,1)S(1)}, bf16[5,16,96,128]{3,2,1,0:T(8,128)(2,1)S(1)}) custom-call(s32[1]{0:T(128)} %bitcast.3.active, bf16[2,96,1024]{2,1,0:T(8,128)(2,1)S(1)} %collective-permute-done.3.state_ref, bf16[16,4,64,1024]{3,2,1,0:T(8,128)(2,1)S(1)} %bitcast.21, ...), custom_call_target="tpu_custom_call", output_to_operand_aliasing={{1}: (4, {})} | custom-call | tf_op jit(solution)/shard_map/stage/pallas_call | solution.py:115
  182.6 7.8 %collective-permute-done.4.state_ref = bf16[2,96,1024]{2,1,0:T(8,128)(2,1)S(1)} collective-permute-done((bf16[2,96,1024]{2,1,0:T(8,128)(2,1)S(1)}, bf16[2,96,1024]{2,1,0:T(8,128)(2,1)S(1)}, u32[]{:S(2)}, u32[]{:S(2)}) %collective-permute-start.4) | collective-permute-done | bytes 393248 | tf_op jit(solution)/shard_map/ppermute | solution.py:190
  190.4 3.4 %copy-done.5 = bf16[64,64,1024]{2,1,0:T(8,128)(2,1)S(1)} copy-done((bf16[64,64,1024]{2,1,0:T(8,128)(2,1)S(1)}, bf16[64,64,1024]{2,1,0:T(8,128)(2,1)}, u32[]{:S(2)}) %copy-start.5) | copy-done | bytes 8388632
  193.8 4.4 %stage.13 = (bf16[2,96,1024]{2,1,0:T(8,128)(2,1)S(1)}, bf16[5,16,96,128]{3,2,1,0:T(8,128)(2,1)S(1)}) custom-call(s32[1]{0:T(128)} %bitcast.2.active, bf16[2,96,1024]{2,1,0:T(8,128)(2,1)S(1)} %collective-permute-done.4.state_ref, bf16[16,4,64,1024]{3,2,1,0:T(8,128)(2,1)S(1)} %bitcast.22, ...), custom_call_target="tpu_custom_call", output_to_operand_aliasing={{1}: (4, {})} | custom-call | tf_op jit(solution)/shard_map/stage/pallas_call | solution.py:115
  200.1 7.8 %collective-permute-done.5.state_ref = bf16[2,96,1024]{2,1,0:T(8,128)(2,1)S(1)} collective-permute-done((bf16[2,96,1024]{2,1,0:T(8,128)(2,1)S(1)}, bf16[2,96,1024]{2,1,0:T(8,128)(2,1)S(1)}, u32[]{:S(2)}, u32[]{:S(2)}) %collective-permute-start.5) | collective-permute-done | bytes 393248 | tf_op jit(solution)/shard_map/ppermute | solution.py:190
  207.9 3.4 %copy-done.6 = bf16[64,64,1024]{2,1,0:T(8,128)(2,1)S(1)} copy-done((bf16[64,64,1024]{2,1,0:T(8,128)(2,1)S(1)}, bf16[64,64,1024]{2,1,0:T(8,128)(2,1)}, u32[]{:S(2)}) %copy-start.6) | copy-done | bytes 8388632
  211.3 4.4 %stage.14 = (bf16[2,96,1024]{2,1,0:T(8,128)(2,1)S(1)}, bf16[5,16,96,128]{3,2,1,0:T(8,128)(2,1)S(1)}) custom-call(s32[1]{0:T(128)} %bitcast.1.active, bf16[2,96,1024]{2,1,0:T(8,128)(2,1)S(1)} %collective-permute-done.5.state_ref, bf16[16,4,64,1024]{3,2,1,0:T(8,128)(2,1)S(1)} %bitcast.23, ...), custom_call_target="tpu_custom_call", output_to_operand_aliasing={{1}: (4, {})} | custom-call | tf_op jit(solution)/shard_map/stage/pallas_call | solution.py:115
  217.6 7.8 %collective-permute-done.6.state_ref = bf16[2,96,1024]{2,1,0:T(8,128)(2,1)S(1)} collective-permute-done((bf16[2,96,1024]{2,1,0:T(8,128)(2,1)S(1)}, bf16[2,96,1024]{2,1,0:T(8,128)(2,1)S(1)}, u32[]{:S(2)}, u32[]{:S(2)}) %collective-permute-start.6) | collective-permute-done | bytes 393248 | tf_op jit(solution)/shard_map/ppermute | solution.py:190
  225.4 3.4 %copy-done.7 = bf16[64,64,1024]{2,1,0:T(8,128)(2,1)S(1)} copy-done((bf16[64,64,1024]{2,1,0:T(8,128)(2,1)S(1)}, bf16[64,64,1024]{2,1,0:T(8,128)(2,1)}, u32[]{:S(2)}) %copy-start.7) | copy-done | bytes 8388632
  228.8 5.1 %stage.15 = (bf16[2,96,1024]{2,1,0:T(8,128)(2,1)}, bf16[5,16,96,128]{3,2,1,0:T(8,128)(2,1)S(1)}) custom-call(s32[1]{0:T(128)} %bitcast.active, bf16[2,96,1024]{2,1,0:T(8,128)(2,1)S(1)} %collective-permute-done.6.state_ref, bf16[16,4,64,1024]{3,2,1,0:T(8,128)(2,1)S(1)} %bitcast.24, ...), custom_call_target="tpu_custom_call", output_to_operand_aliasing={{1}: (4, {})} | custom-call | tf_op jit(solution)/shard_map/stage/pallas_call | solution.py:115
  234.0 54.5 %all_to_all.10 = bf16[64,96,128]{2,1,0:T(8,128)(2,1)} all-to-all(bf16[64,96,128]{2,1,0:T(8,128)(2,1)S(1)} %bitcast.25), channel_id=1, replica_groups=mesh['y'=8,'x'=4,'z'=8,'core'=2] {'x','z','core'}, dimensions={0} | all-to-all | bytes 3145728 | tf_op jit(solution)/shard_map/all_to_all | solution.py:193
  288.5 4.9 %finish.1 = bf16[6,64,2048]{2,1,0:T(8,128)(2,1)} custom-call(bf16[64,6,16,128]{3,2,1,0:T(8,128)(2,1)} %bitcast.26), custom_call_target="tpu_custom_call" | custom-call | tf_op jit(solution)/shard_map/finish/pallas_call | solution.py:156
  (35 shorter events, 15.9 us)
Async XLA Ops:
  6.5 86.3 %all-gather.4.cloned.1.call-start = ((), (), s32[]{:S(2)}) async-start(), calls=%async_computation.2 | async-start | bytes 8912896 | tf_op jit(solution)/shard_map/all_gather | solution.py:175
  19.1 40.7 %copy-start.10 = (f32[6]{0:T(128)S(1)}, f32[6]{0:T(128)}, u32[]{:S(2)}) copy-start(f32[6]{0:T(128)} %param.5) | copy-start | bytes 76
  23.2 33.7 %all-to-all-start = ((bf16[16,112,128]{2,1,0:T(8,128)(2,1)}), bf16[16,112,128]{2,1,0:T(8,128)(2,1)S(1)}, u32[]{:S(2)}, u32[]{:S(2)}) async-start(bf16[16,112,128]{2,1,0:T(8,128)(2,1)} %bitcast.29), calls=%async_computation | async-start | bytes 917504 | tf_op jit(solution)/shard_map/all_to_all | solution.py:181
  56.9 0.8 copy-start.9
  59.8 33.4 %copy-start.8 = (bf16[2,96,1024]{2,1,0:T(8,128)(2,1)S(1)}, bf16[2,96,1024]{2,1,0:T(8,128)(2,1)}, u32[]{:S(2)}) copy-start(bf16[2,96,1024]{2,1,0:T(8,128)(2,1)} %join.1.state_ref) | copy-start | bytes 1179652
  93.2 3.4 %copy-start = (bf16[64,64,1024]{2,1,0:T(8,128)(2,1)S(1)}, bf16[64,64,1024]{2,1,0:T(8,128)(2,1)}, u32[]{:S(2)}) copy-start(bf16[64,64,1024]{2,1,0:T(8,128)(2,1)} %all-gather.4.cloned.1.call-done) | copy-start | bytes 25165828
  100.9 13.6 %collective-permute-start = (bf16[2,96,1024]{2,1,0:T(8,128)(2,1)S(1)}, bf16[2,96,1024]{2,1,0:T(8,128)(2,1)S(1)}, u32[]{:S(2)}, u32[]{:S(2)}) collective-permute-start(bf16[2,96,1024]{2,1,0:T(8,128)(2,1)S(1)} %get-tuple-element.20), channel_id=1, source_target_pairs={{0,64},{64,128},{128,192},{192,256},{256,320},{320,384},{384,448},... | collective-permute-start | bytes 1179656 | tf_op jit(solution)/shard_map/ppermute | solution.py:190
  114.5 3.4 %copy-start.1 = (bf16[64,64,1024]{2,1,0:T(8,128)(2,1)S(1)}, bf16[64,64,1024]{2,1,0:T(8,128)(2,1)}, u32[]{:S(2)}) copy-start(bf16[64,64,1024]{2,1,0:T(8,128)(2,1)} %all-gather.4.cloned.1.call-done) | copy-start | bytes 25165828
  122.2 12.6 %collective-permute-start.1 = (bf16[2,96,1024]{2,1,0:T(8,128)(2,1)S(1)}, bf16[2,96,1024]{2,1,0:T(8,128)(2,1)S(1)}, u32[]{:S(2)}, u32[]{:S(2)}) collective-permute-start(bf16[2,96,1024]{2,1,0:T(8,128)(2,1)S(1)} %get-tuple-element.22), channel_id=1, source_target_pairs={{0,64},{64,128},{128,192},{192,256},{256,320},{320,384},{384,448},... | collective-permute-start | bytes 1179656 | tf_op jit(solution)/shard_map/ppermute | solution.py:190
  134.9 3.4 %copy-start.2 = (bf16[64,64,1024]{2,1,0:T(8,128)(2,1)S(1)}, bf16[64,64,1024]{2,1,0:T(8,128)(2,1)}, u32[]{:S(2)}) copy-start(bf16[64,64,1024]{2,1,0:T(8,128)(2,1)} %all-gather.4.cloned.1.call-done) | copy-start | bytes 25165828
  142.6 11.7 %collective-permute-start.2 = (bf16[2,96,1024]{2,1,0:T(8,128)(2,1)S(1)}, bf16[2,96,1024]{2,1,0:T(8,128)(2,1)S(1)}, u32[]{:S(2)}, u32[]{:S(2)}) collective-permute-start(bf16[2,96,1024]{2,1,0:T(8,128)(2,1)S(1)} %get-tuple-element.24), channel_id=1, source_target_pairs={{0,64},{64,128},{128,192},{192,256},{256,320},{320,384},{384,448},... | collective-permute-start | bytes 1179656 | tf_op jit(solution)/shard_map/ppermute | solution.py:190
  154.3 3.4 %copy-start.3 = (bf16[64,64,1024]{2,1,0:T(8,128)(2,1)S(1)}, bf16[64,64,1024]{2,1,0:T(8,128)(2,1)}, u32[]{:S(2)}) copy-start(bf16[64,64,1024]{2,1,0:T(8,128)(2,1)} %all-gather.4.cloned.1.call-done) | copy-start | bytes 25165828
  162.1 10.8 %collective-permute-start.3 = (bf16[2,96,1024]{2,1,0:T(8,128)(2,1)S(1)}, bf16[2,96,1024]{2,1,0:T(8,128)(2,1)S(1)}, u32[]{:S(2)}, u32[]{:S(2)}) collective-permute-start(bf16[2,96,1024]{2,1,0:T(8,128)(2,1)S(1)} %get-tuple-element.26), channel_id=1, source_target_pairs={{0,64},{64,128},{128,192},{192,256},{256,320},{320,384},{384,448},... | collective-permute-start | bytes 1179656 | tf_op jit(solution)/shard_map/ppermute | solution.py:190
  172.9 3.4 %copy-start.4 = (bf16[64,64,1024]{2,1,0:T(8,128)(2,1)S(1)}, bf16[64,64,1024]{2,1,0:T(8,128)(2,1)}, u32[]{:S(2)}) copy-start(bf16[64,64,1024]{2,1,0:T(8,128)(2,1)} %all-gather.4.cloned.1.call-done) | copy-start | bytes 25165828
  180.7 9.7 %collective-permute-start.4 = (bf16[2,96,1024]{2,1,0:T(8,128)(2,1)S(1)}, bf16[2,96,1024]{2,1,0:T(8,128)(2,1)S(1)}, u32[]{:S(2)}, u32[]{:S(2)}) collective-permute-start(bf16[2,96,1024]{2,1,0:T(8,128)(2,1)S(1)} %get-tuple-element.28), channel_id=1, source_target_pairs={{0,64},{64,128},{128,192},{192,256},{256,320},{320,384},{384,448},... | collective-permute-start | bytes 1179656 | tf_op jit(solution)/shard_map/ppermute | solution.py:190
  190.4 3.4 %copy-start.5 = (bf16[64,64,1024]{2,1,0:T(8,128)(2,1)S(1)}, bf16[64,64,1024]{2,1,0:T(8,128)(2,1)}, u32[]{:S(2)}) copy-start(bf16[64,64,1024]{2,1,0:T(8,128)(2,1)} %all-gather.4.cloned.1.call-done) | copy-start | bytes 25165828
  198.2 9.7 %collective-permute-start.5 = (bf16[2,96,1024]{2,1,0:T(8,128)(2,1)S(1)}, bf16[2,96,1024]{2,1,0:T(8,128)(2,1)S(1)}, u32[]{:S(2)}, u32[]{:S(2)}) collective-permute-start(bf16[2,96,1024]{2,1,0:T(8,128)(2,1)S(1)} %get-tuple-element.30), channel_id=1, source_target_pairs={{0,64},{64,128},{128,192},{192,256},{256,320},{320,384},{384,448},... | collective-permute-start | bytes 1179656 | tf_op jit(solution)/shard_map/ppermute | solution.py:190
  207.9 3.4 %copy-start.6 = (bf16[64,64,1024]{2,1,0:T(8,128)(2,1)S(1)}, bf16[64,64,1024]{2,1,0:T(8,128)(2,1)}, u32[]{:S(2)}) copy-start(bf16[64,64,1024]{2,1,0:T(8,128)(2,1)} %all-gather.4.cloned.1.call-done) | copy-start | bytes 25165828
  215.7 9.7 %collective-permute-start.6 = (bf16[2,96,1024]{2,1,0:T(8,128)(2,1)S(1)}, bf16[2,96,1024]{2,1,0:T(8,128)(2,1)S(1)}, u32[]{:S(2)}, u32[]{:S(2)}) collective-permute-start(bf16[2,96,1024]{2,1,0:T(8,128)(2,1)S(1)} %get-tuple-element.32), channel_id=1, source_target_pairs={{0,64},{64,128},{128,192},{192,256},{256,320},{320,384},{384,448},... | collective-permute-start | bytes 1179656 | tf_op jit(solution)/shard_map/ppermute | solution.py:190
  225.4 3.4 %copy-start.7 = (bf16[64,64,1024]{2,1,0:T(8,128)(2,1)S(1)}, bf16[64,64,1024]{2,1,0:T(8,128)(2,1)}, u32[]{:S(2)}) copy-start(bf16[64,64,1024]{2,1,0:T(8,128)(2,1)} %all-gather.4.cloned.1.call-done) | copy-start | bytes 25165828
Sparse Core Ops, SparseCore 0:
  18.5 74.2 all-gather.3

commit v3 on v2

--- a/solution.py
+++ b/solution.py
@@ -10,7 +10,7 @@
 SIZES = (8, 4, 8, 2)
 CH_AXES = ("z", "core")
 PLANE = ("x", "z", "core")
-VMEM = 16 * 1024 * 1024
+MIB = 1024 * 1024
 
 
 def spread_kernel(x_ref, v_ref, p_ref, limit_ref, out_ref):
@@ -66,8 +66,32 @@
     )(pieces)
 
 
-def stage_kernel(active, state_ref, basis_ref, coef_ref, kept_ref, next_ref, out_ref, now, rot):
-    del active, kept_ref
+def turn_kernel(*refs):
+    out_ref = refs[-1]
+    for q, ref in enumerate(refs[:-1]):
+        groups, _, share, channels = ref.shape
+        block = ref[...].reshape(groups * share, channels)
+        out_ref[0, :, pl.ds(groups * share * q, groups * share)] = block.T
+
+
+def turn(basis):
+    groups, sectors, share, channels = basis.shape
+    part = groups // 4
+    specs = [pl.BlockSpec((part, 1, share, channels), lambda s, q=q: (q, s, 0, 0)) for q in range(4)]
+    return pl.pallas_call(
+        turn_kernel,
+        grid=(sectors,),
+        in_specs=specs,
+        out_specs=pl.BlockSpec((1, channels, groups * share), lambda s: (s, 0, 0)),
+        out_shape=jax.ShapeDtypeStruct((sectors, channels, groups * share), basis.dtype),
+        compiler_params=pltpu.CompilerParams(vmem_limit_bytes=40 * MIB),
+        name="turn",
+    )(basis, basis, basis, basis)
+
+
+def stage_kernel(y_ref, state_ref, basis_ref, coef_ref, *refs):
+    next_ref, out_ref, now, rot = refs[-4:]
+    del y_ref
     s = pl.program_id(0)
     energies = coef_ref.shape[2]
     rows = state_ref.shape[1]
@@ -86,13 +110,7 @@
         slopes = now[pl.ds(rows + per * e, per), :].astype(jnp.float32)
         rot[pl.ds(per * e, per), :] = (cosine * values + ratio * slopes).astype(rot.dtype)
         rot[pl.ds(rows + per * e, per), :] = (cosine * slopes - product * values).astype(rot.dtype)
-    channels = now.shape[1]
-    fresh = lax.dot_general(
-        rot[...],
-        basis_ref[...].reshape(channels, channels),
-        (((1,), (1,)), ((), ())),
-        preferred_element_type=jnp.float32,
-    )
+    fresh = jnp.dot(rot[...], basis_ref[0], preferred_element_type=jnp.float32)
     rounded = fresh.astype(now.dtype)
     now[...] = rounded
     low = lax.broadcasted_iota(jnp.int32, (rows, 128), 1) < 64
@@ -109,23 +127,24 @@
         next_ref[1] = rounded[rows:]
 
 
-def stage(active, state, basis, coefs, kept):
-    groups, sectors, share, channels = basis.shape
+def stage(step, y_index, state, basis, coefs, kept):
+    sectors, channels, _ = basis.shape
     rows = state.shape[1]
+    first = kept is None
     return pl.pallas_call(
         stage_kernel,
         grid_spec=pltpu.PrefetchScalarGridSpec(
             num_scalar_prefetch=1,
             grid=(sectors,),
             in_specs=[
-                pl.BlockSpec(state.shape, lambda s, a: (0, 0, 0)),
-                pl.BlockSpec((groups, 1, share, channels), lambda s, a: (0, s, 0, 0)),
-                pl.BlockSpec((1,) + coefs.shape[1:], lambda s, a: (s, 0, 0, 0)),
-                pl.BlockSpec(memory_space=pl.ANY),
-            ],
+                pl.BlockSpec(state.shape, lambda s, y: (0, 0, 0)),
+                pl.BlockSpec((1, channels, channels), lambda s, y: (s, 0, 0)),
+                pl.BlockSpec((1,) + coefs.shape[1:], lambda s, y: (s, 0, 0, 0)),
+            ]
+            + ([] if first else [pl.BlockSpec(memory_space=pl.ANY)]),
             out_specs=[
-                pl.BlockSpec(state.shape, lambda s, a: (0, 0, 0)),
-                pl.BlockSpec((1, 16, rows, 128), lambda s, a: (jnp.where(a[0] == 1, s, sectors), 0, 0, 0)),
+                pl.BlockSpec(state.shape, lambda s, y: (0, 0, 0)),
+                pl.BlockSpec((1, 16, rows, 128), lambda s, y: (jnp.where(y[0] == step, s, sectors), 0, 0, 0)),
             ],
             scratch_shapes=[
                 pltpu.VMEM((2 * rows, channels), state.dtype),
@@ -134,45 +153,48 @@
         ),
         out_shape=[
             jax.ShapeDtypeStruct(state.shape, state.dtype),
-            jax.ShapeDtypeStruct(kept.shape, kept.dtype),
+            jax.ShapeDtypeStruct((sectors + 1, 16, rows, 128), state.dtype),
         ],
-        input_output_aliases={4: 1},
-        compiler_params=pltpu.CompilerParams(vmem_limit_bytes=VMEM),
+        input_output_aliases={} if first else {4: 1},
+        compiler_params=pltpu.CompilerParams(vmem_limit_bytes=16 * MIB),
         name="stage",
-    )(active, state, basis, coefs, kept)
+    )(y_index, state, basis, coefs, *([] if first else [kept]))
 
 
 def finish_kernel(in_ref, out_ref):
-    groups, _, per, lanes = in_ref.shape
-    turned = in_ref[...].reshape(groups * per, lanes).astype(jnp.float32).T.astype(out_ref.dtype)
+    groups, energies, per, lanes = in_ref.shape
     half = lanes // 2
     cols = groups * per
-    out_ref[0, :, pl.ds(0, cols)] = turned[:half]
-    out_ref[0, :, pl.ds(cols, cols)] = turned[half:]
+    for e in range(energies):
+        turned = in_ref[:, e].reshape(cols, lanes).T
+        out_ref[e, :, pl.ds(0, cols)] = turned[:half]
+        out_ref[e, :, pl.ds(cols, cols)] = turned[half:]
 
 
 def finish(pieces):
     groups, energies, per, lanes = pieces.shape
+    batch = 2
     return pl.pallas_call(
         finish_kernel,
-        grid=(energies,),
-        in_specs=[pl.BlockSpec((groups, 1, per, lanes), lambda e: (0, e, 0, 0))],
-        out_specs=pl.BlockSpec((1, lanes // 2, 2 * groups * per), lambda e: (e, 0, 0)),
+        grid=(energies // batch,),
+        in_specs=[pl.BlockSpec((groups, batch, per, lanes), lambda e: (0, e, 0, 0))],
+        out_specs=pl.BlockSpec((batch, lanes // 2, 2 * groups * per), lambda e: (e, 0, 0)),
         out_shape=jax.ShapeDtypeStruct((energies, lanes // 2, 2 * groups * per), pieces.dtype),
+        compiler_params=pltpu.CompilerParams(vmem_limit_bytes=16 * MIB),
         name="finish",
     )(pieces)
 
 
 def per_device(start_amps, energies, thresholds, intersection):
     planes = lax.axis_size("y")
-    y_index = lax.axis_index("y")
+    y_index = lax.axis_index("y").astype(jnp.int32).reshape(1)
     x_index = lax.axis_index("x").astype(jnp.int32).reshape(1)
     count = energies.shape[0]
     channels = intersection.shape[2]
     share = intersection.shape[1]
     extra = jnp.pad(thresholds, ((0, 7), (0, channels - share)))
     ring = lax.all_gather(jnp.concatenate([intersection[0], extra]), "x")
-    basis = lax.all_gather(ring[:, :share], CH_AXES)
+    basis = turn(lax.all_gather(ring[:, :share], CH_AXES))
     limits = jnp.pad(ring[:, share, :share].reshape(2, 2 * share), ((0, 14), (0, 0)))
 
     blocks = spread(x_index, start_amps, limits)
@@ -184,12 +206,11 @@
     wave = jnp.sqrt(energies[None, :, None] - limits.astype(jnp.float32))
     sine = jnp.sin(wave)
     coefs = jnp.stack([jnp.cos(wave), sine / wave, wave * sine], axis=1)
-    kept = jnp.zeros((5, 16, rows, lanes), jnp.bfloat16)
+    kept = None
     for step in range(planes):
         if step:
             state = lax.ppermute(state, "y", [(k, k + 1) for k in range(planes - 1)])
-        active = (y_index == step).astype(jnp.int32).reshape(1)
-        state, kept = stage(active, state, basis, coefs, kept)
+        state, kept = stage(step, y_index, state, basis, coefs, kept)
     back = lax.all_to_all(kept[:4].reshape(64, rows, lanes), PLANE, 0, 0)
     return finish(back.reshape(64, count, per, lanes))[None]
 

time: 301 us -> 263 us (0.87)
  local copies, waits for them, and re-layouts: 29.8 us -> 2.48 us
  Pallas kernels: 46.7 us -> 36.3 us
    unnamed x22 -> x6, local copies, waits for them, and re-layouts: 27.7 us -> 0.62 us
    pallas_call x8, Pallas kernels: 35.7 us -> 22.9 us  [stage(): pl.pallas_call(stage_kernel, grid_spec=pltpu.PrefetchScalarGridSpec(num_s...]
    pallas_call x1 -> x2, Pallas kernels: 4.87 us -> 7.28 us  [the longest x1 5.22 us: turn(): pl.pallas_call(turn_kernel, grid=(sectors,), in_specs=specs, out_specs=pl...]
where the time goes in v3:
time: 263 us; the launch traced here: 262 us
  waiting for transfers between devices  116 us (44%)
  blocking collectives  64.4 us (24%)
  Pallas kernels  36.3 us (14%)
  starting transfers between devices  28.4 us (11%)
  between operations  13.6 us (5%)
    ppermute x7, waiting for transfers between devices, per_device(): state = lax.ppermute(state, 'y', [(k, k + 1) for k in range(planes - 1)])  64 us
    all_to_all x1, blocking collectives, per_device(): back = lax.all_to_all(kept[:4].reshape(64, rows, lanes), PLANE, 0, 0)  54.3 us
    all_gather x1, waiting for transfers between devices, per_device(): basis = turn(lax.all_gather(ring[:, :share], CH_AXES))  32.4 us
    pallas_call x8, Pallas kernels, stage(): pl.pallas_call(stage_kernel, grid_spec=pltpu.PrefetchScalarGridSpec(num_s...  22.9 us
    all_to_all x1, waiting for transfers between devices, per_device(): lax.all_to_all(blocks.reshape(16, rows + per, lanes), CH_AXES, 0, 0)  19.2 us
    all_to_all x1, starting transfers between devices, per_device(): lax.all_to_all(blocks.reshape(16, rows + per, lanes), CH_AXES, 0, 0)  14.6 us
    ppermute x7, starting transfers between devices, per_device(): state = lax.ppermute(state, 'y', [(k, k + 1) for k in range(planes - 1)])  13.8 us
    all_gather x1, blocking collectives, per_device(): ring = lax.all_gather(jnp.concatenate([intersection[0], extra]), 'x')  10 us
  transfers between devices with their start and end apart: 9, of which 9 were waited for; matrix products, arithmetic and copies ran while one was open for 1% of the time, Pallas kernels for 2%

profile of v3, /device:TPU:39, one launch (start us, length us, event | category | flops | bytes accessed | tf_op | source)
XLA Modules:
  0.0 262.2 jit_solution(1227890505205223857)
XLA Ops:
  6.5 0.9 fusion.1
  7.5 10.0 %all-gather = bf16[288,1024]{1,0:T(8,128)(2,1)S(1)} all-gather(bf16[72,1024]{1,0:T(8,128)(2,1)S(1)} %fusion.1), channel_id=2, replica_groups=mesh['y'=8,'x'=4,'z'=8,'core'=2] {'x'}, dimensions={0}, use_global_device_ids=true | all-gather | bytes 737280 | tf_op jit(solution)/shard_map/all_gather | solution.py:196
  19.1 4.1 %spread.1 = bf16[16,7,16,128]{3,2,1,0:T(8,128)(2,1)} custom-call(s32[1]{0:T(128)} %bitcast.1.x_ref, bf16[6,64,2048]{2,1,0:T(8,128)(2,1)} %p_ref.1, bf16[6,64,2048]{2,1,0:T(8,128)(2,1)} %p_ref.1, bf16[16,128]{1,0:T(8,128)(2,1)} %pad.9.limit_ref), custom_call_target="tpu_custom_call" | custom-call | tf_op jit(solution)/shard_map/spread/pallas_call | solution.py:33
  23.2 14.6 %all-to-all-start = ((bf16[16,112,128]{2,1,0:T(8,128)(2,1)}), bf16[16,112,128]{2,1,0:T(8,128)(2,1)S(1)}, u32[]{:S(2)}, u32[]{:S(2)}) async-start(bf16[16,112,128]{2,1,0:T(8,128)(2,1)} %bitcast.18), calls=%async_computation | async-start | bytes 917504 | tf_op jit(solution)/shard_map/all_to_all | solution.py:203
  37.8 19.2 %all-to-all-done.in_ref = bf16[16,112,128]{2,1,0:T(8,128)(2,1)S(1)} async-done(((bf16[16,112,128]{2,1,0:T(8,128)(2,1)}), bf16[16,112,128]{2,1,0:T(8,128)(2,1)S(1)}, u32[]{:S(2)}, u32[]{:S(2)}) %all-to-all-start) | async-done | bytes 458784 | tf_op jit(solution)/shard_map/all_to_all | solution.py:203
  57.8 2.0 join.1.state_ref
  60.4 32.4 %all-gather.4.cloned.1.call-done = bf16[64,64,1024]{2,1,0:T(8,128)(2,1)} async-done(((bf16[4,64,1024]{2,1,0:T(8,128)(2,1)}), bf16[64,64,1024]{2,1,0:T(8,128)(2,1)}) %all-gather.4.cloned.1.call-update) | async-done | bytes 8388624 | tf_op jit(solution)/shard_map/all_gather | solution.py:197
  92.8 5.2 %turn.1.basis_ref = bf16[4,1024,1024]{2,1,0:T(8,128)(2,1)S(1)} custom-call(bf16[16,4,64,1024]{3,2,1,0:T(8,128)(2,1)} %bitcast.11, bf16[16,4,64,1024]{3,2,1,0:T(8,128)(2,1)} %bitcast.12, bf16[16,4,64,1024]{3,2,1,0:T(8,128)(2,1)} %bitcast.13, bf16[16,4,64,1024]{3,2,1,0:T(8,128)(2,1)} %bitcast.14), custom_call_target="tpu_custom_call" | custom-call | tf_op jit(solution)/shard_map/turn/pallas_call | solution.py:81
  98.1 2.8 %stage.8 = (bf16[2,96,1024]{2,1,0:T(8,128)(2,1)S(1)}, bf16[5,16,96,128]{3,2,1,0:T(8,128)(2,1)S(1)}) custom-call(s32[1]{0:T(128)} %bitcast.y_ref, bf16[2,96,1024]{2,1,0:T(8,128)(2,1)S(1)} %copy-done, bf16[4,1024,1024]{2,1,0:T(8,128)(2,1)S(1)} %turn.1.basis_ref, f32[4,3,6,1024]{3,2,1,0:T(8,128)S(1)} %pad_maximum_fusion.coef_ref), custom_call_target="tpu_custom_call" | custom-call | tf_op jit(solution)/shard_map/stage/pallas_call | solution.py:134
  100.9 2.3 collective-permute-start
  103.2 11.3 %collective-permute-done.state_ref = bf16[2,96,1024]{2,1,0:T(8,128)(2,1)S(1)} collective-permute-done((bf16[2,96,1024]{2,1,0:T(8,128)(2,1)S(1)}, bf16[2,96,1024]{2,1,0:T(8,128)(2,1)S(1)}, u32[]{:S(2)}, u32[]{:S(2)}) %collective-permute-start) | collective-permute-done | bytes 393248 | tf_op jit(solution)/shard_map/ppermute | solution.py:212
  114.4 2.8 %stage.9 = (bf16[2,96,1024]{2,1,0:T(8,128)(2,1)S(1)}, bf16[5,16,96,128]{3,2,1,0:T(8,128)(2,1)S(1)}) custom-call(s32[1]{0:T(128)} %bitcast.y_ref, bf16[2,96,1024]{2,1,0:T(8,128)(2,1)S(1)} %collective-permute-done.state_ref, bf16[4,1024,1024]{2,1,0:T(8,128)(2,1)S(1)} %turn.1.basis_ref, ...), custom_call_target="tpu_custom_call", output_to_operand_aliasing={{1}: (4, {})} | custom-call | tf_op jit(solution)/shard_map/stage/pallas_call | solution.py:134
  117.2 1.9 collective-permute-start.1
  119.2 10.7 %collective-permute-done.1.state_ref = bf16[2,96,1024]{2,1,0:T(8,128)(2,1)S(1)} collective-permute-done((bf16[2,96,1024]{2,1,0:T(8,128)(2,1)S(1)}, bf16[2,96,1024]{2,1,0:T(8,128)(2,1)S(1)}, u32[]{:S(2)}, u32[]{:S(2)}) %collective-permute-start.1) | collective-permute-done | bytes 393248 | tf_op jit(solution)/shard_map/ppermute | solution.py:212
  129.9 2.7 %stage.10 = (bf16[2,96,1024]{2,1,0:T(8,128)(2,1)S(1)}, bf16[5,16,96,128]{3,2,1,0:T(8,128)(2,1)S(1)}) custom-call(s32[1]{0:T(128)} %bitcast.y_ref, bf16[2,96,1024]{2,1,0:T(8,128)(2,1)S(1)} %collective-permute-done.1.state_ref, bf16[4,1024,1024]{2,1,0:T(8,128)(2,1)S(1)} %turn.1.basis_ref, ...), custom_call_target="tpu_custom_call", output_to_operand_aliasing={{1}: (4, {})} | custom-call | tf_op jit(solution)/shard_map/stage/pallas_call | solution.py:134
  132.6 1.9 collective-permute-start.2
  134.6 9.8 %collective-permute-done.2.state_ref = bf16[2,96,1024]{2,1,0:T(8,128)(2,1)S(1)} collective-permute-done((bf16[2,96,1024]{2,1,0:T(8,128)(2,1)S(1)}, bf16[2,96,1024]{2,1,0:T(8,128)(2,1)S(1)}, u32[]{:S(2)}, u32[]{:S(2)}) %collective-permute-start.2) | collective-permute-done | bytes 393248 | tf_op jit(solution)/shard_map/ppermute | solution.py:212
  144.3 2.8 %stage.11 = (bf16[2,96,1024]{2,1,0:T(8,128)(2,1)S(1)}, bf16[5,16,96,128]{3,2,1,0:T(8,128)(2,1)S(1)}) custom-call(s32[1]{0:T(128)} %bitcast.y_ref, bf16[2,96,1024]{2,1,0:T(8,128)(2,1)S(1)} %collective-permute-done.2.state_ref, bf16[4,1024,1024]{2,1,0:T(8,128)(2,1)S(1)} %turn.1.basis_ref, ...), custom_call_target="tpu_custom_call", output_to_operand_aliasing={{1}: (4, {})} | custom-call | tf_op jit(solution)/shard_map/stage/pallas_call | solution.py:134
  147.1 1.9 collective-permute-start.3
  149.0 8.8 %collective-permute-done.3.state_ref = bf16[2,96,1024]{2,1,0:T(8,128)(2,1)S(1)} collective-permute-done((bf16[2,96,1024]{2,1,0:T(8,128)(2,1)S(1)}, bf16[2,96,1024]{2,1,0:T(8,128)(2,1)S(1)}, u32[]{:S(2)}, u32[]{:S(2)}) %collective-permute-start.3) | collective-permute-done | bytes 393248 | tf_op jit(solution)/shard_map/ppermute | solution.py:212
  157.9 2.8 %stage.12 = (bf16[2,96,1024]{2,1,0:T(8,128)(2,1)S(1)}, bf16[5,16,96,128]{3,2,1,0:T(8,128)(2,1)S(1)}) custom-call(s32[1]{0:T(128)} %bitcast.y_ref, bf16[2,96,1024]{2,1,0:T(8,128)(2,1)S(1)} %collective-permute-done.3.state_ref, bf16[4,1024,1024]{2,1,0:T(8,128)(2,1)S(1)} %turn.1.basis_ref, ...), custom_call_target="tpu_custom_call", output_to_operand_aliasing={{1}: (4, {})} | custom-call | tf_op jit(solution)/shard_map/stage/pallas_call | solution.py:134
  160.6 1.9 collective-permute-start.4
  162.5 7.8 %collective-permute-done.4.state_ref = bf16[2,96,1024]{2,1,0:T(8,128)(2,1)S(1)} collective-permute-done((bf16[2,96,1024]{2,1,0:T(8,128)(2,1)S(1)}, bf16[2,96,1024]{2,1,0:T(8,128)(2,1)S(1)}, u32[]{:S(2)}, u32[]{:S(2)}) %collective-permute-start.4) | collective-permute-done | bytes 393248 | tf_op jit(solution)/shard_map/ppermute | solution.py:212
  170.3 2.7 %stage.13 = (bf16[2,96,1024]{2,1,0:T(8,128)(2,1)S(1)}, bf16[5,16,96,128]{3,2,1,0:T(8,128)(2,1)S(1)}) custom-call(s32[1]{0:T(128)} %bitcast.y_ref, bf16[2,96,1024]{2,1,0:T(8,128)(2,1)S(1)} %collective-permute-done.4.state_ref, bf16[4,1024,1024]{2,1,0:T(8,128)(2,1)S(1)} %turn.1.basis_ref, ...), custom_call_target="tpu_custom_call", output_to_operand_aliasing={{1}: (4, {})} | custom-call | tf_op jit(solution)/shard_map/stage/pallas_call | solution.py:134
  173.1 1.9 collective-permute-start.5
  175.0 7.8 %collective-permute-done.5.state_ref = bf16[2,96,1024]{2,1,0:T(8,128)(2,1)S(1)} collective-permute-done((bf16[2,96,1024]{2,1,0:T(8,128)(2,1)S(1)}, bf16[2,96,1024]{2,1,0:T(8,128)(2,1)S(1)}, u32[]{:S(2)}, u32[]{:S(2)}) %collective-permute-start.5) | collective-permute-done | bytes 393248 | tf_op jit(solution)/shard_map/ppermute | solution.py:212
  182.8 2.8 %stage.14 = (bf16[2,96,1024]{2,1,0:T(8,128)(2,1)S(1)}, bf16[5,16,96,128]{3,2,1,0:T(8,128)(2,1)S(1)}) custom-call(s32[1]{0:T(128)} %bitcast.y_ref, bf16[2,96,1024]{2,1,0:T(8,128)(2,1)S(1)} %collective-permute-done.5.state_ref, bf16[4,1024,1024]{2,1,0:T(8,128)(2,1)S(1)} %turn.1.basis_ref, ...), custom_call_target="tpu_custom_call", output_to_operand_aliasing={{1}: (4, {})} | custom-call | tf_op jit(solution)/shard_map/stage/pallas_call | solution.py:134
  185.6 1.9 collective-permute-start.6
  187.5 7.8 %collective-permute-done.6.state_ref = bf16[2,96,1024]{2,1,0:T(8,128)(2,1)S(1)} collective-permute-done((bf16[2,96,1024]{2,1,0:T(8,128)(2,1)S(1)}, bf16[2,96,1024]{2,1,0:T(8,128)(2,1)S(1)}, u32[]{:S(2)}, u32[]{:S(2)}) %collective-permute-start.6) | collective-permute-done | bytes 393248 | tf_op jit(solution)/shard_map/ppermute | solution.py:212
  195.3 3.5 %stage.15 = (bf16[2,96,1024]{2,1,0:T(8,128)(2,1)}, bf16[5,16,96,128]{3,2,1,0:T(8,128)(2,1)S(1)}) custom-call(s32[1]{0:T(128)} %bitcast.y_ref, bf16[2,96,1024]{2,1,0:T(8,128)(2,1)S(1)} %collective-permute-done.6.state_ref, bf16[4,1024,1024]{2,1,0:T(8,128)(2,1)S(1)} %turn.1.basis_ref, ...), custom_call_target="tpu_custom_call", output_to_operand_aliasing={{1}: (4, {})} | custom-call | tf_op jit(solution)/shard_map/stage/pallas_call | solution.py:134
  199.0 54.3 %all_to_all.10 = bf16[64,96,128]{2,1,0:T(8,128)(2,1)S(1)} all-to-all(bf16[64,96,128]{2,1,0:T(8,128)(2,1)S(1)} %bitcast.15), channel_id=1, replica_groups=mesh['y'=8,'x'=4,'z'=8,'core'=2] {'x','z','core'}, dimensions={0} | all-to-all | bytes 3145728 | tf_op jit(solution)/shard_map/all_to_all | solution.py:214
  253.3 2.1 finish.1
  (19 shorter events, 3.1 us)
Async XLA Ops:
  6.5 86.3 %all-gather.4.cloned.1.call-start = ((), (), s32[]{:S(2)}) async-start(), calls=%async_computation.2 | async-start | bytes 8912896 | tf_op jit(solution)/shard_map/all_gather | solution.py:197
  19.1 40.7 %copy-start.2 = (f32[6]{0:T(128)S(1)}, f32[6]{0:T(128)}, u32[]{:S(2)}) copy-start(f32[6]{0:T(128)} %param.5) | copy-start | bytes 76
  23.2 33.7 %all-to-all-start = ((bf16[16,112,128]{2,1,0:T(8,128)(2,1)}), bf16[16,112,128]{2,1,0:T(8,128)(2,1)S(1)}, u32[]{:S(2)}, u32[]{:S(2)}) async-start(bf16[16,112,128]{2,1,0:T(8,128)(2,1)} %bitcast.18), calls=%async_computation | async-start | bytes 917504 | tf_op jit(solution)/shard_map/all_to_all | solution.py:203
  57.0 0.8 copy-start.1
  92.8 5.2 %copy-start = (bf16[2,96,1024]{2,1,0:T(8,128)(2,1)S(1)}, bf16[2,96,1024]{2,1,0:T(8,128)(2,1)}, u32[]{:S(2)}) copy-start(bf16[2,96,1024]{2,1,0:T(8,128)(2,1)} %join.1.state_ref) | copy-start | bytes 1179652
  100.9 13.6 %collective-permute-start = (bf16[2,96,1024]{2,1,0:T(8,128)(2,1)S(1)}, bf16[2,96,1024]{2,1,0:T(8,128)(2,1)S(1)}, u32[]{:S(2)}, u32[]{:S(2)}) collective-permute-start(bf16[2,96,1024]{2,1,0:T(8,128)(2,1)S(1)} %get-tuple-element.20), channel_id=1, source_target_pairs={{0,64},{64,128},{128,192},{192,256},{256,320},{320,384},{384,448},... | collective-permute-start | bytes 1179656 | tf_op jit(solution)/shard_map/ppermute | solution.py:212
  117.2 12.6 %collective-permute-start.1 = (bf16[2,96,1024]{2,1,0:T(8,128)(2,1)S(1)}, bf16[2,96,1024]{2,1,0:T(8,128)(2,1)S(1)}, u32[]{:S(2)}, u32[]{:S(2)}) collective-permute-start(bf16[2,96,1024]{2,1,0:T(8,128)(2,1)S(1)} %get-tuple-element.22), channel_id=1, source_target_pairs={{0,64},{64,128},{128,192},{192,256},{256,320},{320,384},{384,448},... | collective-permute-start | bytes 1179656 | tf_op jit(solution)/shard_map/ppermute | solution.py:212
  132.6 11.7 %collective-permute-start.2 = (bf16[2,96,1024]{2,1,0:T(8,128)(2,1)S(1)}, bf16[2,96,1024]{2,1,0:T(8,128)(2,1)S(1)}, u32[]{:S(2)}, u32[]{:S(2)}) collective-permute-start(bf16[2,96,1024]{2,1,0:T(8,128)(2,1)S(1)} %get-tuple-element.24), channel_id=1, source_target_pairs={{0,64},{64,128},{128,192},{192,256},{256,320},{320,384},{384,448},... | collective-permute-start | bytes 1179656 | tf_op jit(solution)/shard_map/ppermute | solution.py:212
  147.1 10.8 %collective-permute-start.3 = (bf16[2,96,1024]{2,1,0:T(8,128)(2,1)S(1)}, bf16[2,96,1024]{2,1,0:T(8,128)(2,1)S(1)}, u32[]{:S(2)}, u32[]{:S(2)}) collective-permute-start(bf16[2,96,1024]{2,1,0:T(8,128)(2,1)S(1)} %get-tuple-element.26), channel_id=1, source_target_pairs={{0,64},{64,128},{128,192},{192,256},{256,320},{320,384},{384,448},... | collective-permute-start | bytes 1179656 | tf_op jit(solution)/shard_map/ppermute | solution.py:212
  160.6 9.7 %collective-permute-start.4 = (bf16[2,96,1024]{2,1,0:T(8,128)(2,1)S(1)}, bf16[2,96,1024]{2,1,0:T(8,128)(2,1)S(1)}, u32[]{:S(2)}, u32[]{:S(2)}) collective-permute-start(bf16[2,96,1024]{2,1,0:T(8,128)(2,1)S(1)} %get-tuple-element.28), channel_id=1, source_target_pairs={{0,64},{64,128},{128,192},{192,256},{256,320},{320,384},{384,448},... | collective-permute-start | bytes 1179656 | tf_op jit(solution)/shard_map/ppermute | solution.py:212
  173.1 9.7 %collective-permute-start.5 = (bf16[2,96,1024]{2,1,0:T(8,128)(2,1)S(1)}, bf16[2,96,1024]{2,1,0:T(8,128)(2,1)S(1)}, u32[]{:S(2)}, u32[]{:S(2)}) collective-permute-start(bf16[2,96,1024]{2,1,0:T(8,128)(2,1)S(1)} %get-tuple-element.30), channel_id=1, source_target_pairs={{0,64},{64,128},{128,192},{192,256},{256,320},{320,384},{384,448},... | collective-permute-start | bytes 1179656 | tf_op jit(solution)/shard_map/ppermute | solution.py:212
  185.6 9.7 %collective-permute-start.6 = (bf16[2,96,1024]{2,1,0:T(8,128)(2,1)S(1)}, bf16[2,96,1024]{2,1,0:T(8,128)(2,1)S(1)}, u32[]{:S(2)}, u32[]{:S(2)}) collective-permute-start(bf16[2,96,1024]{2,1,0:T(8,128)(2,1)S(1)} %get-tuple-element.32), channel_id=1, source_target_pairs={{0,64},{64,128},{128,192},{192,256},{256,320},{320,384},{384,448},... | collective-permute-start | bytes 1179656 | tf_op jit(solution)/shard_map/ppermute | solution.py:212
Sparse Core Ops, SparseCore 0:
  18.5 74.2 all-gather.3

commit v4 on v3

--- a/solution.py
+++ b/solution.py
@@ -1,3 +1,5 @@
+import functools
+
 import jax
 import jax.numpy as jnp
 from jax import lax
@@ -89,12 +91,13 @@
     )(basis, basis, basis, basis)
 
 
-def stage_kernel(y_ref, state_ref, basis_ref, coef_ref, *refs):
+def stage_kernel(parts, y_ref, state_ref, *refs):
+    basis_refs, coef_ref = refs[:parts], refs[parts]
     next_ref, out_ref, now, rot = refs[-4:]
     del y_ref
     s = pl.program_id(0)
     energies = coef_ref.shape[2]
-    rows = state_ref.shape[1]
+    rows, channels = state_ref.shape[1:]
     per = rows // energies
 
     @pl.when(s == 0)
@@ -110,37 +113,50 @@
         slopes = now[pl.ds(rows + per * e, per), :].astype(jnp.float32)
         rot[pl.ds(per * e, per), :] = (cosine * values + ratio * slopes).astype(rot.dtype)
         rot[pl.ds(rows + per * e, per), :] = (cosine * slopes - product * values).astype(rot.dtype)
-    fresh = jnp.dot(rot[...], basis_ref[0], preferred_element_type=jnp.float32)
-    rounded = fresh.astype(now.dtype)
-    now[...] = rounded
     low = lax.broadcasted_iota(jnp.int32, (rows, 128), 1) < 64
-    for z in range(8):
-        lanes = slice(128 * z, 128 * z + 128)
-        values = fresh[:rows, lanes]
-        slopes = fresh[rows:, lanes]
-        out_ref[0, 2 * z] = jnp.where(low, values, pltpu.roll(slopes, 64, 1)).astype(out_ref.dtype)
-        out_ref[0, 2 * z + 1] = jnp.where(low, pltpu.roll(values, 64, 1), slopes).astype(out_ref.dtype)
+    width = channels // parts
+    for q, basis_ref in enumerate(basis_refs):
+        if parts == 1:
+            fresh = jnp.dot(rot[...], basis_ref[0], preferred_element_type=jnp.float32)
+        else:
+            block = basis_ref[...].reshape(width, channels)
+            fresh = lax.dot_general(
+                rot[...], block, (((1,), (1,)), ((), ())), preferred_element_type=jnp.float32
+            )
+        now[:, pl.ds(width * q, width)] = fresh.astype(now.dtype)
+        for k in range(width // 128):
+            z = width // 128 * q + k
+            lanes = slice(128 * k, 128 * k + 128)
+            values = fresh[:rows, lanes]
+            slopes = fresh[rows:, lanes]
+            out_ref[0, 2 * z] = jnp.where(low, values, pltpu.roll(slopes, 64, 1)).astype(out_ref.dtype)
+            out_ref[0, 2 * z + 1] = jnp.where(low, pltpu.roll(values, 64, 1), slopes).astype(out_ref.dtype)
 
     @pl.when(s == pl.num_programs(0) - 1)
     def _():
-        next_ref[0] = rounded[:rows]
-        next_ref[1] = rounded[rows:]
+        next_ref[0] = now[pl.ds(0, rows)]
+        next_ref[1] = now[pl.ds(rows, rows)]
 
 
 def stage(step, y_index, state, basis, coefs, kept):
-    sectors, channels, _ = basis.shape
-    rows = state.shape[1]
+    sectors = coefs.shape[0]
+    _, rows, channels = state.shape
     first = kept is None
-    return pl.pallas_call(
-        stage_kernel,
+    parts = 4 if first else 1
+    if first:
+        groups, _, share, _ = basis.shape
+        block = (groups // parts, 1, share, channels)
+        basis_specs = [pl.BlockSpec(block, lambda s, y, q=q: (q, s, 0, 0)) for q in range(parts)]
+    else:
+        basis_specs = [pl.BlockSpec((1, channels, channels), lambda s, y: (s, 0, 0))]
+    return pl.pallas_call(
+        functools.partial(stage_kernel, parts),
         grid_spec=pltpu.PrefetchScalarGridSpec(
             num_scalar_prefetch=1,
             grid=(sectors,),
-            in_specs=[
-                pl.BlockSpec(state.shape, lambda s, y: (0, 0, 0)),
-                pl.BlockSpec((1, channels, channels), lambda s, y: (s, 0, 0)),
-                pl.BlockSpec((1,) + coefs.shape[1:], lambda s, y: (s, 0, 0, 0)),
-            ]
+            in_specs=[pl.BlockSpec(state.shape, lambda s, y: (0, 0, 0))]
+            + basis_specs
+            + [pl.BlockSpec((1,) + coefs.shape[1:], lambda s, y: (s, 0, 0, 0))]
             + ([] if first else [pl.BlockSpec(memory_space=pl.ANY)]),
             out_specs=[
                 pl.BlockSpec(state.shape, lambda s, y: (0, 0, 0)),
@@ -156,9 +172,9 @@
             jax.ShapeDtypeStruct((sectors + 1, 16, rows, 128), state.dtype),
         ],
         input_output_aliases={} if first else {4: 1},
-        compiler_params=pltpu.CompilerParams(vmem_limit_bytes=16 * MIB),
+        compiler_params=pltpu.CompilerParams(vmem_limit_bytes=(48 if first else 16) * MIB),
         name="stage",
-    )(y_index, state, basis, coefs, *([] if first else [kept]))
+    )(y_index, state, *[basis] * parts, coefs, *([] if first else [kept]))
 
 
 def finish_kernel(in_ref, out_ref):
@@ -194,7 +210,7 @@
     share = intersection.shape[1]
     extra = jnp.pad(thresholds, ((0, 7), (0, channels - share)))
     ring = lax.all_gather(jnp.concatenate([intersection[0], extra]), "x")
-    basis = turn(lax.all_gather(ring[:, :share], CH_AXES))
+    basis = lax.all_gather(ring[:, :share], CH_AXES)
     limits = jnp.pad(ring[:, share, :share].reshape(2, 2 * share), ((0, 14), (0, 0)))
 
     blocks = spread(x_index, start_amps, limits)
@@ -209,7 +225,9 @@
     kept = None
     for step in range(planes):
         if step:
-            state = lax.ppermute(state, "y", [(k, k + 1) for k in range(planes - 1)])
+            state = lax.ppermute(state, "y", [(step - 1, step)])
+        if step == 1:
+            basis = turn(basis)
         state, kept = stage(step, y_index, state, basis, coefs, kept)
     back = lax.all_to_all(kept[:4].reshape(64, rows, lanes), PLANE, 0, 0)
     return finish(back.reshape(64, count, per, lanes))[None]

time: 263 us -> 247 us (0.939)
  the two profiles are of different devices: /device:TPU:39 before, /device:TPU:63 now
where the time goes in v4:
time: 247 us; the launch traced here: 246 us
  waiting for transfers between devices  105 us (43%)
  blocking collectives  62.6 us (25%)
  Pallas kernels  39.6 us (16%)
  starting transfers between devices  20 us (8%)
  between operations  13.6 us (6%)
  local copies, waits for them, and re-layouts  3.46 us (1%)
    ppermute x7, waiting for transfers between devices, per_device(): state = lax.ppermute(state, 'y', [(step - 1, step)])  53.4 us
    all_to_all x1, blocking collectives, per_device(): back = lax.all_to_all(kept[:4].reshape(64, rows, lanes), PLANE, 0, 0)  52.6 us
    all_gather x1, waiting for transfers between devices, per_device(): basis = lax.all_gather(ring[:, :share], CH_AXES)  32.2 us
    pallas_call x8, Pallas kernels, stage(): pl.pallas_call(functools.partial(stage_kernel, parts), grid_spec=pltpu.Pr...  26.2 us
    all_to_all x1, waiting for transfers between devices, per_device(): lax.all_to_all(blocks.reshape(16, rows + per, lanes), CH_AXES, 0, 0)  19.5 us
    all_to_all x1, starting transfers between devices, per_device(): lax.all_to_all(blocks.reshape(16, rows + per, lanes), CH_AXES, 0, 0)  14.6 us
    all_gather x1, blocking collectives, per_device(): ring = lax.all_gather(jnp.concatenate([intersection[0], extra]), 'x')  10 us
    ppermute x7, starting transfers between devices, per_device(): state = lax.ppermute(state, 'y', [(step - 1, step)])  5.41 us
  transfers between devices with their start and end apart: 9, of which 3 were waited for; matrix products, arithmetic and copies ran while one was open for 1% of the time, Pallas kernels for 5%

profile of v4, /device:TPU:63, one launch (start us, length us, event | category | flops | bytes accessed | tf_op | source)
XLA Modules:
  0.0 245.9 jit_solution(7786857761409226486)
XLA Ops:
  6.5 0.9 fusion.1
  7.5 10.0 %all-gather = bf16[288,1024]{1,0:T(8,128)(2,1)S(1)} all-gather(bf16[72,1024]{1,0:T(8,128)(2,1)S(1)} %fusion.1), channel_id=2, replica_groups=mesh['y'=8,'x'=4,'z'=8,'core'=2] {'x'}, dimensions={0}, use_global_device_ids=true | all-gather | bytes 737280 | tf_op jit(solution)/shard_map/all_gather | solution.py:212
  17.5 0.8 slice.17
  18.5 0.6 pad.9.limit_ref
  19.1 4.1 %spread.1 = bf16[16,7,16,128]{3,2,1,0:T(8,128)(2,1)} custom-call(s32[1]{0:T(128)} %bitcast.1.x_ref, bf16[6,64,2048]{2,1,0:T(8,128)(2,1)} %p_ref.1, bf16[6,64,2048]{2,1,0:T(8,128)(2,1)} %p_ref.1, bf16[16,128]{1,0:T(8,128)(2,1)} %pad.9.limit_ref), custom_call_target="tpu_custom_call" | custom-call | tf_op jit(solution)/shard_map/spread/pallas_call | solution.py:35
  23.2 14.6 %all-to-all-start = ((bf16[16,112,128]{2,1,0:T(8,128)(2,1)}), bf16[16,112,128]{2,1,0:T(8,128)(2,1)S(1)}, u32[]{:S(2)}, u32[]{:S(2)}) async-start(bf16[16,112,128]{2,1,0:T(8,128)(2,1)} %bitcast.22), calls=%async_computation | async-start | bytes 917504 | tf_op jit(solution)/shard_map/all_to_all | solution.py:219
  37.8 19.5 %all-to-all-done.in_ref = bf16[16,112,128]{2,1,0:T(8,128)(2,1)S(1)} async-done(((bf16[16,112,128]{2,1,0:T(8,128)(2,1)}), bf16[16,112,128]{2,1,0:T(8,128)(2,1)S(1)}, u32[]{:S(2)}, u32[]{:S(2)}) %all-to-all-start) | async-done | bytes 458784 | tf_op jit(solution)/shard_map/all_to_all | solution.py:219
  57.4 0.6 copy-done.1
  58.0 2.0 join.1.state_ref
  60.0 0.6 fusion.5
  60.7 32.2 %all-gather.4.cloned.1.call-done = bf16[64,64,1024]{2,1,0:T(8,128)(2,1)} async-done(((bf16[4,64,1024]{2,1,0:T(8,128)(2,1)}), bf16[64,64,1024]{2,1,0:T(8,128)(2,1)}) %all-gather.4.cloned.1.call-update) | async-done | bytes 8388624 | tf_op jit(solution)/shard_map/all_gather | solution.py:213
  92.8 1.0 copy-done
  93.8 6.1 %stage.8 = (bf16[2,96,1024]{2,1,0:T(8,128)(2,1)S(1)}, bf16[5,16,96,128]{3,2,1,0:T(8,128)(2,1)S(1)}) custom-call(s32[1]{0:T(128)} %bitcast.y_ref, bf16[2,96,1024]{2,1,0:T(8,128)(2,1)S(1)} %copy-done, bf16[16,4,64,1024]{3,2,1,0:T(8,128)(2,1)} %bitcast.11, bf16[16,4,64,1024]{3,2,1,0:T(8,128)(2,1)} %bitcast.12, bf16[16,4,64,1024]{3,2,1,0:T(8,128)(2,1)} %bitcast.13, ...), custom_call_target="tpu_custom_call" | custom-call | tf_op jit(solution)/shard_map/stage/pallas_call | solution.py:152
  99.9 0.7 collective-permute-start
  100.6 5.2 %turn.1.refs_0_ = bf16[4,1024,1024]{2,1,0:T(8,128)(2,1)S(1)} custom-call(bf16[16,4,64,1024]{3,2,1,0:T(8,128)(2,1)} %bitcast.15, bf16[16,4,64,1024]{3,2,1,0:T(8,128)(2,1)} %bitcast.16, bf16[16,4,64,1024]{3,2,1,0:T(8,128)(2,1)} %bitcast.17, bf16[16,4,64,1024]{3,2,1,0:T(8,128)(2,1)} %bitcast.18), custom_call_target="tpu_custom_call" | custom-call | tf_op jit(solution)/shard_map/turn/pallas_call | solution.py:83
  105.8 2.8 %stage.9 = (bf16[2,96,1024]{2,1,0:T(8,128)(2,1)S(1)}, bf16[5,16,96,128]{3,2,1,0:T(8,128)(2,1)S(1)}) custom-call(s32[1]{0:T(128)} %bitcast.y_ref, bf16[2,96,1024]{2,1,0:T(8,128)(2,1)S(1)} %collective-permute-done.state_ref, bf16[4,1024,1024]{2,1,0:T(8,128)(2,1)S(1)} %turn.1.refs_0_, ...), custom_call_target="tpu_custom_call", output_to_operand_aliasing={{1}: (4, {})} | custom-call | tf_op jit(solution)/shard_map/stage/pallas_call | solution.py:152
  108.6 0.7 collective-permute-start.1
  109.3 2.8 %stage.10 = (bf16[2,96,1024]{2,1,0:T(8,128)(2,1)S(1)}, bf16[5,16,96,128]{3,2,1,0:T(8,128)(2,1)S(1)}) custom-call(s32[1]{0:T(128)} %bitcast.y_ref, bf16[2,96,1024]{2,1,0:T(8,128)(2,1)S(1)} %collective-permute-done.1.state_ref, bf16[4,1024,1024]{2,1,0:T(8,128)(2,1)S(1)} %turn.1.refs_0_, ...), custom_call_target="tpu_custom_call", output_to_operand_aliasing={{1}: (4, {})} | custom-call | tf_op jit(solution)/shard_map/stage/pallas_call | solution.py:152
  112.1 0.7 collective-permute-start.2
  112.8 2.8 %stage.11 = (bf16[2,96,1024]{2,1,0:T(8,128)(2,1)S(1)}, bf16[5,16,96,128]{3,2,1,0:T(8,128)(2,1)S(1)}) custom-call(s32[1]{0:T(128)} %bitcast.y_ref, bf16[2,96,1024]{2,1,0:T(8,128)(2,1)S(1)} %collective-permute-done.2.state_ref, bf16[4,1024,1024]{2,1,0:T(8,128)(2,1)S(1)} %turn.1.refs_0_, ...), custom_call_target="tpu_custom_call", output_to_operand_aliasing={{1}: (4, {})} | custom-call | tf_op jit(solution)/shard_map/stage/pallas_call | solution.py:152
  115.6 0.7 collective-permute-start.3
  116.3 2.8 %stage.12 = (bf16[2,96,1024]{2,1,0:T(8,128)(2,1)S(1)}, bf16[5,16,96,128]{3,2,1,0:T(8,128)(2,1)S(1)}) custom-call(s32[1]{0:T(128)} %bitcast.y_ref, bf16[2,96,1024]{2,1,0:T(8,128)(2,1)S(1)} %collective-permute-done.3.state_ref, bf16[4,1024,1024]{2,1,0:T(8,128)(2,1)S(1)} %turn.1.refs_0_, ...), custom_call_target="tpu_custom_call", output_to_operand_aliasing={{1}: (4, {})} | custom-call | tf_op jit(solution)/shard_map/stage/pallas_call | solution.py:152
  119.0 0.7 collective-permute-start.4
  119.7 2.8 %stage.13 = (bf16[2,96,1024]{2,1,0:T(8,128)(2,1)S(1)}, bf16[5,16,96,128]{3,2,1,0:T(8,128)(2,1)S(1)}) custom-call(s32[1]{0:T(128)} %bitcast.y_ref, bf16[2,96,1024]{2,1,0:T(8,128)(2,1)S(1)} %collective-permute-done.4.state_ref, bf16[4,1024,1024]{2,1,0:T(8,128)(2,1)S(1)} %turn.1.refs_0_, ...), custom_call_target="tpu_custom_call", output_to_operand_aliasing={{1}: (4, {})} | custom-call | tf_op jit(solution)/shard_map/stage/pallas_call | solution.py:152
  122.5 0.7 collective-permute-start.5
  123.2 2.8 %stage.14 = (bf16[2,96,1024]{2,1,0:T(8,128)(2,1)S(1)}, bf16[5,16,96,128]{3,2,1,0:T(8,128)(2,1)S(1)}) custom-call(s32[1]{0:T(128)} %bitcast.y_ref, bf16[2,96,1024]{2,1,0:T(8,128)(2,1)S(1)} %collective-permute-done.5.state_ref, bf16[4,1024,1024]{2,1,0:T(8,128)(2,1)S(1)} %turn.1.refs_0_, ...), custom_call_target="tpu_custom_call", output_to_operand_aliasing={{1}: (4, {})} | custom-call | tf_op jit(solution)/shard_map/stage/pallas_call | solution.py:152
  126.0 1.3 collective-permute-start.6
  127.3 53.4 %collective-permute-done.6.state_ref = bf16[2,96,1024]{2,1,0:T(8,128)(2,1)S(1)} collective-permute-done((bf16[2,96,1024]{2,1,0:T(8,128)(2,1)S(1)}, bf16[2,96,1024]{2,1,0:T(8,128)(2,1)S(1)}, u32[]{:S(2)}, u32[]{:S(2)}) %collective-permute-start.6) | collective-permute-done | bytes 393248 | tf_op jit(solution)/shard_map/ppermute | solution.py:228
  180.8 3.5 %stage.15 = (bf16[2,96,1024]{2,1,0:T(8,128)(2,1)}, bf16[5,16,96,128]{3,2,1,0:T(8,128)(2,1)S(1)}) custom-call(s32[1]{0:T(128)} %bitcast.y_ref, bf16[2,96,1024]{2,1,0:T(8,128)(2,1)S(1)} %collective-permute-done.6.state_ref, bf16[4,1024,1024]{2,1,0:T(8,128)(2,1)S(1)} %turn.1.refs_0_, ...), custom_call_target="tpu_custom_call", output_to_operand_aliasing={{1}: (4, {})} | custom-call | tf_op jit(solution)/shard_map/stage/pallas_call | solution.py:152
  184.3 0.1 slice.15
  184.4 52.6 %all_to_all.10 = bf16[64,96,128]{2,1,0:T(8,128)(2,1)S(1)} all-to-all(bf16[64,96,128]{2,1,0:T(8,128)(2,1)S(1)} %bitcast.19), channel_id=1, replica_groups=mesh['y'=8,'x'=4,'z'=8,'core'=2] {'x','z','core'}, dimensions={0} | all-to-all | bytes 3145728 | tf_op jit(solution)/shard_map/all_to_all | solution.py:232
  237.0 2.1 finish.1
  (19 shorter events, 0.4 us)
Async XLA Ops:
  6.5 86.3 %all-gather.4.cloned.1.call-start = ((), (), s32[]{:S(2)}) async-start(), calls=%async_computation.2 | async-start | bytes 8912896 | tf_op jit(solution)/shard_map/all_gather | solution.py:213
  19.1 41.0 %copy-start.2 = (f32[6]{0:T(128)S(1)}, f32[6]{0:T(128)}, u32[]{:S(2)}) copy-start(f32[6]{0:T(128)} %param.5) | copy-start | bytes 76
  23.2 34.0 %all-to-all-start = ((bf16[16,112,128]{2,1,0:T(8,128)(2,1)}), bf16[16,112,128]{2,1,0:T(8,128)(2,1)S(1)}, u32[]{:S(2)}, u32[]{:S(2)}) async-start(bf16[16,112,128]{2,1,0:T(8,128)(2,1)} %bitcast.22), calls=%async_computation | async-start | bytes 917504 | tf_op jit(solution)/shard_map/all_to_all | solution.py:219
  57.2 0.8 copy-start.1
  92.8 1.0 copy-start
  99.9 5.9 %collective-permute-start = (bf16[2,96,1024]{2,1,0:T(8,128)(2,1)S(1)}, bf16[2,96,1024]{2,1,0:T(8,128)(2,1)S(1)}, u32[]{:S(2)}, u32[]{:S(2)}) collective-permute-start(bf16[2,96,1024]{2,1,0:T(8,128)(2,1)S(1)} %get-tuple-element.20), channel_id=1, source_target_pairs={{0,64},{1,65},{2,66},{3,67},{4,68},{5,69},{6,70},{7,71},{8,72},{9,... | collective-permute-start | bytes 1179656 | tf_op jit(solution)/shard_map/ppermute | solution.py:228
  108.6 0.7 collective-permute-start.1
  112.1 0.7 collective-permute-start.2
  115.6 0.7 collective-permute-start.3
  119.0 0.7 collective-permute-start.4
  122.5 0.7 collective-permute-start.5
  126.0 54.7 %collective-permute-start.6 = (bf16[2,96,1024]{2,1,0:T(8,128)(2,1)S(1)}, bf16[2,96,1024]{2,1,0:T(8,128)(2,1)S(1)}, u32[]{:S(2)}, u32[]{:S(2)}) collective-permute-start(bf16[2,96,1024]{2,1,0:T(8,128)(2,1)S(1)} %get-tuple-element.32), channel_id=1, source_target_pairs={{384,448},{385,449},{386,450},{387,451},{388,452},{389,453},{390,4... | collective-permute-start | bytes 1179656 | tf_op jit(solution)/shard_map/ppermute | solution.py:228
Sparse Core Ops, SparseCore 0:
  18.5 74.3 all-gather.3

commit v5 on v4

--- a/solution.py
+++ b/solution.py
@@ -13,6 +13,7 @@
 CH_AXES = ("z", "core")
 PLANE = ("x", "z", "core")
 MIB = 1024 * 1024
+PARTS = 2
 
 
 def spread_kernel(x_ref, v_ref, p_ref, limit_ref, out_ref):
@@ -91,32 +92,34 @@
     )(basis, basis, basis, basis)
 
 
-def stage_kernel(parts, y_ref, state_ref, *refs):
-    basis_refs, coef_ref = refs[:parts], refs[parts]
-    next_ref, out_ref, now, rot = refs[-4:]
+def stage_kernel(pieces, parts, y_ref, state_ref, *refs):
+    basis_refs, coef_ref = refs[:pieces], refs[pieces]
+    next_refs, (out_ref, now, rot) = refs[-3 - parts : -3], refs[-3:]
     del y_ref
     s = pl.program_id(0)
-    energies = coef_ref.shape[2]
+    energies = coef_ref.shape[3]
     rows, channels = state_ref.shape[1:]
-    per = rows // energies
+    own = rows // parts
+    per = own // energies
 
     @pl.when(s == 0)
     def _():
         now[pl.ds(0, rows)] = state_ref[0]
         now[pl.ds(rows, rows)] = state_ref[1]
 
-    for e in range(energies):
-        cosine = coef_ref[0, 0, pl.ds(e, 1), :]
-        ratio = coef_ref[0, 1, pl.ds(e, 1), :]
-        product = coef_ref[0, 2, pl.ds(e, 1), :]
-        values = now[pl.ds(per * e, per), :].astype(jnp.float32)
-        slopes = now[pl.ds(rows + per * e, per), :].astype(jnp.float32)
-        rot[pl.ds(per * e, per), :] = (cosine * values + ratio * slopes).astype(rot.dtype)
-        rot[pl.ds(rows + per * e, per), :] = (cosine * slopes - product * values).astype(rot.dtype)
+    for k in range(parts * energies):
+        part, e = divmod(k, energies)
+        cosine = coef_ref[part, 0, 0, pl.ds(e, 1), :]
+        ratio = coef_ref[part, 0, 1, pl.ds(e, 1), :]
+        product = coef_ref[part, 0, 2, pl.ds(e, 1), :]
+        values = now[pl.ds(per * k, per), :].astype(jnp.float32)
+        slopes = now[pl.ds(rows + per * k, per), :].astype(jnp.float32)
+        rot[pl.ds(per * k, per), :] = (cosine * values + ratio * slopes).astype(rot.dtype)
+        rot[pl.ds(rows + per * k, per), :] = (cosine * slopes - product * values).astype(rot.dtype)
     low = lax.broadcasted_iota(jnp.int32, (rows, 128), 1) < 64
-    width = channels // parts
+    width = channels // pieces
     for q, basis_ref in enumerate(basis_refs):
-        if parts == 1:
+        if pieces == 1:
             fresh = jnp.dot(rot[...], basis_ref[0], preferred_element_type=jnp.float32)
         else:
             block = basis_ref[...].reshape(width, channels)
@@ -129,52 +132,58 @@
             lanes = slice(128 * k, 128 * k + 128)
             values = fresh[:rows, lanes]
             slopes = fresh[rows:, lanes]
-            out_ref[0, 2 * z] = jnp.where(low, values, pltpu.roll(slopes, 64, 1)).astype(out_ref.dtype)
-            out_ref[0, 2 * z + 1] = jnp.where(low, pltpu.roll(values, 64, 1), slopes).astype(out_ref.dtype)
+            one = jnp.where(low, values, pltpu.roll(slopes, 64, 1)).astype(out_ref.dtype)
+            two = jnp.where(low, pltpu.roll(values, 64, 1), slopes).astype(out_ref.dtype)
+            out_ref[0, 2 * z] = one.reshape(parts, own, 128)
+            out_ref[0, 2 * z + 1] = two.reshape(parts, own, 128)
 
     @pl.when(s == pl.num_programs(0) - 1)
     def _():
-        next_ref[0] = now[pl.ds(0, rows)]
-        next_ref[1] = now[pl.ds(rows, rows)]
-
-
-def stage(step, y_index, state, basis, coefs, kept):
-    sectors = coefs.shape[0]
+        for part, next_ref in enumerate(next_refs):
+            next_ref[0] = now[pl.ds(own * part, own)]
+            next_ref[1] = now[pl.ds(rows + own * part, own)]
+
+
+def stage(step, part, y_index, state, basis, coefs, kept):
+    sectors = coefs.shape[1]
     _, rows, channels = state.shape
-    first = kept is None
-    parts = 4 if first else 1
+    first = step == 0
+    pieces, parts = (4, PARTS) if first else (1, 1)
+    own = rows // parts
     if first:
         groups, _, share, _ = basis.shape
-        block = (groups // parts, 1, share, channels)
-        basis_specs = [pl.BlockSpec(block, lambda s, y, q=q: (q, s, 0, 0)) for q in range(parts)]
+        block = (groups // pieces, 1, share, channels)
+        basis_specs = [pl.BlockSpec(block, lambda s, y, q=q: (q, s, 0, 0)) for q in range(pieces)]
     else:
         basis_specs = [pl.BlockSpec((1, channels, channels), lambda s, y: (s, 0, 0))]
-    return pl.pallas_call(
-        functools.partial(stage_kernel, parts),
+    outs = pl.pallas_call(
+        functools.partial(stage_kernel, pieces, parts),
         grid_spec=pltpu.PrefetchScalarGridSpec(
             num_scalar_prefetch=1,
             grid=(sectors,),
             in_specs=[pl.BlockSpec(state.shape, lambda s, y: (0, 0, 0))]
             + basis_specs
-            + [pl.BlockSpec((1,) + coefs.shape[1:], lambda s, y: (s, 0, 0, 0))]
+            + [pl.BlockSpec((parts, 1) + coefs.shape[2:], lambda s, y: (part, s, 0, 0, 0))]
             + ([] if first else [pl.BlockSpec(memory_space=pl.ANY)]),
-            out_specs=[
-                pl.BlockSpec(state.shape, lambda s, y: (0, 0, 0)),
-                pl.BlockSpec((1, 16, rows, 128), lambda s, y: (jnp.where(y[0] == step, s, sectors), 0, 0, 0)),
+            out_specs=[pl.BlockSpec((2, own, channels), lambda s, y: (0, 0, 0))] * parts
+            + [
+                pl.BlockSpec(
+                    (1, 16, parts, own, 128),
+                    lambda s, y: (jnp.where(y[0] == step, s, sectors), 0, part, 0, 0),
+                ),
             ],
             scratch_shapes=[
                 pltpu.VMEM((2 * rows, channels), state.dtype),
                 pltpu.VMEM((2 * rows, channels), state.dtype),
             ],
         ),
-        out_shape=[
-            jax.ShapeDtypeStruct(state.shape, state.dtype),
-            jax.ShapeDtypeStruct((sectors + 1, 16, rows, 128), state.dtype),
-        ],
+        out_shape=[jax.ShapeDtypeStruct((2, own, channels), state.dtype)] * parts
+        + [jax.ShapeDtypeStruct((sectors + 1, 16, PARTS, own, 128), state.dtype)],
         input_output_aliases={} if first else {4: 1},
         compiler_params=pltpu.CompilerParams(vmem_limit_bytes=(48 if first else 16) * MIB),
         name="stage",
-    )(y_index, state, *[basis] * parts, coefs, *([] if first else [kept]))
+    )(y_index, state, *[basis] * pieces, coefs, *([] if first else [kept]))
+    return list(outs[:-1]), outs[-1]
 
 
 def finish_kernel(in_ref, out_ref):
@@ -222,13 +231,13 @@
     wave = jnp.sqrt(energies[None, :, None] - limits.astype(jnp.float32))
     sine = jnp.sin(wave)
     coefs = jnp.stack([jnp.cos(wave), sine / wave, wave * sine], axis=1)
-    kept = None
-    for step in range(planes):
-        if step:
-            state = lax.ppermute(state, "y", [(step - 1, step)])
-        if step == 1:
-            basis = turn(basis)
-        state, kept = stage(step, y_index, state, basis, coefs, kept)
+    coefs = coefs.reshape(4, 3, PARTS, count // PARTS, channels).transpose(2, 0, 1, 3, 4)
+    states, kept = stage(0, 0, y_index, state, basis, coefs, None)
+    basis = turn(basis)
+    for step in range(1, planes):
+        for part in range(PARTS):
+            state = lax.ppermute(states[part], "y", [(step - 1, step)])
+            (states[part],), kept = stage(step, part, y_index, state, basis, coefs, kept)
     back = lax.all_to_all(kept[:4].reshape(64, rows, lanes), PLANE, 0, 0)
     return finish(back.reshape(64, count, per, lanes))[None]
 

time: 247 us -> 228 us (0.923)
  waiting for transfers between devices: 105 us -> 68 us
  Pallas kernels: 39.6 us -> 53.3 us
  starting transfers between devices: 20 us -> 25.2 us
    ppermute x7 -> x14, waiting for transfers between devices: 53.4 us -> 17.1 us  [per_device(): state = lax.ppermute(states[part], 'y', [(step - 1, step)])]
    pallas_call x8 -> x15, Pallas kernels: 26.2 us -> 40 us  [stage(): pl.pallas_call(functools.partial(stage_kernel, pieces, parts), grid_spec=...]
    ppermute x7 -> x14, starting transfers between devices: 5.41 us -> 10.7 us  [per_device(): state = lax.ppermute(states[part], 'y', [(step - 1, step)])]
  transfers between devices with their start and end apart: 9 -> 16, of which waited for: 3 -> 4; matrix products, arithmetic and copies ran while one was open for 1% -> 1% of each run, Pallas kernels for 5% -> 19%
where the time goes in v5:
time: 228 us; the launch traced here: 227 us
  waiting for transfers between devices  68 us (30%)
  blocking collectives  60.5 us (27%)
  Pallas kernels  53.3 us (23%)
  starting transfers between devices  25.2 us (11%)
  between operations  13.8 us (6%)
  local copies, waits for them, and re-layouts  3.55 us (2%)
    all_to_all x1, blocking collectives, per_device(): back = lax.all_to_all(kept[:4].reshape(64, rows, lanes), PLANE, 0, 0)  50.4 us
    pallas_call x15, Pallas kernels, stage(): pl.pallas_call(functools.partial(stage_kernel, pieces, parts), grid_spec=...  40 us
    all_gather x1, waiting for transfers between devices, per_device(): basis = lax.all_gather(ring[:, :share], CH_AXES)  31.5 us
    all_to_all x1, waiting for transfers between devices, per_device(): lax.all_to_all(blocks.reshape(16, rows + per, lanes), CH_AXES, 0, 0)  19.4 us
    ppermute x14, waiting for transfers between devices, per_device(): state = lax.ppermute(states[part], 'y', [(step - 1, step)])  17.1 us
    all_to_all x1, starting transfers between devices, per_device(): lax.all_to_all(blocks.reshape(16, rows + per, lanes), CH_AXES, 0, 0)  14.6 us
    ppermute x14, starting transfers between devices, per_device(): state = lax.ppermute(states[part], 'y', [(step - 1, step)])  10.7 us
    all_gather x1, blocking collectives, per_device(): ring = lax.all_gather(jnp.concatenate([intersection[0], extra]), 'x')  10 us
  transfers between devices with their start and end apart: 16, of which 4 were waited for; matrix products, arithmetic and copies ran while one was open for 1% of the time, Pallas kernels for 19%

profile of v5, /device:TPU:63, one launch (start us, length us, event | category | flops | bytes accessed | tf_op | source)
XLA Modules:
  0.0 226.6 jit_solution(6708066429156138913)
XLA Ops:
  6.5 0.9 fusion.1
  7.5 10.0 %all-gather = bf16[288,1024]{1,0:T(8,128)(2,1)S(1)} all-gather(bf16[72,1024]{1,0:T(8,128)(2,1)S(1)} %fusion.1), channel_id=2, replica_groups=mesh['y'=8,'x'=4,'z'=8,'core'=2] {'x'}, dimensions={0}, use_global_device_ids=true | all-gather | bytes 737280 | tf_op jit(solution)/shard_map/all_gather | solution.py:221
  17.5 0.8 slice.17
  19.1 4.1 %spread.1 = bf16[16,7,16,128]{3,2,1,0:T(8,128)(2,1)} custom-call(s32[1]{0:T(128)} %bitcast.1.x_ref, bf16[6,64,2048]{2,1,0:T(8,128)(2,1)} %p_ref.1, bf16[6,64,2048]{2,1,0:T(8,128)(2,1)} %p_ref.1, bf16[16,128]{1,0:T(8,128)(2,1)} %pad.9.limit_ref), custom_call_target="tpu_custom_call" | custom-call | tf_op jit(solution)/shard_map/spread/pallas_call | solution.py:36
  23.2 14.6 %all-to-all-start = ((bf16[16,112,128]{2,1,0:T(8,128)(2,1)}), bf16[16,112,128]{2,1,0:T(8,128)(2,1)S(1)}, u32[]{:S(2)}, u32[]{:S(2)}) async-start(bf16[16,112,128]{2,1,0:T(8,128)(2,1)} %bitcast.24), calls=%async_computation | async-start | bytes 917504 | tf_op jit(solution)/shard_map/all_to_all | solution.py:228
  37.9 19.4 %all-to-all-done.in_ref = bf16[16,112,128]{2,1,0:T(8,128)(2,1)S(1)} async-done(((bf16[16,112,128]{2,1,0:T(8,128)(2,1)}), bf16[16,112,128]{2,1,0:T(8,128)(2,1)S(1)}, u32[]{:S(2)}, u32[]{:S(2)}) %all-to-all-start) | async-done | bytes 458784 | tf_op jit(solution)/shard_map/all_to_all | solution.py:228
  58.1 2.0 join.1.state_ref
  60.0 1.2 fusion.5
  61.3 31.5 %all-gather.4.cloned.1.call-done = bf16[64,64,1024]{2,1,0:T(8,128)(2,1)} async-done(((bf16[4,64,1024]{2,1,0:T(8,128)(2,1)}), bf16[64,64,1024]{2,1,0:T(8,128)(2,1)}) %all-gather.4.cloned.1.call-update) | async-done | bytes 8388624 | tf_op jit(solution)/shard_map/all_gather | solution.py:222
  92.8 1.0 copy-done
  93.8 6.1 %stage.15 = (bf16[2,48,1024]{2,1,0:T(8,128)(2,1)S(1)}, bf16[2,48,1024]{2,1,0:T(8,128)(2,1)S(1)}, bf16[5,16,2,48,128]{4,3,2,1,0:T(8,128)(2,1)S(1)}) custom-call(s32[1]{0:T(128)} %bitcast.y_ref, bf16[2,96,1024]{2,1,0:T(8,128)(2,1)S(1)} %copy-done, bf16[16,4,64,1024]{3,2,1,0:T(8,128)(2,1)} %bitcast.13, bf16[16,4,64,1024]{3,2,1,0:T(8,128)(2,1)} %bitcast.14, ...), custom_call_target="tpu_custom_call" | custom-call | tf_op jit(solution)/shard_map/stage/pallas_call | solution.py:159
  101.3 5.2 %turn.1.refs_0_ = bf16[4,1024,1024]{2,1,0:T(8,128)(2,1)S(1)} custom-call(bf16[16,4,64,1024]{3,2,1,0:T(8,128)(2,1)} %bitcast.17, bf16[16,4,64,1024]{3,2,1,0:T(8,128)(2,1)} %bitcast.18, bf16[16,4,64,1024]{3,2,1,0:T(8,128)(2,1)} %bitcast.19, bf16[16,4,64,1024]{3,2,1,0:T(8,128)(2,1)} %bitcast.20), custom_call_target="tpu_custom_call" | custom-call | tf_op jit(solution)/shard_map/turn/pallas_call | solution.py:84
  106.5 2.3 %stage.16 = (bf16[2,48,1024]{2,1,0:T(8,128)(2,1)S(1)}, bf16[5,16,2,48,128]{4,3,2,1,0:T(8,128)(2,1)S(1)}) custom-call(s32[1]{0:T(128)} %bitcast.y_ref, bf16[2,48,1024]{2,1,0:T(8,128)(2,1)S(1)} %collective-permute-done.1.state_ref, bf16[4,1024,1024]{2,1,0:T(8,128)(2,1)S(1)} %turn.1.refs_0_, ...), custom_call_target="tpu_custom_call", output_to_operand_aliasing={{1}: (4, {})} | custom-call | tf_op jit(solution)/shard_map/stage/pallas_call | solution.py:159
  109.5 2.3 %stage.17 = (bf16[2,48,1024]{2,1,0:T(8,128)(2,1)S(1)}, bf16[5,16,2,48,128]{4,3,2,1,0:T(8,128)(2,1)S(1)}) custom-call(s32[1]{0:T(128)} %bitcast.y_ref, bf16[2,48,1024]{2,1,0:T(8,128)(2,1)S(1)} %collective-permute-done.state_ref, bf16[4,1024,1024]{2,1,0:T(8,128)(2,1)S(1)} %turn.1.refs_0_, ...), custom_call_target="tpu_custom_call", output_to_operand_aliasing={{1}: (4, {})} | custom-call | tf_op jit(solution)/shard_map/stage/pallas_call | solution.py:159
  112.5 2.3 %stage.18 = (bf16[2,48,1024]{2,1,0:T(8,128)(2,1)S(1)}, bf16[5,16,2,48,128]{4,3,2,1,0:T(8,128)(2,1)S(1)}) custom-call(s32[1]{0:T(128)} %bitcast.y_ref, bf16[2,48,1024]{2,1,0:T(8,128)(2,1)S(1)} %collective-permute-done.3.state_ref, bf16[4,1024,1024]{2,1,0:T(8,128)(2,1)S(1)} %turn.1.refs_0_, ...), custom_call_target="tpu_custom_call", output_to_operand_aliasing={{1}: (4, {})} | custom-call | tf_op jit(solution)/shard_map/stage/pallas_call | solution.py:159
  115.6 2.3 %stage.19 = (bf16[2,48,1024]{2,1,0:T(8,128)(2,1)S(1)}, bf16[5,16,2,48,128]{4,3,2,1,0:T(8,128)(2,1)S(1)}) custom-call(s32[1]{0:T(128)} %bitcast.y_ref, bf16[2,48,1024]{2,1,0:T(8,128)(2,1)S(1)} %collective-permute-done.2.state_ref, bf16[4,1024,1024]{2,1,0:T(8,128)(2,1)S(1)} %turn.1.refs_0_, ...), custom_call_target="tpu_custom_call", output_to_operand_aliasing={{1}: (4, {})} | custom-call | tf_op jit(solution)/shard_map/stage/pallas_call | solution.py:159
  118.6 2.3 %stage.20 = (bf16[2,48,1024]{2,1,0:T(8,128)(2,1)S(1)}, bf16[5,16,2,48,128]{4,3,2,1,0:T(8,128)(2,1)S(1)}) custom-call(s32[1]{0:T(128)} %bitcast.y_ref, bf16[2,48,1024]{2,1,0:T(8,128)(2,1)S(1)} %collective-permute-done.5.state_ref, bf16[4,1024,1024]{2,1,0:T(8,128)(2,1)S(1)} %turn.1.refs_0_, ...), custom_call_target="tpu_custom_call", output_to_operand_aliasing={{1}: (4, {})} | custom-call | tf_op jit(solution)/shard_map/stage/pallas_call | solution.py:159
  121.6 2.3 %stage.21 = (bf16[2,48,1024]{2,1,0:T(8,128)(2,1)S(1)}, bf16[5,16,2,48,128]{4,3,2,1,0:T(8,128)(2,1)S(1)}) custom-call(s32[1]{0:T(128)} %bitcast.y_ref, bf16[2,48,1024]{2,1,0:T(8,128)(2,1)S(1)} %collective-permute-done.4.state_ref, bf16[4,1024,1024]{2,1,0:T(8,128)(2,1)S(1)} %turn.1.refs_0_, ...), custom_call_target="tpu_custom_call", output_to_operand_aliasing={{1}: (4, {})} | custom-call | tf_op jit(solution)/shard_map/stage/pallas_call | solution.py:159
  124.6 2.3 %stage.22 = (bf16[2,48,1024]{2,1,0:T(8,128)(2,1)S(1)}, bf16[5,16,2,48,128]{4,3,2,1,0:T(8,128)(2,1)S(1)}) custom-call(s32[1]{0:T(128)} %bitcast.y_ref, bf16[2,48,1024]{2,1,0:T(8,128)(2,1)S(1)} %collective-permute-done.7.state_ref, bf16[4,1024,1024]{2,1,0:T(8,128)(2,1)S(1)} %turn.1.refs_0_, ...), custom_call_target="tpu_custom_call", output_to_operand_aliasing={{1}: (4, {})} | custom-call | tf_op jit(solution)/shard_map/stage/pallas_call | solution.py:159
  127.7 2.3 %stage.23 = (bf16[2,48,1024]{2,1,0:T(8,128)(2,1)S(1)}, bf16[5,16,2,48,128]{4,3,2,1,0:T(8,128)(2,1)S(1)}) custom-call(s32[1]{0:T(128)} %bitcast.y_ref, bf16[2,48,1024]{2,1,0:T(8,128)(2,1)S(1)} %collective-permute-done.6.state_ref, bf16[4,1024,1024]{2,1,0:T(8,128)(2,1)S(1)} %turn.1.refs_0_, ...), custom_call_target="tpu_custom_call", output_to_operand_aliasing={{1}: (4, {})} | custom-call | tf_op jit(solution)/shard_map/stage/pallas_call | solution.py:159
  130.7 2.3 %stage.24 = (bf16[2,48,1024]{2,1,0:T(8,128)(2,1)S(1)}, bf16[5,16,2,48,128]{4,3,2,1,0:T(8,128)(2,1)S(1)}) custom-call(s32[1]{0:T(128)} %bitcast.y_ref, bf16[2,48,1024]{2,1,0:T(8,128)(2,1)S(1)} %collective-permute-done.9.state_ref, bf16[4,1024,1024]{2,1,0:T(8,128)(2,1)S(1)} %turn.1.refs_0_, ...), custom_call_target="tpu_custom_call", output_to_operand_aliasing={{1}: (4, {})} | custom-call | tf_op jit(solution)/shard_map/stage/pallas_call | solution.py:159
  133.7 2.3 %stage.25 = (bf16[2,48,1024]{2,1,0:T(8,128)(2,1)S(1)}, bf16[5,16,2,48,128]{4,3,2,1,0:T(8,128)(2,1)S(1)}) custom-call(s32[1]{0:T(128)} %bitcast.y_ref, bf16[2,48,1024]{2,1,0:T(8,128)(2,1)S(1)} %collective-permute-done.8.state_ref, bf16[4,1024,1024]{2,1,0:T(8,128)(2,1)S(1)} %turn.1.refs_0_, ...), custom_call_target="tpu_custom_call", output_to_operand_aliasing={{1}: (4, {})} | custom-call | tf_op jit(solution)/shard_map/stage/pallas_call | solution.py:159
  136.8 2.3 %stage.26 = (bf16[2,48,1024]{2,1,0:T(8,128)(2,1)S(1)}, bf16[5,16,2,48,128]{4,3,2,1,0:T(8,128)(2,1)S(1)}) custom-call(s32[1]{0:T(128)} %bitcast.y_ref, bf16[2,48,1024]{2,1,0:T(8,128)(2,1)S(1)} %collective-permute-done.11.state_ref, bf16[4,1024,1024]{2,1,0:T(8,128)(2,1)S(1)} %turn.1.refs_0_, ...), custom_call_target="tpu_custom_call", output_to_operand_aliasing={{1}: (4, {})} | custom-call | tf_op jit(solution)/shard_map/stage/pallas_call | solution.py:159
  139.1 1.3 collective-permute-start.13
  140.4 2.3 %stage.27 = (bf16[2,48,1024]{2,1,0:T(8,128)(2,1)S(1)}, bf16[5,16,2,48,128]{4,3,2,1,0:T(8,128)(2,1)S(1)}) custom-call(s32[1]{0:T(128)} %bitcast.y_ref, bf16[2,48,1024]{2,1,0:T(8,128)(2,1)S(1)} %collective-permute-done.10.state_ref, bf16[4,1024,1024]{2,1,0:T(8,128)(2,1)S(1)} %turn.1.refs_0_, ...), custom_call_target="tpu_custom_call", output_to_operand_aliasing={{1}: (4, {})} | custom-call | tf_op jit(solution)/shard_map/stage/pallas_call | solution.py:159
  142.7 1.3 collective-permute-start.12
  144.0 8.9 %collective-permute-done.13.state_ref = bf16[2,48,1024]{2,1,0:T(8,128)(2,1)S(1)} collective-permute-done((bf16[2,48,1024]{2,1,0:T(8,128)(2,1)S(1)}, bf16[2,48,1024]{2,1,0:T(8,128)(2,1)S(1)}, u32[]{:S(2)}, u32[]{:S(2)}) %collective-permute-start.13) | collective-permute-done | bytes 196640 | tf_op jit(solution)/shard_map/ppermute | solution.py:239
  152.9 3.0 %stage.28 = (bf16[2,48,1024]{2,1,0:T(8,128)(2,1)}, bf16[5,16,2,48,128]{4,3,2,1,0:T(8,128)(2,1)S(1)}) custom-call(s32[1]{0:T(128)} %bitcast.y_ref, bf16[2,48,1024]{2,1,0:T(8,128)(2,1)S(1)} %collective-permute-done.13.state_ref, bf16[4,1024,1024]{2,1,0:T(8,128)(2,1)S(1)} %turn.1.refs_0_, ...), custom_call_target="tpu_custom_call", output_to_operand_aliasing={{1}: (4, {})} | custom-call | tf_op jit(solution)/shard_map/stage/pallas_call | solution.py:159
  155.9 8.2 %collective-permute-done.12.state_ref = bf16[2,48,1024]{2,1,0:T(8,128)(2,1)S(1)} collective-permute-done((bf16[2,48,1024]{2,1,0:T(8,128)(2,1)S(1)}, bf16[2,48,1024]{2,1,0:T(8,128)(2,1)S(1)}, u32[]{:S(2)}, u32[]{:S(2)}) %collective-permute-start.12) | collective-permute-done | bytes 196640 | tf_op jit(solution)/shard_map/ppermute | solution.py:239
  164.2 3.0 %stage.29 = (bf16[2,48,1024]{2,1,0:T(8,128)(2,1)}, bf16[5,16,2,48,128]{4,3,2,1,0:T(8,128)(2,1)S(1)}) custom-call(s32[1]{0:T(128)} %bitcast.y_ref, bf16[2,48,1024]{2,1,0:T(8,128)(2,1)S(1)} %collective-permute-done.12.state_ref, bf16[4,1024,1024]{2,1,0:T(8,128)(2,1)S(1)} %turn.1.refs_0_, ...), custom_call_target="tpu_custom_call", output_to_operand_aliasing={{1}: (4, {})} | custom-call | tf_op jit(solution)/shard_map/stage/pallas_call | solution.py:159
  167.3 50.4 %all_to_all.10 = bf16[64,96,128]{2,1,0:T(8,128)(2,1)S(1)} all-to-all(bf16[64,96,128]{2,1,0:T(8,128)(2,1)S(1)} %bitcast.21), channel_id=1, replica_groups=mesh['y'=8,'x'=4,'z'=8,'core'=2] {'x','z','core'}, dimensions={0} | all-to-all | bytes 3145728 | tf_op jit(solution)/shard_map/all_to_all | solution.py:241
  217.7 2.1 finish.1
  (41 shorter events, 10.0 us)
Async XLA Ops:
  6.5 86.3 %all-gather.4.cloned.1.call-start = ((), (), s32[]{:S(2)}) async-start(), calls=%async_computation.2 | async-start | bytes 8912896 | tf_op jit(solution)/shard_map/all_gather | solution.py:222
  19.1 18.7 %copy-start.2 = (f32[6]{0:T(128)S(1)}, f32[6]{0:T(128)}, u32[]{:S(2)}) copy-start(f32[6]{0:T(128)} %param.5) | copy-start | bytes 76
  23.2 34.0 %all-to-all-start = ((bf16[16,112,128]{2,1,0:T(8,128)(2,1)}), bf16[16,112,128]{2,1,0:T(8,128)(2,1)S(1)}, u32[]{:S(2)}, u32[]{:S(2)}) async-start(bf16[16,112,128]{2,1,0:T(8,128)(2,1)} %bitcast.24), calls=%async_computation | async-start | bytes 917504 | tf_op jit(solution)/shard_map/all_to_all | solution.py:228
  57.2 0.8 copy-start.1
  92.8 1.0 copy-start
  99.9 6.6 %collective-permute-start.1 = (bf16[2,48,1024]{2,1,0:T(8,128)(2,1)S(1)}, bf16[2,48,1024]{2,1,0:T(8,128)(2,1)S(1)}, u32[]{:S(2)}, u32[]{:S(2)}) collective-permute-start(bf16[2,48,1024]{2,1,0:T(8,128)(2,1)S(1)} %get-tuple-element.35), channel_id=1, source_target_pairs={{0,64},{1,65},{2,66},{3,67},{4,68},{5,69},{6,70},{7,71},{8,72},{9,... | collective-permute-start | bytes 589832 | tf_op jit(solution)/shard_map/ppermute | solution.py:239
  100.6 8.9 %collective-permute-start = (bf16[2,48,1024]{2,1,0:T(8,128)(2,1)S(1)}, bf16[2,48,1024]{2,1,0:T(8,128)(2,1)S(1)}, u32[]{:S(2)}, u32[]{:S(2)}) collective-permute-start(bf16[2,48,1024]{2,1,0:T(8,128)(2,1)S(1)} %get-tuple-element.34), channel_id=1, source_target_pairs={{0,64},{1,65},{2,66},{3,67},{4,68},{5,69},{6,70},{7,71},{8,72},{9,... | collective-permute-start | bytes 589832 | tf_op jit(solution)/shard_map/ppermute | solution.py:239
  108.8 3.7 %collective-permute-start.3 = (bf16[2,48,1024]{2,1,0:T(8,128)(2,1)S(1)}, bf16[2,48,1024]{2,1,0:T(8,128)(2,1)S(1)}, u32[]{:S(2)}, u32[]{:S(2)}) collective-permute-start(bf16[2,48,1024]{2,1,0:T(8,128)(2,1)S(1)} %get-tuple-element.39), channel_id=1, source_target_pairs={{64,128},{65,129},{66,130},{67,131},{68,132},{69,133},{70,134},{71... | collective-permute-start | bytes 589832 | tf_op jit(solution)/shard_map/ppermute | solution.py:239
  111.8 3.7 %collective-permute-start.2 = (bf16[2,48,1024]{2,1,0:T(8,128)(2,1)S(1)}, bf16[2,48,1024]{2,1,0:T(8,128)(2,1)S(1)}, u32[]{:S(2)}, u32[]{:S(2)}) collective-permute-start(bf16[2,48,1024]{2,1,0:T(8,128)(2,1)S(1)} %get-tuple-element.38), channel_id=1, source_target_pairs={{64,128},{65,129},{66,130},{67,131},{68,132},{69,133},{70,134},{71... | collective-permute-start | bytes 589832 | tf_op jit(solution)/shard_map/ppermute | solution.py:239
  114.9 3.7 %collective-permute-start.5 = (bf16[2,48,1024]{2,1,0:T(8,128)(2,1)S(1)}, bf16[2,48,1024]{2,1,0:T(8,128)(2,1)S(1)}, u32[]{:S(2)}, u32[]{:S(2)}) collective-permute-start(bf16[2,48,1024]{2,1,0:T(8,128)(2,1)S(1)} %get-tuple-element.43), channel_id=1, source_target_pairs={{128,192},{129,193},{130,194},{131,195},{132,196},{133,197},{134,1... | collective-permute-start | bytes 589832 | tf_op jit(solution)/shard_map/ppermute | solution.py:239
  117.9 3.7 %collective-permute-start.4 = (bf16[2,48,1024]{2,1,0:T(8,128)(2,1)S(1)}, bf16[2,48,1024]{2,1,0:T(8,128)(2,1)S(1)}, u32[]{:S(2)}, u32[]{:S(2)}) collective-permute-start(bf16[2,48,1024]{2,1,0:T(8,128)(2,1)S(1)} %get-tuple-element.42), channel_id=1, source_target_pairs={{128,192},{129,193},{130,194},{131,195},{132,196},{133,197},{134,1... | collective-permute-start | bytes 589832 | tf_op jit(solution)/shard_map/ppermute | solution.py:239
  120.9 3.7 %collective-permute-start.7 = (bf16[2,48,1024]{2,1,0:T(8,128)(2,1)S(1)}, bf16[2,48,1024]{2,1,0:T(8,128)(2,1)S(1)}, u32[]{:S(2)}, u32[]{:S(2)}) collective-permute-start(bf16[2,48,1024]{2,1,0:T(8,128)(2,1)S(1)} %get-tuple-element.47), channel_id=1, source_target_pairs={{192,256},{193,257},{194,258},{195,259},{196,260},{197,261},{198,2... | collective-permute-start | bytes 589832 | tf_op jit(solution)/shard_map/ppermute | solution.py:239
  124.0 3.7 %collective-permute-start.6 = (bf16[2,48,1024]{2,1,0:T(8,128)(2,1)S(1)}, bf16[2,48,1024]{2,1,0:T(8,128)(2,1)S(1)}, u32[]{:S(2)}, u32[]{:S(2)}) collective-permute-start(bf16[2,48,1024]{2,1,0:T(8,128)(2,1)S(1)} %get-tuple-element.46), channel_id=1, source_target_pairs={{192,256},{193,257},{194,258},{195,259},{196,260},{197,261},{198,2... | collective-permute-start | bytes 589832 | tf_op jit(solution)/shard_map/ppermute | solution.py:239
  127.0 3.7 %collective-permute-start.9 = (bf16[2,48,1024]{2,1,0:T(8,128)(2,1)S(1)}, bf16[2,48,1024]{2,1,0:T(8,128)(2,1)S(1)}, u32[]{:S(2)}, u32[]{:S(2)}) collective-permute-start(bf16[2,48,1024]{2,1,0:T(8,128)(2,1)S(1)} %get-tuple-element.51), channel_id=1, source_target_pairs={{256,320},{257,321},{258,322},{259,323},{260,324},{261,325},{262,3... | collective-permute-start | bytes 589832 | tf_op jit(solution)/shard_map/ppermute | solution.py:239
  130.0 3.7 %collective-permute-start.8 = (bf16[2,48,1024]{2,1,0:T(8,128)(2,1)S(1)}, bf16[2,48,1024]{2,1,0:T(8,128)(2,1)S(1)}, u32[]{:S(2)}, u32[]{:S(2)}) collective-permute-start(bf16[2,48,1024]{2,1,0:T(8,128)(2,1)S(1)} %get-tuple-element.50), channel_id=1, source_target_pairs={{256,320},{257,321},{258,322},{259,323},{260,324},{261,325},{262,3... | collective-permute-start | bytes 589832 | tf_op jit(solution)/shard_map/ppermute | solution.py:239
  133.0 3.7 %collective-permute-start.11 = (bf16[2,48,1024]{2,1,0:T(8,128)(2,1)S(1)}, bf16[2,48,1024]{2,1,0:T(8,128)(2,1)S(1)}, u32[]{:S(2)}, u32[]{:S(2)}) collective-permute-start(bf16[2,48,1024]{2,1,0:T(8,128)(2,1)S(1)} %get-tuple-element.55), channel_id=1, source_target_pairs={{320,384},{321,385},{322,386},{323,387},{324,388},{325,389},{326,3... | collective-permute-start | bytes 589832 | tf_op jit(solution)/shard_map/ppermute | solution.py:239
  136.1 4.3 %collective-permute-start.10 = (bf16[2,48,1024]{2,1,0:T(8,128)(2,1)S(1)}, bf16[2,48,1024]{2,1,0:T(8,128)(2,1)S(1)}, u32[]{:S(2)}, u32[]{:S(2)}) collective-permute-start(bf16[2,48,1024]{2,1,0:T(8,128)(2,1)S(1)} %get-tuple-element.54), channel_id=1, source_target_pairs={{320,384},{321,385},{322,386},{323,387},{324,388},{325,389},{326,3... | collective-permute-start | bytes 589832 | tf_op jit(solution)/shard_map/ppermute | solution.py:239
  139.1 13.8 %collective-permute-start.13 = (bf16[2,48,1024]{2,1,0:T(8,128)(2,1)S(1)}, bf16[2,48,1024]{2,1,0:T(8,128)(2,1)S(1)}, u32[]{:S(2)}, u32[]{:S(2)}) collective-permute-start(bf16[2,48,1024]{2,1,0:T(8,128)(2,1)S(1)} %get-tuple-element.59), channel_id=1, source_target_pairs={{384,448},{385,449},{386,450},{387,451},{388,452},{389,453},{390,4... | collective-permute-start | bytes 589832 | tf_op jit(solution)/shard_map/ppermute | solution.py:239
  142.7 21.4 %collective-permute-start.12 = (bf16[2,48,1024]{2,1,0:T(8,128)(2,1)S(1)}, bf16[2,48,1024]{2,1,0:T(8,128)(2,1)S(1)}, u32[]{:S(2)}, u32[]{:S(2)}) collective-permute-start(bf16[2,48,1024]{2,1,0:T(8,128)(2,1)S(1)} %get-tuple-element.58), channel_id=1, source_target_pairs={{384,448},{385,449},{386,450},{387,451},{388,452},{389,453},{390,4... | collective-permute-start | bytes 589832 | tf_op jit(solution)/shard_map/ppermute | solution.py:239
Sparse Core Ops, SparseCore 0:
  18.5 74.2 all-gather.3

commit v6 on v5

--- a/solution.py
+++ b/solution.py
@@ -13,7 +13,7 @@
 CH_AXES = ("z", "core")
 PLANE = ("x", "z", "core")
 MIB = 1024 * 1024
-PARTS = 2
+PARTS = 3
 
 
 def spread_kernel(x_ref, v_ref, p_ref, limit_ref, out_ref):

time: 228 us -> 234 us (1.026)
  the two profiles are of different devices: /device:TPU:63 before, /device:TPU:31 now
where the time goes in v6:
time: 234 us; the launch traced here: 233 us
  Pallas kernels  71.1 us (30%)
  blocking collectives  57.6 us (25%)
  waiting for transfers between devices  50.4 us (22%)
  starting transfers between devices  33.8 us (14%)
  between operations  13.9 us (6%)
  local copies, waits for them, and re-layouts  3.68 us (2%)
  other arithmetic  2.74 us (1%)
    pallas_call x22, Pallas kernels, stage(): pl.pallas_call(functools.partial(stage_kernel, pieces, parts), grid_spec=...  57.8 us
    all_to_all x1, blocking collectives, per_device(): back = lax.all_to_all(kept[:4].reshape(64, rows, lanes), PLANE, 0, 0)  47.6 us
    all_gather x1, waiting for transfers between devices, per_device(): basis = lax.all_gather(ring[:, :share], CH_AXES)  31.3 us
    ppermute x21, starting transfers between devices, per_device(): state = lax.ppermute(states[part], 'y', [(step - 1, step)])  19.2 us
    all_to_all x1, waiting for transfers between devices, per_device(): lax.all_to_all(blocks.reshape(16, rows + per, lanes), CH_AXES, 0, 0)  19 us
    all_to_all x1, starting transfers between devices, per_device(): lax.all_to_all(blocks.reshape(16, rows + per, lanes), CH_AXES, 0, 0)  14.6 us
    all_gather x1, blocking collectives, per_device(): ring = lax.all_gather(jnp.concatenate([intersection[0], extra]), 'x')  10 us
    pallas_call x1, Pallas kernels, turn(): pl.pallas_call(turn_kernel, grid=(sectors,), in_specs=specs, out_specs=pl...  5.19 us
  transfers between devices with their start and end apart: 23, of which 2 were waited for; matrix products, arithmetic and copies ran while one was open for 1% of the time, Pallas kernels for 26%

profile of v6, /device:TPU:31, one launch (start us, length us, event | category | flops | bytes accessed | tf_op | source)
XLA Modules:
  0.0 233.3 jit_solution(17717535651270414154)
XLA Ops:
  7.5 10.0 %all-gather = bf16[288,1024]{1,0:T(8,128)(2,1)S(1)} all-gather(bf16[72,1024]{1,0:T(8,128)(2,1)S(1)} %fusion.1), channel_id=2, replica_groups=mesh['y'=8,'x'=4,'z'=8,'core'=2] {'x'}, dimensions={0}, use_global_device_ids=true | all-gather | bytes 737280 | tf_op jit(solution)/shard_map/all_gather | solution.py:221
  19.1 4.1 %spread.1 = bf16[16,7,16,128]{3,2,1,0:T(8,128)(2,1)} custom-call(s32[1]{0:T(128)} %bitcast.1.x_ref, bf16[6,64,2048]{2,1,0:T(8,128)(2,1)} %p_ref.1, bf16[6,64,2048]{2,1,0:T(8,128)(2,1)} %p_ref.1, bf16[16,128]{1,0:T(8,128)(2,1)} %pad.9.limit_ref), custom_call_target="tpu_custom_call" | custom-call | tf_op jit(solution)/shard_map/spread/pallas_call | solution.py:36
  23.2 14.6 %all-to-all-start = ((bf16[16,112,128]{2,1,0:T(8,128)(2,1)}), bf16[16,112,128]{2,1,0:T(8,128)(2,1)S(1)}, u32[]{:S(2)}, u32[]{:S(2)}) async-start(bf16[16,112,128]{2,1,0:T(8,128)(2,1)} %bitcast.24), calls=%async_computation | async-start | bytes 917504 | tf_op jit(solution)/shard_map/all_to_all | solution.py:228
  37.8 19.0 %all-to-all-done.in_ref = bf16[16,112,128]{2,1,0:T(8,128)(2,1)S(1)} async-done(((bf16[16,112,128]{2,1,0:T(8,128)(2,1)}), bf16[16,112,128]{2,1,0:T(8,128)(2,1)S(1)}, u32[]{:S(2)}, u32[]{:S(2)}) %all-to-all-start) | async-done | bytes 458784 | tf_op jit(solution)/shard_map/all_to_all | solution.py:228
  57.7 2.0 join.1.state_ref
  61.5 31.3 %all-gather.4.cloned.1.call-done = bf16[64,64,1024]{2,1,0:T(8,128)(2,1)} async-done(((bf16[4,64,1024]{2,1,0:T(8,128)(2,1)}), bf16[64,64,1024]{2,1,0:T(8,128)(2,1)}) %all-gather.4.cloned.1.call-update) | async-done | bytes 8388624 | tf_op jit(solution)/shard_map/all_gather | solution.py:222
  93.8 6.1 %stage.22 = (bf16[2,32,1024]{2,1,0:T(8,128)(2,1)S(1)}, bf16[2,32,1024]{2,1,0:T(8,128)(2,1)S(1)}, bf16[2,32,1024]{2,1,0:T(8,128)(2,1)S(1)}, bf16[5,16,3,32,128]{4,3,2,1,0:T(8,128)(2,1)S(1)}) custom-call(s32[1]{0:T(128)} %bitcast.y_ref, bf16[2,96,1024]{2,1,0:T(8,128)(2,1)S(1)} %copy-done, bf16[16,4,64,1024]{3,2,1,0:T(8,128)(2,1)} %bitcast.13, ...), custom_call_target="tpu_custom_call" | custom-call | tf_op jit(solution)/shard_map/stage/pallas_call | solution.py:159
  101.9 5.2 %turn.1.refs_0_ = bf16[4,1024,1024]{2,1,0:T(8,128)(2,1)S(1)} custom-call(bf16[16,4,64,1024]{3,2,1,0:T(8,128)(2,1)} %bitcast.17, bf16[16,4,64,1024]{3,2,1,0:T(8,128)(2,1)} %bitcast.18, bf16[16,4,64,1024]{3,2,1,0:T(8,128)(2,1)} %bitcast.19, bf16[16,4,64,1024]{3,2,1,0:T(8,128)(2,1)} %bitcast.20), custom_call_target="tpu_custom_call" | custom-call | tf_op jit(solution)/shard_map/turn/pallas_call | solution.py:84
  107.1 2.4 %stage.23 = (bf16[2,32,1024]{2,1,0:T(8,128)(2,1)S(1)}, bf16[5,16,3,32,128]{4,3,2,1,0:T(8,128)(2,1)S(1)}) custom-call(s32[1]{0:T(128)} %bitcast.y_ref, bf16[2,32,1024]{2,1,0:T(8,128)(2,1)S(1)} %collective-permute-done.2.state_ref, bf16[4,1024,1024]{2,1,0:T(8,128)(2,1)S(1)} %turn.1.refs_0_, ...), custom_call_target="tpu_custom_call", output_to_operand_aliasing={{1}: (4, {})} | custom-call | tf_op jit(solution)/shard_map/stage/pallas_call | solution.py:159
  110.2 2.4 %stage.24 = (bf16[2,32,1024]{2,1,0:T(8,128)(2,1)S(1)}, bf16[5,16,3,32,128]{4,3,2,1,0:T(8,128)(2,1)S(1)}) custom-call(s32[1]{0:T(128)} %bitcast.y_ref, bf16[2,32,1024]{2,1,0:T(8,128)(2,1)S(1)} %collective-permute-done.1.state_ref, bf16[4,1024,1024]{2,1,0:T(8,128)(2,1)S(1)} %turn.1.refs_0_, ...), custom_call_target="tpu_custom_call", output_to_operand_aliasing={{1}: (4, {})} | custom-call | tf_op jit(solution)/shard_map/stage/pallas_call | solution.py:159
  113.2 2.4 %stage.25 = (bf16[2,32,1024]{2,1,0:T(8,128)(2,1)S(1)}, bf16[5,16,3,32,128]{4,3,2,1,0:T(8,128)(2,1)S(1)}) custom-call(s32[1]{0:T(128)} %bitcast.y_ref, bf16[2,32,1024]{2,1,0:T(8,128)(2,1)S(1)} %collective-permute-done.state_ref, bf16[4,1024,1024]{2,1,0:T(8,128)(2,1)S(1)} %turn.1.refs_0_, ...), custom_call_target="tpu_custom_call", output_to_operand_aliasing={{1}: (4, {})} | custom-call | tf_op jit(solution)/shard_map/stage/pallas_call | solution.py:159
  116.3 2.4 %stage.26 = (bf16[2,32,1024]{2,1,0:T(8,128)(2,1)S(1)}, bf16[5,16,3,32,128]{4,3,2,1,0:T(8,128)(2,1)S(1)}) custom-call(s32[1]{0:T(128)} %bitcast.y_ref, bf16[2,32,1024]{2,1,0:T(8,128)(2,1)S(1)} %collective-permute-done.5.state_ref, bf16[4,1024,1024]{2,1,0:T(8,128)(2,1)S(1)} %turn.1.refs_0_, ...), custom_call_target="tpu_custom_call", output_to_operand_aliasing={{1}: (4, {})} | custom-call | tf_op jit(solution)/shard_map/stage/pallas_call | solution.py:159
  120.0 2.4 %stage.27 = (bf16[2,32,1024]{2,1,0:T(8,128)(2,1)S(1)}, bf16[5,16,3,32,128]{4,3,2,1,0:T(8,128)(2,1)S(1)}) custom-call(s32[1]{0:T(128)} %bitcast.y_ref, bf16[2,32,1024]{2,1,0:T(8,128)(2,1)S(1)} %collective-permute-done.4.state_ref, bf16[4,1024,1024]{2,1,0:T(8,128)(2,1)S(1)} %turn.1.refs_0_, ...), custom_call_target="tpu_custom_call", output_to_operand_aliasing={{1}: (4, {})} | custom-call | tf_op jit(solution)/shard_map/stage/pallas_call | solution.py:159
  123.7 2.4 %stage.28 = (bf16[2,32,1024]{2,1,0:T(8,128)(2,1)S(1)}, bf16[5,16,3,32,128]{4,3,2,1,0:T(8,128)(2,1)S(1)}) custom-call(s32[1]{0:T(128)} %bitcast.y_ref, bf16[2,32,1024]{2,1,0:T(8,128)(2,1)S(1)} %collective-permute-done.3.state_ref, bf16[4,1024,1024]{2,1,0:T(8,128)(2,1)S(1)} %turn.1.refs_0_, ...), custom_call_target="tpu_custom_call", output_to_operand_aliasing={{1}: (4, {})} | custom-call | tf_op jit(solution)/shard_map/stage/pallas_call | solution.py:159
  127.4 2.4 %stage.29 = (bf16[2,32,1024]{2,1,0:T(8,128)(2,1)S(1)}, bf16[5,16,3,32,128]{4,3,2,1,0:T(8,128)(2,1)S(1)}) custom-call(s32[1]{0:T(128)} %bitcast.y_ref, bf16[2,32,1024]{2,1,0:T(8,128)(2,1)S(1)} %collective-permute-done.8.state_ref, bf16[4,1024,1024]{2,1,0:T(8,128)(2,1)S(1)} %turn.1.refs_0_, ...), custom_call_target="tpu_custom_call", output_to_operand_aliasing={{1}: (4, {})} | custom-call | tf_op jit(solution)/shard_map/stage/pallas_call | solution.py:159
  129.8 2.5 %collective-permute-start.11 = (bf16[2,32,1024]{2,1,0:T(8,128)(2,1)S(1)}, bf16[2,32,1024]{2,1,0:T(8,128)(2,1)S(1)}, u32[]{:S(2)}, u32[]{:S(2)}) collective-permute-start(bf16[2,32,1024]{2,1,0:T(8,128)(2,1)S(1)} %get-tuple-element.68), channel_id=1, source_target_pairs={{192,256},{193,257},{194,258},{195,259},{196,260},{197,261},{198,2... | collective-permute-start | bytes 393224 | tf_op jit(solution)/shard_map/ppermute | solution.py:239
  132.3 2.4 %stage.30 = (bf16[2,32,1024]{2,1,0:T(8,128)(2,1)S(1)}, bf16[5,16,3,32,128]{4,3,2,1,0:T(8,128)(2,1)S(1)}) custom-call(s32[1]{0:T(128)} %bitcast.y_ref, bf16[2,32,1024]{2,1,0:T(8,128)(2,1)S(1)} %collective-permute-done.7.state_ref, bf16[4,1024,1024]{2,1,0:T(8,128)(2,1)S(1)} %turn.1.refs_0_, ...), custom_call_target="tpu_custom_call", output_to_operand_aliasing={{1}: (4, {})} | custom-call | tf_op jit(solution)/shard_map/stage/pallas_call | solution.py:159
  136.1 2.4 %stage.31 = (bf16[2,32,1024]{2,1,0:T(8,128)(2,1)S(1)}, bf16[5,16,3,32,128]{4,3,2,1,0:T(8,128)(2,1)S(1)}) custom-call(s32[1]{0:T(128)} %bitcast.y_ref, bf16[2,32,1024]{2,1,0:T(8,128)(2,1)S(1)} %collective-permute-done.6.state_ref, bf16[4,1024,1024]{2,1,0:T(8,128)(2,1)S(1)} %turn.1.refs_0_, ...), custom_call_target="tpu_custom_call", output_to_operand_aliasing={{1}: (4, {})} | custom-call | tf_op jit(solution)/shard_map/stage/pallas_call | solution.py:159
  139.8 2.4 %stage.32 = (bf16[2,32,1024]{2,1,0:T(8,128)(2,1)S(1)}, bf16[5,16,3,32,128]{4,3,2,1,0:T(8,128)(2,1)S(1)}) custom-call(s32[1]{0:T(128)} %bitcast.y_ref, bf16[2,32,1024]{2,1,0:T(8,128)(2,1)S(1)} %collective-permute-done.11.state_ref, bf16[4,1024,1024]{2,1,0:T(8,128)(2,1)S(1)} %turn.1.refs_0_, ...), custom_call_target="tpu_custom_call", output_to_operand_aliasing={{1}: (4, {})} | custom-call | tf_op jit(solution)/shard_map/stage/pallas_call | solution.py:159
  142.8 2.4 %stage.33 = (bf16[2,32,1024]{2,1,0:T(8,128)(2,1)S(1)}, bf16[5,16,3,32,128]{4,3,2,1,0:T(8,128)(2,1)S(1)}) custom-call(s32[1]{0:T(128)} %bitcast.y_ref, bf16[2,32,1024]{2,1,0:T(8,128)(2,1)S(1)} %collective-permute-done.10.state_ref, bf16[4,1024,1024]{2,1,0:T(8,128)(2,1)S(1)} %turn.1.refs_0_, ...), custom_call_target="tpu_custom_call", output_to_operand_aliasing={{1}: (4, {})} | custom-call | tf_op jit(solution)/shard_map/stage/pallas_call | solution.py:159
  145.9 2.4 %stage.34 = (bf16[2,32,1024]{2,1,0:T(8,128)(2,1)S(1)}, bf16[5,16,3,32,128]{4,3,2,1,0:T(8,128)(2,1)S(1)}) custom-call(s32[1]{0:T(128)} %bitcast.y_ref, bf16[2,32,1024]{2,1,0:T(8,128)(2,1)S(1)} %collective-permute-done.9.state_ref, bf16[4,1024,1024]{2,1,0:T(8,128)(2,1)S(1)} %turn.1.refs_0_, ...), custom_call_target="tpu_custom_call", output_to_operand_aliasing={{1}: (4, {})} | custom-call | tf_op jit(solution)/shard_map/stage/pallas_call | solution.py:159
  149.0 2.4 %stage.35 = (bf16[2,32,1024]{2,1,0:T(8,128)(2,1)S(1)}, bf16[5,16,3,32,128]{4,3,2,1,0:T(8,128)(2,1)S(1)}) custom-call(s32[1]{0:T(128)} %bitcast.y_ref, bf16[2,32,1024]{2,1,0:T(8,128)(2,1)S(1)} %collective-permute-done.14.state_ref, bf16[4,1024,1024]{2,1,0:T(8,128)(2,1)S(1)} %turn.1.refs_0_, ...), custom_call_target="tpu_custom_call", output_to_operand_aliasing={{1}: (4, {})} | custom-call | tf_op jit(solution)/shard_map/stage/pallas_call | solution.py:159
  152.0 2.4 %stage.36 = (bf16[2,32,1024]{2,1,0:T(8,128)(2,1)S(1)}, bf16[5,16,3,32,128]{4,3,2,1,0:T(8,128)(2,1)S(1)}) custom-call(s32[1]{0:T(128)} %bitcast.y_ref, bf16[2,32,1024]{2,1,0:T(8,128)(2,1)S(1)} %collective-permute-done.13.state_ref, bf16[4,1024,1024]{2,1,0:T(8,128)(2,1)S(1)} %turn.1.refs_0_, ...), custom_call_target="tpu_custom_call", output_to_operand_aliasing={{1}: (4, {})} | custom-call | tf_op jit(solution)/shard_map/stage/pallas_call | solution.py:159
  155.1 2.4 %stage.37 = (bf16[2,32,1024]{2,1,0:T(8,128)(2,1)S(1)}, bf16[5,16,3,32,128]{4,3,2,1,0:T(8,128)(2,1)S(1)}) custom-call(s32[1]{0:T(128)} %bitcast.y_ref, bf16[2,32,1024]{2,1,0:T(8,128)(2,1)S(1)} %collective-permute-done.12.state_ref, bf16[4,1024,1024]{2,1,0:T(8,128)(2,1)S(1)} %turn.1.refs_0_, ...), custom_call_target="tpu_custom_call", output_to_operand_aliasing={{1}: (4, {})} | custom-call | tf_op jit(solution)/shard_map/stage/pallas_call | solution.py:159
  158.2 2.4 %stage.38 = (bf16[2,32,1024]{2,1,0:T(8,128)(2,1)S(1)}, bf16[5,16,3,32,128]{4,3,2,1,0:T(8,128)(2,1)S(1)}) custom-call(s32[1]{0:T(128)} %bitcast.y_ref, bf16[2,32,1024]{2,1,0:T(8,128)(2,1)S(1)} %collective-permute-done.17.state_ref, bf16[4,1024,1024]{2,1,0:T(8,128)(2,1)S(1)} %turn.1.refs_0_, ...), custom_call_target="tpu_custom_call", output_to_operand_aliasing={{1}: (4, {})} | custom-call | tf_op jit(solution)/shard_map/stage/pallas_call | solution.py:159
  161.2 2.4 %stage.39 = (bf16[2,32,1024]{2,1,0:T(8,128)(2,1)S(1)}, bf16[5,16,3,32,128]{4,3,2,1,0:T(8,128)(2,1)S(1)}) custom-call(s32[1]{0:T(128)} %bitcast.y_ref, bf16[2,32,1024]{2,1,0:T(8,128)(2,1)S(1)} %collective-permute-done.16.state_ref, bf16[4,1024,1024]{2,1,0:T(8,128)(2,1)S(1)} %turn.1.refs_0_, ...), custom_call_target="tpu_custom_call", output_to_operand_aliasing={{1}: (4, {})} | custom-call | tf_op jit(solution)/shard_map/stage/pallas_call | solution.py:159
  164.3 2.4 %stage.40 = (bf16[2,32,1024]{2,1,0:T(8,128)(2,1)S(1)}, bf16[5,16,3,32,128]{4,3,2,1,0:T(8,128)(2,1)S(1)}) custom-call(s32[1]{0:T(128)} %bitcast.y_ref, bf16[2,32,1024]{2,1,0:T(8,128)(2,1)S(1)} %collective-permute-done.15.state_ref, bf16[4,1024,1024]{2,1,0:T(8,128)(2,1)S(1)} %turn.1.refs_0_, ...), custom_call_target="tpu_custom_call", output_to_operand_aliasing={{1}: (4, {})} | custom-call | tf_op jit(solution)/shard_map/stage/pallas_call | solution.py:159
  167.5 3.0 %stage.41 = (bf16[2,32,1024]{2,1,0:T(8,128)(2,1)}, bf16[5,16,3,32,128]{4,3,2,1,0:T(8,128)(2,1)S(1)}) custom-call(s32[1]{0:T(128)} %bitcast.y_ref, bf16[2,32,1024]{2,1,0:T(8,128)(2,1)S(1)} %collective-permute-done.20.state_ref, bf16[4,1024,1024]{2,1,0:T(8,128)(2,1)S(1)} %turn.1.refs_0_, ...), custom_call_target="tpu_custom_call", output_to_operand_aliasing={{1}: (4, {})} | custom-call | tf_op jit(solution)/shard_map/stage/pallas_call | solution.py:159
  170.5 3.0 %stage.42 = (bf16[2,32,1024]{2,1,0:T(8,128)(2,1)}, bf16[5,16,3,32,128]{4,3,2,1,0:T(8,128)(2,1)S(1)}) custom-call(s32[1]{0:T(128)} %bitcast.y_ref, bf16[2,32,1024]{2,1,0:T(8,128)(2,1)S(1)} %collective-permute-done.19.state_ref, bf16[4,1024,1024]{2,1,0:T(8,128)(2,1)S(1)} %turn.1.refs_0_, ...), custom_call_target="tpu_custom_call", output_to_operand_aliasing={{1}: (4, {})} | custom-call | tf_op jit(solution)/shard_map/stage/pallas_call | solution.py:159
  173.5 3.0 %stage.43 = (bf16[2,32,1024]{2,1,0:T(8,128)(2,1)}, bf16[5,16,3,32,128]{4,3,2,1,0:T(8,128)(2,1)S(1)}) custom-call(s32[1]{0:T(128)} %bitcast.y_ref, bf16[2,32,1024]{2,1,0:T(8,128)(2,1)S(1)} %collective-permute-done.18.state_ref, bf16[4,1024,1024]{2,1,0:T(8,128)(2,1)S(1)} %turn.1.refs_0_, ...), custom_call_target="tpu_custom_call", output_to_operand_aliasing={{1}: (4, {})} | custom-call | tf_op jit(solution)/shard_map/stage/pallas_call | solution.py:159
  176.8 47.6 %all_to_all.10 = bf16[64,96,128]{2,1,0:T(8,128)(2,1)S(1)} all-to-all(bf16[64,96,128]{2,1,0:T(8,128)(2,1)S(1)} %bitcast.21), channel_id=1, replica_groups=mesh['y'=8,'x'=4,'z'=8,'core'=2] {'x','z','core'}, dimensions={0} | all-to-all | bytes 3145728 | tf_op jit(solution)/shard_map/all_to_all | solution.py:241
  224.4 2.1 finish.1
  (62 shorter events, 23.2 us)
Async XLA Ops:
  6.5 86.3 %all-gather.4.cloned.1.call-start = ((), (), s32[]{:S(2)}) async-start(), calls=%async_computation.2 | async-start | bytes 8912896 | tf_op jit(solution)/shard_map/all_gather | solution.py:222
  19.1 18.7 %copy-start.2 = (f32[6]{0:T(128)S(1)}, f32[6]{0:T(128)}, u32[]{:S(2)}) copy-start(f32[6]{0:T(128)} %param.5) | copy-start | bytes 76
  23.2 33.7 %all-to-all-start = ((bf16[16,112,128]{2,1,0:T(8,128)(2,1)}), bf16[16,112,128]{2,1,0:T(8,128)(2,1)S(1)}, u32[]{:S(2)}, u32[]{:S(2)}) async-start(bf16[16,112,128]{2,1,0:T(8,128)(2,1)} %bitcast.24), calls=%async_computation | async-start | bytes 917504 | tf_op jit(solution)/shard_map/all_to_all | solution.py:228
  56.9 0.8 copy-start.1
  92.8 1.0 copy-start
  99.9 7.2 %collective-permute-start.2 = (bf16[2,32,1024]{2,1,0:T(8,128)(2,1)S(1)}, bf16[2,32,1024]{2,1,0:T(8,128)(2,1)S(1)}, u32[]{:S(2)}, u32[]{:S(2)}) collective-permute-start(bf16[2,32,1024]{2,1,0:T(8,128)(2,1)S(1)} %get-tuple-element.50), channel_id=1, source_target_pairs={{0,64},{1,65},{2,66},{3,67},{4,68},{5,69},{6,70},{7,71},{8,72},{9,... | collective-permute-start | bytes 393224 | tf_op jit(solution)/shard_map/ppermute | solution.py:239
  100.6 9.6 %collective-permute-start.1 = (bf16[2,32,1024]{2,1,0:T(8,128)(2,1)S(1)}, bf16[2,32,1024]{2,1,0:T(8,128)(2,1)S(1)}, u32[]{:S(2)}, u32[]{:S(2)}) collective-permute-start(bf16[2,32,1024]{2,1,0:T(8,128)(2,1)S(1)} %get-tuple-element.49), channel_id=1, source_target_pairs={{0,64},{1,65},{2,66},{3,67},{4,68},{5,69},{6,70},{7,71},{8,72},{9,... | collective-permute-start | bytes 393224 | tf_op jit(solution)/shard_map/ppermute | solution.py:239
  101.2 12.0 %collective-permute-start = (bf16[2,32,1024]{2,1,0:T(8,128)(2,1)S(1)}, bf16[2,32,1024]{2,1,0:T(8,128)(2,1)S(1)}, u32[]{:S(2)}, u32[]{:S(2)}) collective-permute-start(bf16[2,32,1024]{2,1,0:T(8,128)(2,1)S(1)} %get-tuple-element.48), channel_id=1, source_target_pairs={{0,64},{1,65},{2,66},{3,67},{4,68},{5,69},{6,70},{7,71},{8,72},{9,... | collective-permute-start | bytes 393224 | tf_op jit(solution)/shard_map/ppermute | solution.py:239
  109.5 6.8 %collective-permute-start.5 = (bf16[2,32,1024]{2,1,0:T(8,128)(2,1)S(1)}, bf16[2,32,1024]{2,1,0:T(8,128)(2,1)S(1)}, u32[]{:S(2)}, u32[]{:S(2)}) collective-permute-start(bf16[2,32,1024]{2,1,0:T(8,128)(2,1)S(1)} %get-tuple-element.56), channel_id=1, source_target_pairs={{64,128},{65,129},{66,130},{67,131},{68,132},{69,133},{70,134},{71... | collective-permute-start | bytes 393224 | tf_op jit(solution)/shard_map/ppermute | solution.py:239
  112.6 7.4 %collective-permute-start.4 = (bf16[2,32,1024]{2,1,0:T(8,128)(2,1)S(1)}, bf16[2,32,1024]{2,1,0:T(8,128)(2,1)S(1)}, u32[]{:S(2)}, u32[]{:S(2)}) collective-permute-start(bf16[2,32,1024]{2,1,0:T(8,128)(2,1)S(1)} %get-tuple-element.55), channel_id=1, source_target_pairs={{64,128},{65,129},{66,130},{67,131},{68,132},{69,133},{70,134},{71... | collective-permute-start | bytes 393224 | tf_op jit(solution)/shard_map/ppermute | solution.py:239
  115.6 8.1 %collective-permute-start.3 = (bf16[2,32,1024]{2,1,0:T(8,128)(2,1)S(1)}, bf16[2,32,1024]{2,1,0:T(8,128)(2,1)S(1)}, u32[]{:S(2)}, u32[]{:S(2)}) collective-permute-start(bf16[2,32,1024]{2,1,0:T(8,128)(2,1)S(1)} %get-tuple-element.54), channel_id=1, source_target_pairs={{64,128},{65,129},{66,130},{67,131},{68,132},{69,133},{70,134},{71... | collective-permute-start | bytes 393224 | tf_op jit(solution)/shard_map/ppermute | solution.py:239
  118.7 8.7 %collective-permute-start.8 = (bf16[2,32,1024]{2,1,0:T(8,128)(2,1)S(1)}, bf16[2,32,1024]{2,1,0:T(8,128)(2,1)S(1)}, u32[]{:S(2)}, u32[]{:S(2)}) collective-permute-start(bf16[2,32,1024]{2,1,0:T(8,128)(2,1)S(1)} %get-tuple-element.62), channel_id=1, source_target_pairs={{128,192},{129,193},{130,194},{131,195},{132,196},{133,197},{134,1... | collective-permute-start | bytes 393224 | tf_op jit(solution)/shard_map/ppermute | solution.py:239
  122.4 9.9 %collective-permute-start.7 = (bf16[2,32,1024]{2,1,0:T(8,128)(2,1)S(1)}, bf16[2,32,1024]{2,1,0:T(8,128)(2,1)S(1)}, u32[]{:S(2)}, u32[]{:S(2)}) collective-permute-start(bf16[2,32,1024]{2,1,0:T(8,128)(2,1)S(1)} %get-tuple-element.61), channel_id=1, source_target_pairs={{128,192},{129,193},{130,194},{131,195},{132,196},{133,197},{134,1... | collective-permute-start | bytes 393224 | tf_op jit(solution)/shard_map/ppermute | solution.py:239
  126.1 10.0 %collective-permute-start.6 = (bf16[2,32,1024]{2,1,0:T(8,128)(2,1)S(1)}, bf16[2,32,1024]{2,1,0:T(8,128)(2,1)S(1)}, u32[]{:S(2)}, u32[]{:S(2)}) collective-permute-start(bf16[2,32,1024]{2,1,0:T(8,128)(2,1)S(1)} %get-tuple-element.60), channel_id=1, source_target_pairs={{128,192},{129,193},{130,194},{131,195},{132,196},{133,197},{134,1... | collective-permute-start | bytes 393224 | tf_op jit(solution)/shard_map/ppermute | solution.py:239
  129.8 10.0 %collective-permute-start.11 = (bf16[2,32,1024]{2,1,0:T(8,128)(2,1)S(1)}, bf16[2,32,1024]{2,1,0:T(8,128)(2,1)S(1)}, u32[]{:S(2)}, u32[]{:S(2)}) collective-permute-start(bf16[2,32,1024]{2,1,0:T(8,128)(2,1)S(1)} %get-tuple-element.68), channel_id=1, source_target_pairs={{192,256},{193,257},{194,258},{195,259},{196,260},{197,261},{198,2... | collective-permute-start | bytes 393224 | tf_op jit(solution)/shard_map/ppermute | solution.py:239
  134.7 8.1 %collective-permute-start.10 = (bf16[2,32,1024]{2,1,0:T(8,128)(2,1)S(1)}, bf16[2,32,1024]{2,1,0:T(8,128)(2,1)S(1)}, u32[]{:S(2)}, u32[]{:S(2)}) collective-permute-start(bf16[2,32,1024]{2,1,0:T(8,128)(2,1)S(1)} %get-tuple-element.67), channel_id=1, source_target_pairs={{192,256},{193,257},{194,258},{195,259},{196,260},{197,261},{198,2... | collective-permute-start | bytes 393224 | tf_op jit(solution)/shard_map/ppermute | solution.py:239
  138.5 7.4 %collective-permute-start.9 = (bf16[2,32,1024]{2,1,0:T(8,128)(2,1)S(1)}, bf16[2,32,1024]{2,1,0:T(8,128)(2,1)S(1)}, u32[]{:S(2)}, u32[]{:S(2)}) collective-permute-start(bf16[2,32,1024]{2,1,0:T(8,128)(2,1)S(1)} %get-tuple-element.66), channel_id=1, source_target_pairs={{192,256},{193,257},{194,258},{195,259},{196,260},{197,261},{198,2... | collective-permute-start | bytes 393224 | tf_op jit(solution)/shard_map/ppermute | solution.py:239
  142.2 6.8 %collective-permute-start.14 = (bf16[2,32,1024]{2,1,0:T(8,128)(2,1)S(1)}, bf16[2,32,1024]{2,1,0:T(8,128)(2,1)S(1)}, u32[]{:S(2)}, u32[]{:S(2)}) collective-permute-start(bf16[2,32,1024]{2,1,0:T(8,128)(2,1)S(1)} %get-tuple-element.74), channel_id=1, source_target_pairs={{256,320},{257,321},{258,322},{259,323},{260,324},{261,325},{262,3... | collective-permute-start | bytes 393224 | tf_op jit(solution)/shard_map/ppermute | solution.py:239
  145.2 6.8 %collective-permute-start.13 = (bf16[2,32,1024]{2,1,0:T(8,128)(2,1)S(1)}, bf16[2,32,1024]{2,1,0:T(8,128)(2,1)S(1)}, u32[]{:S(2)}, u32[]{:S(2)}) collective-permute-start(bf16[2,32,1024]{2,1,0:T(8,128)(2,1)S(1)} %get-tuple-element.73), channel_id=1, source_target_pairs={{256,320},{257,321},{258,322},{259,323},{260,324},{261,325},{262,3... | collective-permute-start | bytes 393224 | tf_op jit(solution)/shard_map/ppermute | solution.py:239
  148.3 6.8 %collective-permute-start.12 = (bf16[2,32,1024]{2,1,0:T(8,128)(2,1)S(1)}, bf16[2,32,1024]{2,1,0:T(8,128)(2,1)S(1)}, u32[]{:S(2)}, u32[]{:S(2)}) collective-permute-start(bf16[2,32,1024]{2,1,0:T(8,128)(2,1)S(1)} %get-tuple-element.72), channel_id=1, source_target_pairs={{256,320},{257,321},{258,322},{259,323},{260,324},{261,325},{262,3... | collective-permute-start | bytes 393224 | tf_op jit(solution)/shard_map/ppermute | solution.py:239
  151.3 6.8 %collective-permute-start.17 = (bf16[2,32,1024]{2,1,0:T(8,128)(2,1)S(1)}, bf16[2,32,1024]{2,1,0:T(8,128)(2,1)S(1)}, u32[]{:S(2)}, u32[]{:S(2)}) collective-permute-start(bf16[2,32,1024]{2,1,0:T(8,128)(2,1)S(1)} %get-tuple-element.80), channel_id=1, source_target_pairs={{320,384},{321,385},{322,386},{323,387},{324,388},{325,389},{326,3... | collective-permute-start | bytes 393224 | tf_op jit(solution)/shard_map/ppermute | solution.py:239
  154.4 6.8 %collective-permute-start.16 = (bf16[2,32,1024]{2,1,0:T(8,128)(2,1)S(1)}, bf16[2,32,1024]{2,1,0:T(8,128)(2,1)S(1)}, u32[]{:S(2)}, u32[]{:S(2)}) collective-permute-start(bf16[2,32,1024]{2,1,0:T(8,128)(2,1)S(1)} %get-tuple-element.79), channel_id=1, source_target_pairs={{320,384},{321,385},{322,386},{323,387},{324,388},{325,389},{326,3... | collective-permute-start | bytes 393224 | tf_op jit(solution)/shard_map/ppermute | solution.py:239
  157.5 6.8 %collective-permute-start.15 = (bf16[2,32,1024]{2,1,0:T(8,128)(2,1)S(1)}, bf16[2,32,1024]{2,1,0:T(8,128)(2,1)S(1)}, u32[]{:S(2)}, u32[]{:S(2)}) collective-permute-start(bf16[2,32,1024]{2,1,0:T(8,128)(2,1)S(1)} %get-tuple-element.78), channel_id=1, source_target_pairs={{320,384},{321,385},{322,386},{323,387},{324,388},{325,389},{326,3... | collective-permute-start | bytes 393224 | tf_op jit(solution)/shard_map/ppermute | solution.py:239
  160.5 7.0 %collective-permute-start.20 = (bf16[2,32,1024]{2,1,0:T(8,128)(2,1)S(1)}, bf16[2,32,1024]{2,1,0:T(8,128)(2,1)S(1)}, u32[]{:S(2)}, u32[]{:S(2)}) collective-permute-start(bf16[2,32,1024]{2,1,0:T(8,128)(2,1)S(1)} %get-tuple-element.86), channel_id=1, source_target_pairs={{384,448},{385,449},{386,450},{387,451},{388,452},{389,453},{390,4... | collective-permute-start | bytes 393224 | tf_op jit(solution)/shard_map/ppermute | solution.py:239
  163.6 6.9 %collective-permute-start.19 = (bf16[2,32,1024]{2,1,0:T(8,128)(2,1)S(1)}, bf16[2,32,1024]{2,1,0:T(8,128)(2,1)S(1)}, u32[]{:S(2)}, u32[]{:S(2)}) collective-permute-start(bf16[2,32,1024]{2,1,0:T(8,128)(2,1)S(1)} %get-tuple-element.85), channel_id=1, source_target_pairs={{384,448},{385,449},{386,450},{387,451},{388,452},{389,453},{390,4... | collective-permute-start | bytes 393224 | tf_op jit(solution)/shard_map/ppermute | solution.py:239
  166.7 6.8 %collective-permute-start.18 = (bf16[2,32,1024]{2,1,0:T(8,128)(2,1)S(1)}, bf16[2,32,1024]{2,1,0:T(8,128)(2,1)S(1)}, u32[]{:S(2)}, u32[]{:S(2)}) collective-permute-start(bf16[2,32,1024]{2,1,0:T(8,128)(2,1)S(1)} %get-tuple-element.84), channel_id=1, source_target_pairs={{384,448},{385,449},{386,450},{387,451},{388,452},{389,453},{390,4... | collective-permute-start | bytes 393224 | tf_op jit(solution)/shard_map/ppermute | solution.py:239
Sparse Core Ops, SparseCore 0:
  18.5 74.2 all-gather.3

commit v7 on v6

--- a/solution.py
+++ b/solution.py
@@ -92,56 +92,57 @@
     )(basis, basis, basis, basis)
 
 
-def stage_kernel(pieces, parts, y_ref, state_ref, *refs):
+def stage_kernel(step, pieces, parts, y_ref, state_ref, *refs):
     basis_refs, coef_ref = refs[:pieces], refs[pieces]
     next_refs, (out_ref, now, rot) = refs[-3 - parts : -3], refs[-3:]
-    del y_ref
     s = pl.program_id(0)
     energies = coef_ref.shape[3]
     rows, channels = state_ref.shape[1:]
     own = rows // parts
     per = own // energies
 
-    @pl.when(s == 0)
+    @pl.when(y_ref[0] == step)
     def _():
-        now[pl.ds(0, rows)] = state_ref[0]
-        now[pl.ds(rows, rows)] = state_ref[1]
-
-    for k in range(parts * energies):
-        part, e = divmod(k, energies)
-        cosine = coef_ref[part, 0, 0, pl.ds(e, 1), :]
-        ratio = coef_ref[part, 0, 1, pl.ds(e, 1), :]
-        product = coef_ref[part, 0, 2, pl.ds(e, 1), :]
-        values = now[pl.ds(per * k, per), :].astype(jnp.float32)
-        slopes = now[pl.ds(rows + per * k, per), :].astype(jnp.float32)
-        rot[pl.ds(per * k, per), :] = (cosine * values + ratio * slopes).astype(rot.dtype)
-        rot[pl.ds(rows + per * k, per), :] = (cosine * slopes - product * values).astype(rot.dtype)
-    low = lax.broadcasted_iota(jnp.int32, (rows, 128), 1) < 64
-    width = channels // pieces
-    for q, basis_ref in enumerate(basis_refs):
-        if pieces == 1:
-            fresh = jnp.dot(rot[...], basis_ref[0], preferred_element_type=jnp.float32)
-        else:
-            block = basis_ref[...].reshape(width, channels)
-            fresh = lax.dot_general(
-                rot[...], block, (((1,), (1,)), ((), ())), preferred_element_type=jnp.float32
-            )
-        now[:, pl.ds(width * q, width)] = fresh.astype(now.dtype)
-        for k in range(width // 128):
-            z = width // 128 * q + k
-            lanes = slice(128 * k, 128 * k + 128)
-            values = fresh[:rows, lanes]
-            slopes = fresh[rows:, lanes]
-            one = jnp.where(low, values, pltpu.roll(slopes, 64, 1)).astype(out_ref.dtype)
-            two = jnp.where(low, pltpu.roll(values, 64, 1), slopes).astype(out_ref.dtype)
-            out_ref[0, 2 * z] = one.reshape(parts, own, 128)
-            out_ref[0, 2 * z + 1] = two.reshape(parts, own, 128)
-
-    @pl.when(s == pl.num_programs(0) - 1)
-    def _():
-        for part, next_ref in enumerate(next_refs):
-            next_ref[0] = now[pl.ds(own * part, own)]
-            next_ref[1] = now[pl.ds(rows + own * part, own)]
+        @pl.when(s == 0)
+        def _():
+            now[pl.ds(0, rows)] = state_ref[0]
+            now[pl.ds(rows, rows)] = state_ref[1]
+
+        for k in range(parts * energies):
+            part, e = divmod(k, energies)
+            cosine = coef_ref[part, 0, 0, pl.ds(e, 1), :]
+            ratio = coef_ref[part, 0, 1, pl.ds(e, 1), :]
+            product = coef_ref[part, 0, 2, pl.ds(e, 1), :]
+            values = now[pl.ds(per * k, per), :].astype(jnp.float32)
+            slopes = now[pl.ds(rows + per * k, per), :].astype(jnp.float32)
+            rot[pl.ds(per * k, per), :] = (cosine * values + ratio * slopes).astype(rot.dtype)
+            rot[pl.ds(rows + per * k, per), :] = (cosine * slopes - product * values).astype(rot.dtype)
+        low = lax.broadcasted_iota(jnp.int32, (rows, 128), 1) < 64
+        width = channels // pieces
+        for q, basis_ref in enumerate(basis_refs):
+            if pieces == 1:
+                fresh = jnp.dot(rot[...], basis_ref[0], preferred_element_type=jnp.float32)
+            else:
+                block = basis_ref[...].reshape(width, channels)
+                fresh = lax.dot_general(
+                    rot[...], block, (((1,), (1,)), ((), ())), preferred_element_type=jnp.float32
+                )
+            now[:, pl.ds(width * q, width)] = fresh.astype(now.dtype)
+            for k in range(width // 128):
+                z = width // 128 * q + k
+                lanes = slice(128 * k, 128 * k + 128)
+                values = fresh[:rows, lanes]
+                slopes = fresh[rows:, lanes]
+                one = jnp.where(low, values, pltpu.roll(slopes, 64, 1)).astype(out_ref.dtype)
+                two = jnp.where(low, pltpu.roll(values, 64, 1), slopes).astype(out_ref.dtype)
+                out_ref[0, 2 * z] = one.reshape(parts, own, 128)
+                out_ref[0, 2 * z + 1] = two.reshape(parts, own, 128)
+
+        @pl.when(s == pl.num_programs(0) - 1)
+        def _():
+            for part, next_ref in enumerate(next_refs):
+                next_ref[0] = now[pl.ds(own * part, own)]
+                next_ref[1] = now[pl.ds(rows + own * part, own)]
 
 
 def stage(step, part, y_index, state, basis, coefs, kept):
@@ -155,9 +156,13 @@
         block = (groups // pieces, 1, share, channels)
         basis_specs = [pl.BlockSpec(block, lambda s, y, q=q: (q, s, 0, 0)) for q in range(pieces)]
     else:
-        basis_specs = [pl.BlockSpec((1, channels, channels), lambda s, y: (s, 0, 0))]
+        basis_specs = [
+            pl.BlockSpec(
+                (1, channels, channels), lambda s, y: (jnp.where(y[0] == step, s, 0), 0, 0)
+            )
+        ]
     outs = pl.pallas_call(
-        functools.partial(stage_kernel, pieces, parts),
+        functools.partial(stage_kernel, step, pieces, parts),
         grid_spec=pltpu.PrefetchScalarGridSpec(
             num_scalar_prefetch=1,
             grid=(sectors,),

time: 234 us -> 223 us (0.953)
  the two profiles are of different devices: /device:TPU:31 before, /device:TPU:63 now
where the time goes in v7:
time: 223 us; the launch traced here: 222 us
  waiting for transfers between devices  81.4 us (37%)
  blocking collectives  60.7 us (27%)
  starting transfers between devices  30.7 us (14%)
  Pallas kernels  28.6 us (13%)
  between operations  13.9 us (6%)
  local copies, waits for them, and re-layouts  3.68 us (2%)
  other arithmetic  2.74 us (1%)
    all_to_all x1, blocking collectives, per_device(): back = lax.all_to_all(kept[:4].reshape(64, rows, lanes), PLANE, 0, 0)  50.7 us
    all_gather x1, waiting for transfers between devices, per_device(): basis = lax.all_gather(ring[:, :share], CH_AXES)  31 us
    ppermute x21, waiting for transfers between devices, per_device(): state = lax.ppermute(states[part], 'y', [(step - 1, step)])  31 us
    all_to_all x1, waiting for transfers between devices, per_device(): lax.all_to_all(blocks.reshape(16, rows + per, lanes), CH_AXES, 0, 0)  19.4 us
    ppermute x21, starting transfers between devices, per_device(): state = lax.ppermute(states[part], 'y', [(step - 1, step)])  16.1 us
    pallas_call x22, Pallas kernels, stage(): pl.pallas_call(functools.partial(stage_kernel, step, pieces, parts), grid...  15.3 us
    all_to_all x1, starting transfers between devices, per_device(): lax.all_to_all(blocks.reshape(16, rows + per, lanes), CH_AXES, 0, 0)  14.6 us
    all_gather x1, blocking collectives, per_device(): ring = lax.all_gather(jnp.concatenate([intersection[0], extra]), 'x')  10 us
  transfers between devices with their start and end apart: 23, of which 5 were waited for; matrix products, arithmetic and copies ran while one was open for 1% of the time, Pallas kernels for 9%

profile of v7, /device:TPU:63, one launch (start us, length us, event | category | flops | bytes accessed | tf_op | source)
XLA Modules:
  0.0 221.7 jit_solution(16506249069693875098)
XLA Ops:
  6.5 0.9 fusion.1
  7.5 10.0 %all-gather = bf16[288,1024]{1,0:T(8,128)(2,1)S(1)} all-gather(bf16[72,1024]{1,0:T(8,128)(2,1)S(1)} %fusion.1), channel_id=2, replica_groups=mesh['y'=8,'x'=4,'z'=8,'core'=2] {'x'}, dimensions={0}, use_global_device_ids=true | all-gather | bytes 737280 | tf_op jit(solution)/shard_map/all_gather | solution.py:226
  17.5 0.8 slice.17
  19.1 4.1 %spread.1 = bf16[16,7,16,128]{3,2,1,0:T(8,128)(2,1)} custom-call(s32[1]{0:T(128)} %bitcast.1.x_ref, bf16[6,64,2048]{2,1,0:T(8,128)(2,1)} %p_ref.1, bf16[6,64,2048]{2,1,0:T(8,128)(2,1)} %p_ref.1, bf16[16,128]{1,0:T(8,128)(2,1)} %pad.9.limit_ref), custom_call_target="tpu_custom_call" | custom-call | tf_op jit(solution)/shard_map/spread/pallas_call | solution.py:36
  23.2 14.6 %all-to-all-start = ((bf16[16,112,128]{2,1,0:T(8,128)(2,1)}), bf16[16,112,128]{2,1,0:T(8,128)(2,1)S(1)}, u32[]{:S(2)}, u32[]{:S(2)}) async-start(bf16[16,112,128]{2,1,0:T(8,128)(2,1)} %bitcast.24), calls=%async_computation | async-start | bytes 917504 | tf_op jit(solution)/shard_map/all_to_all | solution.py:233
  37.8 19.4 %all-to-all-done.in_ref = bf16[16,112,128]{2,1,0:T(8,128)(2,1)S(1)} async-done(((bf16[16,112,128]{2,1,0:T(8,128)(2,1)}), bf16[16,112,128]{2,1,0:T(8,128)(2,1)S(1)}, u32[]{:S(2)}, u32[]{:S(2)}) %all-to-all-start) | async-done | bytes 458784 | tf_op jit(solution)/shard_map/all_to_all | solution.py:233
  58.0 2.0 join.1.state_ref
  60.0 1.7 fusion.5
  61.8 31.0 %all-gather.4.cloned.1.call-done = bf16[64,64,1024]{2,1,0:T(8,128)(2,1)} async-done(((bf16[4,64,1024]{2,1,0:T(8,128)(2,1)}), bf16[64,64,1024]{2,1,0:T(8,128)(2,1)}) %all-gather.4.cloned.1.call-update) | async-done | bytes 8388624 | tf_op jit(solution)/shard_map/all_gather | solution.py:227
  92.8 1.0 copy-done
  93.8 3.8 %stage.22 = (bf16[2,32,1024]{2,1,0:T(8,128)(2,1)S(1)}, bf16[2,32,1024]{2,1,0:T(8,128)(2,1)S(1)}, bf16[2,32,1024]{2,1,0:T(8,128)(2,1)S(1)}, bf16[5,16,3,32,128]{4,3,2,1,0:T(8,128)(2,1)S(1)}) custom-call(s32[1]{0:T(128)} %bitcast.y_ref, bf16[2,96,1024]{2,1,0:T(8,128)(2,1)S(1)} %copy-done, bf16[16,4,64,1024]{3,2,1,0:T(8,128)(2,1)} %bitcast.13, ...), custom_call_target="tpu_custom_call" | custom-call | tf_op jit(solution)/shard_map/stage/pallas_call | solution.py:164
  98.3 0.7 collective-permute-start.1
  99.0 0.7 collective-permute-start
  99.6 5.2 %turn.1.refs_0_ = bf16[4,1024,1024]{2,1,0:T(8,128)(2,1)S(1)} custom-call(bf16[16,4,64,1024]{3,2,1,0:T(8,128)(2,1)} %bitcast.17, bf16[16,4,64,1024]{3,2,1,0:T(8,128)(2,1)} %bitcast.18, bf16[16,4,64,1024]{3,2,1,0:T(8,128)(2,1)} %bitcast.19, bf16[16,4,64,1024]{3,2,1,0:T(8,128)(2,1)} %bitcast.20), custom_call_target="tpu_custom_call" | custom-call | tf_op jit(solution)/shard_map/turn/pallas_call | solution.py:84
  105.0 0.7 collective-permute-start.5
  105.8 0.7 collective-permute-start.4
  106.6 0.7 collective-permute-start.3
  108.3 0.7 collective-permute-start.7
  110.8 0.7 collective-permute-start.10
  112.4 0.7 collective-permute-start.14
  114.9 0.7 collective-permute-start.17
  117.4 1.3 collective-permute-start.20
  118.9 1.5 collective-permute-start.19
  120.5 1.3 collective-permute-start.18
  121.8 26.9 %collective-permute-done.20.state_ref = bf16[2,32,1024]{2,1,0:T(8,128)(2,1)S(1)} collective-permute-done((bf16[2,32,1024]{2,1,0:T(8,128)(2,1)S(1)}, bf16[2,32,1024]{2,1,0:T(8,128)(2,1)S(1)}, u32[]{:S(2)}, u32[]{:S(2)}) %collective-permute-start.20) | collective-permute-done | bytes 131104 | tf_op jit(solution)/shard_map/ppermute | solution.py:244
  148.7 3.0 %stage.41 = (bf16[2,32,1024]{2,1,0:T(8,128)(2,1)}, bf16[5,16,3,32,128]{4,3,2,1,0:T(8,128)(2,1)S(1)}) custom-call(s32[1]{0:T(128)} %bitcast.y_ref, bf16[2,32,1024]{2,1,0:T(8,128)(2,1)S(1)} %collective-permute-done.20.state_ref, bf16[4,1024,1024]{2,1,0:T(8,128)(2,1)S(1)} %turn.1.refs_0_, ...), custom_call_target="tpu_custom_call", output_to_operand_aliasing={{1}: (4, {})} | custom-call | tf_op jit(solution)/shard_map/stage/pallas_call | solution.py:164
  151.8 3.0 %collective-permute-done.19.state_ref = bf16[2,32,1024]{2,1,0:T(8,128)(2,1)S(1)} collective-permute-done((bf16[2,32,1024]{2,1,0:T(8,128)(2,1)S(1)}, bf16[2,32,1024]{2,1,0:T(8,128)(2,1)S(1)}, u32[]{:S(2)}, u32[]{:S(2)}) %collective-permute-start.19) | collective-permute-done | bytes 131104 | tf_op jit(solution)/shard_map/ppermute | solution.py:244
  154.8 3.0 %stage.42 = (bf16[2,32,1024]{2,1,0:T(8,128)(2,1)}, bf16[5,16,3,32,128]{4,3,2,1,0:T(8,128)(2,1)S(1)}) custom-call(s32[1]{0:T(128)} %bitcast.y_ref, bf16[2,32,1024]{2,1,0:T(8,128)(2,1)S(1)} %collective-permute-done.19.state_ref, bf16[4,1024,1024]{2,1,0:T(8,128)(2,1)S(1)} %turn.1.refs_0_, ...), custom_call_target="tpu_custom_call", output_to_operand_aliasing={{1}: (4, {})} | custom-call | tf_op jit(solution)/shard_map/stage/pallas_call | solution.py:164
  157.8 1.0 collective-permute-done.18.state_ref
  158.8 3.0 %stage.43 = (bf16[2,32,1024]{2,1,0:T(8,128)(2,1)}, bf16[5,16,3,32,128]{4,3,2,1,0:T(8,128)(2,1)S(1)}) custom-call(s32[1]{0:T(128)} %bitcast.y_ref, bf16[2,32,1024]{2,1,0:T(8,128)(2,1)S(1)} %collective-permute-done.18.state_ref, bf16[4,1024,1024]{2,1,0:T(8,128)(2,1)S(1)} %turn.1.refs_0_, ...), custom_call_target="tpu_custom_call", output_to_operand_aliasing={{1}: (4, {})} | custom-call | tf_op jit(solution)/shard_map/stage/pallas_call | solution.py:164
  162.1 50.7 %all_to_all.10 = bf16[64,96,128]{2,1,0:T(8,128)(2,1)S(1)} all-to-all(bf16[64,96,128]{2,1,0:T(8,128)(2,1)S(1)} %bitcast.21), channel_id=1, replica_groups=mesh['y'=8,'x'=4,'z'=8,'core'=2] {'x','z','core'}, dimensions={0} | all-to-all | bytes 3145728 | tf_op jit(solution)/shard_map/all_to_all | solution.py:246
  212.8 2.1 finish.1
  (62 shorter events, 10.5 us)
Async XLA Ops:
  6.5 86.3 %all-gather.4.cloned.1.call-start = ((), (), s32[]{:S(2)}) async-start(), calls=%async_computation.2 | async-start | bytes 8912896 | tf_op jit(solution)/shard_map/all_gather | solution.py:227
  19.1 18.7 %copy-start.2 = (f32[6]{0:T(128)S(1)}, f32[6]{0:T(128)}, u32[]{:S(2)}) copy-start(f32[6]{0:T(128)} %param.5) | copy-start | bytes 76
  23.2 34.0 %all-to-all-start = ((bf16[16,112,128]{2,1,0:T(8,128)(2,1)}), bf16[16,112,128]{2,1,0:T(8,128)(2,1)S(1)}, u32[]{:S(2)}, u32[]{:S(2)}) async-start(bf16[16,112,128]{2,1,0:T(8,128)(2,1)} %bitcast.24), calls=%async_computation | async-start | bytes 917504 | tf_op jit(solution)/shard_map/all_to_all | solution.py:233
  57.2 0.8 copy-start.1
  92.8 1.0 copy-start
  97.6 7.2 %collective-permute-start.2 = (bf16[2,32,1024]{2,1,0:T(8,128)(2,1)S(1)}, bf16[2,32,1024]{2,1,0:T(8,128)(2,1)S(1)}, u32[]{:S(2)}, u32[]{:S(2)}) collective-permute-start(bf16[2,32,1024]{2,1,0:T(8,128)(2,1)S(1)} %get-tuple-element.50), channel_id=1, source_target_pairs={{0,64},{1,65},{2,66},{3,67},{4,68},{5,69},{6,70},{7,71},{8,72},{9,... | collective-permute-start | bytes 393224 | tf_op jit(solution)/shard_map/ppermute | solution.py:244
  98.3 7.4 %collective-permute-start.1 = (bf16[2,32,1024]{2,1,0:T(8,128)(2,1)S(1)}, bf16[2,32,1024]{2,1,0:T(8,128)(2,1)S(1)}, u32[]{:S(2)}, u32[]{:S(2)}) collective-permute-start(bf16[2,32,1024]{2,1,0:T(8,128)(2,1)S(1)} %get-tuple-element.49), channel_id=1, source_target_pairs={{0,64},{1,65},{2,66},{3,67},{4,68},{5,69},{6,70},{7,71},{8,72},{9,... | collective-permute-start | bytes 393224 | tf_op jit(solution)/shard_map/ppermute | solution.py:244
  99.0 7.5 %collective-permute-start = (bf16[2,32,1024]{2,1,0:T(8,128)(2,1)S(1)}, bf16[2,32,1024]{2,1,0:T(8,128)(2,1)S(1)}, u32[]{:S(2)}, u32[]{:S(2)}) collective-permute-start(bf16[2,32,1024]{2,1,0:T(8,128)(2,1)S(1)} %get-tuple-element.48), channel_id=1, source_target_pairs={{0,64},{1,65},{2,66},{3,67},{4,68},{5,69},{6,70},{7,71},{8,72},{9,... | collective-permute-start | bytes 393224 | tf_op jit(solution)/shard_map/ppermute | solution.py:244
  105.0 2.3 %collective-permute-start.5 = (bf16[2,32,1024]{2,1,0:T(8,128)(2,1)S(1)}, bf16[2,32,1024]{2,1,0:T(8,128)(2,1)S(1)}, u32[]{:S(2)}, u32[]{:S(2)}) collective-permute-start(bf16[2,32,1024]{2,1,0:T(8,128)(2,1)S(1)} %get-tuple-element.56), channel_id=1, source_target_pairs={{64,128},{65,129},{66,130},{67,131},{68,132},{69,133},{70,134},{71... | collective-permute-start | bytes 393224 | tf_op jit(solution)/shard_map/ppermute | solution.py:244
  105.8 2.3 %collective-permute-start.4 = (bf16[2,32,1024]{2,1,0:T(8,128)(2,1)S(1)}, bf16[2,32,1024]{2,1,0:T(8,128)(2,1)S(1)}, u32[]{:S(2)}, u32[]{:S(2)}) collective-permute-start(bf16[2,32,1024]{2,1,0:T(8,128)(2,1)S(1)} %get-tuple-element.55), channel_id=1, source_target_pairs={{64,128},{65,129},{66,130},{67,131},{68,132},{69,133},{70,134},{71... | collective-permute-start | bytes 393224 | tf_op jit(solution)/shard_map/ppermute | solution.py:244
  106.6 2.3 %collective-permute-start.3 = (bf16[2,32,1024]{2,1,0:T(8,128)(2,1)S(1)}, bf16[2,32,1024]{2,1,0:T(8,128)(2,1)S(1)}, u32[]{:S(2)}, u32[]{:S(2)}) collective-permute-start(bf16[2,32,1024]{2,1,0:T(8,128)(2,1)S(1)} %get-tuple-element.54), channel_id=1, source_target_pairs={{64,128},{65,129},{66,130},{67,131},{68,132},{69,133},{70,134},{71... | collective-permute-start | bytes 393224 | tf_op jit(solution)/shard_map/ppermute | solution.py:244
  107.5 2.3 %collective-permute-start.8 = (bf16[2,32,1024]{2,1,0:T(8,128)(2,1)S(1)}, bf16[2,32,1024]{2,1,0:T(8,128)(2,1)S(1)}, u32[]{:S(2)}, u32[]{:S(2)}) collective-permute-start(bf16[2,32,1024]{2,1,0:T(8,128)(2,1)S(1)} %get-tuple-element.62), channel_id=1, source_target_pairs={{128,192},{129,193},{130,194},{131,195},{132,196},{133,197},{134,1... | collective-permute-start | bytes 393224 | tf_op jit(solution)/shard_map/ppermute | solution.py:244
  108.3 2.3 %collective-permute-start.7 = (bf16[2,32,1024]{2,1,0:T(8,128)(2,1)S(1)}, bf16[2,32,1024]{2,1,0:T(8,128)(2,1)S(1)}, u32[]{:S(2)}, u32[]{:S(2)}) collective-permute-start(bf16[2,32,1024]{2,1,0:T(8,128)(2,1)S(1)} %get-tuple-element.61), channel_id=1, source_target_pairs={{128,192},{129,193},{130,194},{131,195},{132,196},{133,197},{134,1... | collective-permute-start | bytes 393224 | tf_op jit(solution)/shard_map/ppermute | solution.py:244
  109.1 2.3 %collective-permute-start.6 = (bf16[2,32,1024]{2,1,0:T(8,128)(2,1)S(1)}, bf16[2,32,1024]{2,1,0:T(8,128)(2,1)S(1)}, u32[]{:S(2)}, u32[]{:S(2)}) collective-permute-start(bf16[2,32,1024]{2,1,0:T(8,128)(2,1)S(1)} %get-tuple-element.60), channel_id=1, source_target_pairs={{128,192},{129,193},{130,194},{131,195},{132,196},{133,197},{134,1... | collective-permute-start | bytes 393224 | tf_op jit(solution)/shard_map/ppermute | solution.py:244
  110.0 2.3 %collective-permute-start.11 = (bf16[2,32,1024]{2,1,0:T(8,128)(2,1)S(1)}, bf16[2,32,1024]{2,1,0:T(8,128)(2,1)S(1)}, u32[]{:S(2)}, u32[]{:S(2)}) collective-permute-start(bf16[2,32,1024]{2,1,0:T(8,128)(2,1)S(1)} %get-tuple-element.68), channel_id=1, source_target_pairs={{192,256},{193,257},{194,258},{195,259},{196,260},{197,261},{198,2... | collective-permute-start | bytes 393224 | tf_op jit(solution)/shard_map/ppermute | solution.py:244
  110.8 2.3 %collective-permute-start.10 = (bf16[2,32,1024]{2,1,0:T(8,128)(2,1)S(1)}, bf16[2,32,1024]{2,1,0:T(8,128)(2,1)S(1)}, u32[]{:S(2)}, u32[]{:S(2)}) collective-permute-start(bf16[2,32,1024]{2,1,0:T(8,128)(2,1)S(1)} %get-tuple-element.67), channel_id=1, source_target_pairs={{192,256},{193,257},{194,258},{195,259},{196,260},{197,261},{198,2... | collective-permute-start | bytes 393224 | tf_op jit(solution)/shard_map/ppermute | solution.py:244
  111.6 2.3 %collective-permute-start.9 = (bf16[2,32,1024]{2,1,0:T(8,128)(2,1)S(1)}, bf16[2,32,1024]{2,1,0:T(8,128)(2,1)S(1)}, u32[]{:S(2)}, u32[]{:S(2)}) collective-permute-start(bf16[2,32,1024]{2,1,0:T(8,128)(2,1)S(1)} %get-tuple-element.66), channel_id=1, source_target_pairs={{192,256},{193,257},{194,258},{195,259},{196,260},{197,261},{198,2... | collective-permute-start | bytes 393224 | tf_op jit(solution)/shard_map/ppermute | solution.py:244
  112.4 2.3 %collective-permute-start.14 = (bf16[2,32,1024]{2,1,0:T(8,128)(2,1)S(1)}, bf16[2,32,1024]{2,1,0:T(8,128)(2,1)S(1)}, u32[]{:S(2)}, u32[]{:S(2)}) collective-permute-start(bf16[2,32,1024]{2,1,0:T(8,128)(2,1)S(1)} %get-tuple-element.74), channel_id=1, source_target_pairs={{256,320},{257,321},{258,322},{259,323},{260,324},{261,325},{262,3... | collective-permute-start | bytes 393224 | tf_op jit(solution)/shard_map/ppermute | solution.py:244
  113.3 2.3 %collective-permute-start.13 = (bf16[2,32,1024]{2,1,0:T(8,128)(2,1)S(1)}, bf16[2,32,1024]{2,1,0:T(8,128)(2,1)S(1)}, u32[]{:S(2)}, u32[]{:S(2)}) collective-permute-start(bf16[2,32,1024]{2,1,0:T(8,128)(2,1)S(1)} %get-tuple-element.73), channel_id=1, source_target_pairs={{256,320},{257,321},{258,322},{259,323},{260,324},{261,325},{262,3... | collective-permute-start | bytes 393224 | tf_op jit(solution)/shard_map/ppermute | solution.py:244
  114.1 2.3 %collective-permute-start.12 = (bf16[2,32,1024]{2,1,0:T(8,128)(2,1)S(1)}, bf16[2,32,1024]{2,1,0:T(8,128)(2,1)S(1)}, u32[]{:S(2)}, u32[]{:S(2)}) collective-permute-start(bf16[2,32,1024]{2,1,0:T(8,128)(2,1)S(1)} %get-tuple-element.72), channel_id=1, source_target_pairs={{256,320},{257,321},{258,322},{259,323},{260,324},{261,325},{262,3... | collective-permute-start | bytes 393224 | tf_op jit(solution)/shard_map/ppermute | solution.py:244
  114.9 2.3 %collective-permute-start.17 = (bf16[2,32,1024]{2,1,0:T(8,128)(2,1)S(1)}, bf16[2,32,1024]{2,1,0:T(8,128)(2,1)S(1)}, u32[]{:S(2)}, u32[]{:S(2)}) collective-permute-start(bf16[2,32,1024]{2,1,0:T(8,128)(2,1)S(1)} %get-tuple-element.80), channel_id=1, source_target_pairs={{320,384},{321,385},{322,386},{323,387},{324,388},{325,389},{326,3... | collective-permute-start | bytes 393224 | tf_op jit(solution)/shard_map/ppermute | solution.py:244
  115.8 3.0 %collective-permute-start.16 = (bf16[2,32,1024]{2,1,0:T(8,128)(2,1)S(1)}, bf16[2,32,1024]{2,1,0:T(8,128)(2,1)S(1)}, u32[]{:S(2)}, u32[]{:S(2)}) collective-permute-start(bf16[2,32,1024]{2,1,0:T(8,128)(2,1)S(1)} %get-tuple-element.79), channel_id=1, source_target_pairs={{320,384},{321,385},{322,386},{323,387},{324,388},{325,389},{326,3... | collective-permute-start | bytes 393224 | tf_op jit(solution)/shard_map/ppermute | solution.py:244
  116.6 3.8 %collective-permute-start.15 = (bf16[2,32,1024]{2,1,0:T(8,128)(2,1)S(1)}, bf16[2,32,1024]{2,1,0:T(8,128)(2,1)S(1)}, u32[]{:S(2)}, u32[]{:S(2)}) collective-permute-start(bf16[2,32,1024]{2,1,0:T(8,128)(2,1)S(1)} %get-tuple-element.78), channel_id=1, source_target_pairs={{320,384},{321,385},{322,386},{323,387},{324,388},{325,389},{326,3... | collective-permute-start | bytes 393224 | tf_op jit(solution)/shard_map/ppermute | solution.py:244
  117.4 31.3 %collective-permute-start.20 = (bf16[2,32,1024]{2,1,0:T(8,128)(2,1)S(1)}, bf16[2,32,1024]{2,1,0:T(8,128)(2,1)S(1)}, u32[]{:S(2)}, u32[]{:S(2)}) collective-permute-start(bf16[2,32,1024]{2,1,0:T(8,128)(2,1)S(1)} %get-tuple-element.86), channel_id=1, source_target_pairs={{384,448},{385,449},{386,450},{387,451},{388,452},{389,453},{390,4... | collective-permute-start | bytes 393224 | tf_op jit(solution)/shard_map/ppermute | solution.py:244
  118.9 35.9 %collective-permute-start.19 = (bf16[2,32,1024]{2,1,0:T(8,128)(2,1)S(1)}, bf16[2,32,1024]{2,1,0:T(8,128)(2,1)S(1)}, u32[]{:S(2)}, u32[]{:S(2)}) collective-permute-start(bf16[2,32,1024]{2,1,0:T(8,128)(2,1)S(1)} %get-tuple-element.85), channel_id=1, source_target_pairs={{384,448},{385,449},{386,450},{387,451},{388,452},{389,453},{390,4... | collective-permute-start | bytes 393224 | tf_op jit(solution)/shard_map/ppermute | solution.py:244
  120.5 38.3 %collective-permute-start.18 = (bf16[2,32,1024]{2,1,0:T(8,128)(2,1)S(1)}, bf16[2,32,1024]{2,1,0:T(8,128)(2,1)S(1)}, u32[]{:S(2)}, u32[]{:S(2)}) collective-permute-start(bf16[2,32,1024]{2,1,0:T(8,128)(2,1)S(1)} %get-tuple-element.84), channel_id=1, source_target_pairs={{384,448},{385,449},{386,450},{387,451},{388,452},{389,453},{390,4... | collective-permute-start | bytes 393224 | tf_op jit(solution)/shard_map/ppermute | solution.py:244
Sparse Core Ops, SparseCore 0:
  18.5 74.2 all-gather.3

commit v8 on v7

--- a/solution.py
+++ b/solution.py
@@ -65,6 +65,7 @@
     return pl.pallas_call(
         join_kernel,
         out_shape=jax.ShapeDtypeStruct((2, rows, 1024), pieces.dtype),
+        compiler_params=pltpu.CompilerParams(vmem_limit_bytes=8 * MIB),
         name="join",
     )(pieces)
 
@@ -92,9 +93,9 @@
     )(basis, basis, basis, basis)
 
 
-def stage_kernel(step, pieces, parts, y_ref, state_ref, *refs):
+def stage_kernel(step, pieces, parts, handed, y_ref, state_ref, *refs):
     basis_refs, coef_ref = refs[:pieces], refs[pieces]
-    next_refs, (out_ref, now, rot) = refs[-3 - parts : -3], refs[-3:]
+    next_refs, (out_ref, now, rot) = refs[-3 - handed : -3], refs[-3:]
     s = pl.program_id(0)
     energies = coef_ref.shape[3]
     rows, channels = state_ref.shape[1:]
@@ -145,12 +146,13 @@
                 next_ref[1] = now[pl.ds(rows + own * part, own)]
 
 
-def stage(step, part, y_index, state, basis, coefs, kept):
+def stage(step, part, last, y_index, state, basis, coefs, kept):
     sectors = coefs.shape[1]
     _, rows, channels = state.shape
     first = step == 0
     pieces, parts = (4, PARTS) if first else (1, 1)
     own = rows // parts
+    handed = 0 if last else parts
     if first:
         groups, _, share, _ = basis.shape
         block = (groups // pieces, 1, share, channels)
@@ -162,7 +164,7 @@
             )
         ]
     outs = pl.pallas_call(
-        functools.partial(stage_kernel, step, pieces, parts),
+        functools.partial(stage_kernel, step, pieces, parts, handed),
         grid_spec=pltpu.PrefetchScalarGridSpec(
             num_scalar_prefetch=1,
             grid=(sectors,),
@@ -170,7 +172,7 @@
             + basis_specs
             + [pl.BlockSpec((parts, 1) + coefs.shape[2:], lambda s, y: (part, s, 0, 0, 0))]
             + ([] if first else [pl.BlockSpec(memory_space=pl.ANY)]),
-            out_specs=[pl.BlockSpec((2, own, channels), lambda s, y: (0, 0, 0))] * parts
+            out_specs=[pl.BlockSpec((2, own, channels), lambda s, y: (0, 0, 0))] * handed
             + [
                 pl.BlockSpec(
                     (1, 16, parts, own, 128),
@@ -182,9 +184,9 @@
                 pltpu.VMEM((2 * rows, channels), state.dtype),
             ],
         ),
-        out_shape=[jax.ShapeDtypeStruct((2, own, channels), state.dtype)] * parts
+        out_shape=[jax.ShapeDtypeStruct((2, own, channels), state.dtype)] * handed
         + [jax.ShapeDtypeStruct((sectors + 1, 16, PARTS, own, 128), state.dtype)],
-        input_output_aliases={} if first else {4: 1},
+        input_output_aliases={} if first else {4: handed},
         compiler_params=pltpu.CompilerParams(vmem_limit_bytes=(48 if first else 16) * MIB),
         name="stage",
     )(y_index, state, *[basis] * pieces, coefs, *([] if first else [kept]))
@@ -215,6 +217,16 @@
     )(pieces)
 
 
+def around_x(values):
+    size = lax.axis_size("x")
+    moved = [values] + [
+        lax.ppermute(values, "x", [(k, (k + shift) % size) for k in range(size)])
+        for shift in range(size - 1, 0, -1)
+    ]
+    start = lax.rem(size - lax.axis_index("x"), size)
+    return lax.dynamic_slice_in_dim(jnp.concatenate(moved + moved), start, size)
+
+
 def per_device(start_amps, energies, thresholds, intersection):
     planes = lax.axis_size("y")
     y_index = lax.axis_index("y").astype(jnp.int32).reshape(1)
@@ -222,27 +234,30 @@
     count = energies.shape[0]
     channels = intersection.shape[2]
     share = intersection.shape[1]
-    extra = jnp.pad(thresholds, ((0, 7), (0, channels - share)))
-    ring = lax.all_gather(jnp.concatenate([intersection[0], extra]), "x")
-    basis = lax.all_gather(ring[:, :share], CH_AXES)
-    limits = jnp.pad(ring[:, share, :share].reshape(2, 2 * share), ((0, 14), (0, 0)))
+    ring = lax.all_gather(intersection[0], "x")
+    basis = lax.all_gather(ring, CH_AXES)
+    limits = around_x(lax.optimization_barrier((thresholds, ring))[0])
+    limits = jnp.pad(limits.reshape(2, 2 * share), ((0, 14), (0, 0)))
 
     blocks = spread(x_index, start_amps, limits)
     per, lanes = blocks.shape[2:]
     rows = count * per
     blocks = lax.all_to_all(blocks.reshape(16, rows + per, lanes), CH_AXES, 0, 0)
-    state = join(blocks, rows)
     limits = blocks[:, rows : rows + 2].reshape(16, 4, share).swapaxes(0, 1).reshape(4, 1, channels)
     wave = jnp.sqrt(energies[None, :, None] - limits.astype(jnp.float32))
     sine = jnp.sin(wave)
     coefs = jnp.stack([jnp.cos(wave), sine / wave, wave * sine], axis=1)
     coefs = coefs.reshape(4, 3, PARTS, count // PARTS, channels).transpose(2, 0, 1, 3, 4)
-    states, kept = stage(0, 0, y_index, state, basis, coefs, None)
+    blocks, coefs = lax.optimization_barrier((blocks, coefs))
+    state = join(blocks, rows)
+    states, kept = stage(0, 0, False, y_index, state, basis, coefs, None)
     basis = turn(basis)
     for step in range(1, planes):
+        last = step == planes - 1
         for part in range(PARTS):
             state = lax.ppermute(states[part], "y", [(step - 1, step)])
-            (states[part],), kept = stage(step, part, y_index, state, basis, coefs, kept)
+            fresh, kept = stage(step, part, last, y_index, state, basis, coefs, kept)
+            states[part] = None if last else fresh[0]
     back = lax.all_to_all(kept[:4].reshape(64, rows, lanes), PLANE, 0, 0)
     return finish(back.reshape(64, count, per, lanes))[None]
 

time: 223 us -> 226 us (1.013)
  starting transfers between devices: 30.7 us -> 39.3 us
  Pallas kernels: 28.6 us -> 24.9 us
  blocking collectives: 60.7 us -> 63.3 us
    all_gather x1, waiting for transfers between devices: 31 us -> 21.4 us  [per_device(): basis = lax.all_gather(ring, CH_AXES)]
    ppermute x0 -> x3, starting transfers between devices: none -> 7.83 us  [around_x(): lax.ppermute(values, 'x', [(k, (k + shift) % size) for k in range(size)])]
    ppermute x0 -> x3, waiting for transfers between devices: none -> 3.68 us  [around_x(): lax.ppermute(values, 'x', [(k, (k + shift) % size) for k in range(size)])]
    ppermute x21, waiting for transfers between devices: 31 us -> 34.3 us  [per_device(): state = lax.ppermute(states[part], 'y', [(step - 1, step)])]
  transfers between devices with their start and end apart: 23 -> 26, of which waited for: 5 -> 6; matrix products, arithmetic and copies ran while one was open for 1% -> 2% of each run, Pallas kernels for 9% -> 7%
where the time goes in v8:
time: 226 us; the launch traced here: 225 us
  waiting for transfers between devices  79.6 us (35%)
  blocking collectives  63.3 us (28%)
  starting transfers between devices  39.3 us (17%)
  Pallas kernels  24.9 us (11%)
  between operations  14 us (6%)
    all_to_all x1, blocking collectives, per_device(): back = lax.all_to_all(kept[:4].reshape(64, rows, lanes), PLANE, 0, 0)  52.4 us
    ppermute x21, waiting for transfers between devices, per_device(): state = lax.ppermute(states[part], 'y', [(step - 1, step)])  34.3 us
    all_gather x1, waiting for transfers between devices, per_device(): basis = lax.all_gather(ring, CH_AXES)  21.4 us
    all_to_all x1, waiting for transfers between devices, per_device(): lax.all_to_all(blocks.reshape(16, rows + per, lanes), CH_AXES, 0, 0)  20.2 us
    ppermute x21, starting transfers between devices, per_device(): state = lax.ppermute(states[part], 'y', [(step - 1, step)])  16.1 us
    all_to_all x1, starting transfers between devices, per_device(): lax.all_to_all(blocks.reshape(16, rows + per, lanes), CH_AXES, 0, 0)  15.3 us
    pallas_call x22, Pallas kernels, stage(): pl.pallas_call(functools.partial(stage_kernel, step, pieces, parts, hande...  13.4 us
    all_gather x1, blocking collectives, per_device(): ring = lax.all_gather(intersection[0], 'x')  10.8 us
  transfers between devices with their start and end apart: 26, of which 6 were waited for; matrix products, arithmetic and copies ran while one was open for 2% of the time, Pallas kernels for 7%

profile of v8, /device:TPU:63, one launch (start us, length us, event | category | flops | bytes accessed | tf_op | source)
XLA Modules:
  0.0 224.8 jit_solution(11642126281766689408)
XLA Ops:
  6.5 10.8 %all_gather.9 = bf16[4,64,1024]{2,1,0:T(8,128)(2,1)} all-gather(bf16[1,64,1024]{2,1,0:T(8,128)(2,1)} %param.7), channel_id=1, replica_groups=mesh['y'=8,'x'=4,'z'=8,'core'=2] {'x'}, dimensions={0}, use_global_device_ids=true | all-gather | bytes 655360 | tf_op jit(solution)/shard_map/all_gather | solution.py:237
  17.4 3.4 %collective-permute-start.2 = (bf16[1,64]{1,0:T(2,128)(2,1)}, bf16[1,64]{1,0:T(2,128)(2,1)S(1)}, u32[]{:S(2)}, u32[]{:S(2)}) collective-permute-start(bf16[1,64]{1,0:T(2,128)(2,1)} %param.6), channel_id=1, source_target_pairs={{0,16},{16,32},{32,48},{48,0},{1,17},{17,33},{33,49},{49,1},{2,18}... | collective-permute-start | bytes 392 | tf_op jit(solution)/shard_map/ppermute | solution.py:223
  20.8 2.5 %collective-permute-start.1 = (bf16[1,64]{1,0:T(2,128)(2,1)}, bf16[1,64]{1,0:T(2,128)(2,1)S(1)}, u32[]{:S(2)}, u32[]{:S(2)}) collective-permute-start(bf16[1,64]{1,0:T(2,128)(2,1)} %param.6), channel_id=1, source_target_pairs={{0,32},{16,48},{32,0},{48,16},{1,33},{17,49},{33,1},{49,17},{2,34}... | collective-permute-start | bytes 392 | tf_op jit(solution)/shard_map/ppermute | solution.py:223
  23.3 1.9 collective-permute-start
  25.3 1.5 collective-permute-done.1
  26.7 2.2 collective-permute-done
  28.9 0.8 concatenate.4
  30.4 4.1 %spread.1 = bf16[16,7,16,128]{3,2,1,0:T(8,128)(2,1)} custom-call(s32[1]{0:T(128)} %bitcast.1.x_ref, bf16[6,64,2048]{2,1,0:T(8,128)(2,1)} %p_ref.1, bf16[6,64,2048]{2,1,0:T(8,128)(2,1)} %p_ref.1, bf16[16,128]{1,0:T(8,128)(2,1)} %pad.4.limit_ref), custom_call_target="tpu_custom_call" | custom-call | tf_op jit(solution)/shard_map/spread/pallas_call | solution.py:36
  34.5 15.3 %all-to-all-start = ((bf16[16,112,128]{2,1,0:T(8,128)(2,1)}), bf16[16,112,128]{2,1,0:T(8,128)(2,1)S(1)}, u32[]{:S(2)}, u32[]{:S(2)}) async-start(bf16[16,112,128]{2,1,0:T(8,128)(2,1)} %bitcast.20), calls=%async_computation | async-start | bytes 917504 | tf_op jit(solution)/shard_map/all_to_all | solution.py:245
  49.9 20.2 %all-to-all-done.in_ref = bf16[16,112,128]{2,1,0:T(8,128)(2,1)S(1)} async-done(((bf16[16,112,128]{2,1,0:T(8,128)(2,1)}), bf16[16,112,128]{2,1,0:T(8,128)(2,1)S(1)}, u32[]{:S(2)}, u32[]{:S(2)}) %all-to-all-start) | async-done | bytes 458784 | tf_op jit(solution)/shard_map/all_to_all | solution.py:245
  70.3 1.7 fusion.3
  72.4 21.4 %all-gather.3.cloned.1.call-done = bf16[64,64,1024]{2,1,0:T(8,128)(2,1)} async-done(((bf16[4,64,1024]{2,1,0:T(8,128)(2,1)}), bf16[64,64,1024]{2,1,0:T(8,128)(2,1)}) %all-gather.3.cloned.1.call-update) | async-done | bytes 8388624 | tf_op jit(solution)/shard_map/all_gather | solution.py:238
  93.7 3.8 %stage.22 = (bf16[2,32,1024]{2,1,0:T(8,128)(2,1)S(1)}, bf16[2,32,1024]{2,1,0:T(8,128)(2,1)S(1)}, bf16[2,32,1024]{2,1,0:T(8,128)(2,1)S(1)}, bf16[5,16,3,32,128]{4,3,2,1,0:T(8,128)(2,1)S(1)}) custom-call(s32[1]{0:T(128)} %bitcast.y_ref, bf16[2,96,1024]{2,1,0:T(8,128)(2,1)S(1)} %join.1.state_ref, bf16[16,4,64,1024]{3,2,1,0:T(8,128)(2,1)} %bitcast.11, ...), custom_call_target="tpu_custom_call" | custom-call | tf_op jit(solution)/shard_map/stage/pallas_call | solution.py:166
  98.2 0.7 collective-permute-start.4
  98.9 0.7 collective-permute-start.3
  99.5 5.2 %turn.1.refs_0_ = bf16[4,1024,1024]{2,1,0:T(8,128)(2,1)S(1)} custom-call(bf16[16,4,64,1024]{3,2,1,0:T(8,128)(2,1)} %bitcast.15, bf16[16,4,64,1024]{3,2,1,0:T(8,128)(2,1)} %bitcast.16, bf16[16,4,64,1024]{3,2,1,0:T(8,128)(2,1)} %bitcast.17, bf16[16,4,64,1024]{3,2,1,0:T(8,128)(2,1)} %bitcast.18), custom_call_target="tpu_custom_call" | custom-call | tf_op jit(solution)/shard_map/turn/pallas_call | solution.py:85
  104.9 0.7 collective-permute-start.8
  106.5 0.7 collective-permute-start.6
  108.2 0.7 collective-permute-start.10
  110.7 0.7 collective-permute-start.13
  113.2 0.7 collective-permute-start.16
  114.8 0.7 collective-permute-start.20
  117.5 1.3 collective-permute-start.22
  118.8 1.5 collective-permute-start.23
  120.4 1.3 collective-permute-start.21
  121.7 33.5 %collective-permute-done.23.state_ref = bf16[2,32,1024]{2,1,0:T(8,128)(2,1)S(1)} collective-permute-done((bf16[2,32,1024]{2,1,0:T(8,128)(2,1)S(1)}, bf16[2,32,1024]{2,1,0:T(8,128)(2,1)S(1)}, u32[]{:S(2)}, u32[]{:S(2)}) %collective-permute-start.23) | collective-permute-done | bytes 131104 | tf_op jit(solution)/shard_map/ppermute | solution.py:258
  155.2 2.4 %stage.41.refs_2_ = bf16[5,16,3,32,128]{4,3,2,1,0:T(8,128)(2,1)S(1)} custom-call(s32[1]{0:T(128)} %bitcast.y_ref, bf16[2,32,1024]{2,1,0:T(8,128)(2,1)S(1)} %collective-permute-done.23.state_ref, bf16[4,1024,1024]{2,1,0:T(8,128)(2,1)S(1)} %turn.1.refs_0_, ...), custom_call_target="tpu_custom_call", output_to_operand_aliasing={{}: (4, {})} | custom-call | tf_op jit(solution)/shard_map/stage/pallas_call | solution.py:166
  157.6 2.4 %stage.42.refs_2_ = bf16[5,16,3,32,128]{4,3,2,1,0:T(8,128)(2,1)S(1)} custom-call(s32[1]{0:T(128)} %bitcast.y_ref, bf16[2,32,1024]{2,1,0:T(8,128)(2,1)S(1)} %collective-permute-done.22.state_ref, bf16[4,1024,1024]{2,1,0:T(8,128)(2,1)S(1)} %turn.1.refs_0_, ...), custom_call_target="tpu_custom_call", output_to_operand_aliasing={{}: (4, {})} | custom-call | tf_op jit(solution)/shard_map/stage/pallas_call | solution.py:166
  160.1 0.7 collective-permute-done.21.state_ref
  160.8 2.4 %stage.43 = bf16[5,16,3,32,128]{4,3,2,1,0:T(8,128)(2,1)S(1)} custom-call(s32[1]{0:T(128)} %bitcast.y_ref, bf16[2,32,1024]{2,1,0:T(8,128)(2,1)S(1)} %collective-permute-done.21.state_ref, bf16[4,1024,1024]{2,1,0:T(8,128)(2,1)S(1)} %turn.1.refs_0_, f32[3,4,3,2,1024]{4,3,2,1,0:T(2,128)S(1)} %maximum_bitcast_fusion.refs_4_.refs_1_, ...), custom_call_target="tpu_custom_call", output_to_operand_aliasing={{}: (4, {})} | custom-call | tf_op jit(solution)/shard_map/stage/pallas_call | solution.py:166
  163.4 52.4 %all_to_all.10 = bf16[64,96,128]{2,1,0:T(8,128)(2,1)S(1)} all-to-all(bf16[64,96,128]{2,1,0:T(8,128)(2,1)S(1)} %bitcast.19), channel_id=1, replica_groups=mesh['y'=8,'x'=4,'z'=8,'core'=2] {'x','z','core'}, dimensions={0} | all-to-all | bytes 3145728 | tf_op jit(solution)/shard_map/all_to_all | solution.py:261
  215.9 2.1 finish.1
  (63 shorter events, 10.7 us)
Async XLA Ops:
  6.5 87.2 %all-gather.3.cloned.1.call-start = ((), (), s32[]{:S(2)}) async-start(), calls=%async_computation.2 | async-start | bytes 8912896 | tf_op jit(solution)/shard_map/all_gather | solution.py:238
  17.4 7.9 %collective-permute-start.2 = (bf16[1,64]{1,0:T(2,128)(2,1)}, bf16[1,64]{1,0:T(2,128)(2,1)S(1)}, u32[]{:S(2)}, u32[]{:S(2)}) collective-permute-start(bf16[1,64]{1,0:T(2,128)(2,1)} %param.6), channel_id=1, source_target_pairs={{0,16},{16,32},{32,48},{48,0},{1,17},{17,33},{33,49},{49,1},{2,18}... | collective-permute-start | bytes 392 | tf_op jit(solution)/shard_map/ppermute | solution.py:223
  20.8 5.9 %collective-permute-start.1 = (bf16[1,64]{1,0:T(2,128)(2,1)}, bf16[1,64]{1,0:T(2,128)(2,1)S(1)}, u32[]{:S(2)}, u32[]{:S(2)}) collective-permute-start(bf16[1,64]{1,0:T(2,128)(2,1)} %param.6), channel_id=1, source_target_pairs={{0,32},{16,48},{32,0},{48,16},{1,33},{17,49},{33,1},{49,17},{2,34}... | collective-permute-start | bytes 392 | tf_op jit(solution)/shard_map/ppermute | solution.py:223
  23.3 5.6 %collective-permute-start = (bf16[1,64]{1,0:T(2,128)(2,1)}, bf16[1,64]{1,0:T(2,128)(2,1)S(1)}, u32[]{:S(2)}, u32[]{:S(2)}) collective-permute-start(bf16[1,64]{1,0:T(2,128)(2,1)} %param.6), channel_id=1, source_target_pairs={{0,48},{16,0},{32,16},{48,32},{1,49},{17,1},{33,17},{49,33},{2,50}... | collective-permute-start | bytes 392 | tf_op jit(solution)/shard_map/ppermute | solution.py:223
  30.4 19.4 %copy-start = (f32[6]{0:T(128)S(1)}, f32[6]{0:T(128)}, u32[]{:S(2)}) copy-start(f32[6]{0:T(128)} %param.5) | copy-start | bytes 76
  34.5 35.6 %all-to-all-start = ((bf16[16,112,128]{2,1,0:T(8,128)(2,1)}), bf16[16,112,128]{2,1,0:T(8,128)(2,1)S(1)}, u32[]{:S(2)}, u32[]{:S(2)}) async-start(bf16[16,112,128]{2,1,0:T(8,128)(2,1)} %bitcast.20), calls=%async_computation | async-start | bytes 917504 | tf_op jit(solution)/shard_map/all_to_all | solution.py:245
  97.5 7.2 %collective-permute-start.5 = (bf16[2,32,1024]{2,1,0:T(8,128)(2,1)S(1)}, bf16[2,32,1024]{2,1,0:T(8,128)(2,1)S(1)}, u32[]{:S(2)}, u32[]{:S(2)}) collective-permute-start(bf16[2,32,1024]{2,1,0:T(8,128)(2,1)S(1)} %get-tuple-element.53), channel_id=1, source_target_pairs={{0,64},{1,65},{2,66},{3,67},{4,68},{5,69},{6,70},{7,71},{8,72},{9,... | collective-permute-start | bytes 393224 | tf_op jit(solution)/shard_map/ppermute | solution.py:258
  98.2 7.4 %collective-permute-start.4 = (bf16[2,32,1024]{2,1,0:T(8,128)(2,1)S(1)}, bf16[2,32,1024]{2,1,0:T(8,128)(2,1)S(1)}, u32[]{:S(2)}, u32[]{:S(2)}) collective-permute-start(bf16[2,32,1024]{2,1,0:T(8,128)(2,1)S(1)} %get-tuple-element.52), channel_id=1, source_target_pairs={{0,64},{1,65},{2,66},{3,67},{4,68},{5,69},{6,70},{7,71},{8,72},{9,... | collective-permute-start | bytes 393224 | tf_op jit(solution)/shard_map/ppermute | solution.py:258
  98.9 7.5 %collective-permute-start.3 = (bf16[2,32,1024]{2,1,0:T(8,128)(2,1)S(1)}, bf16[2,32,1024]{2,1,0:T(8,128)(2,1)S(1)}, u32[]{:S(2)}, u32[]{:S(2)}) collective-permute-start(bf16[2,32,1024]{2,1,0:T(8,128)(2,1)S(1)} %get-tuple-element.51), channel_id=1, source_target_pairs={{0,64},{1,65},{2,66},{3,67},{4,68},{5,69},{6,70},{7,71},{8,72},{9,... | collective-permute-start | bytes 393224 | tf_op jit(solution)/shard_map/ppermute | solution.py:258
  104.9 2.3 %collective-permute-start.8 = (bf16[2,32,1024]{2,1,0:T(8,128)(2,1)S(1)}, bf16[2,32,1024]{2,1,0:T(8,128)(2,1)S(1)}, u32[]{:S(2)}, u32[]{:S(2)}) collective-permute-start(bf16[2,32,1024]{2,1,0:T(8,128)(2,1)S(1)} %get-tuple-element.59), channel_id=1, source_target_pairs={{64,128},{65,129},{66,130},{67,131},{68,132},{69,133},{70,134},{71... | collective-permute-start | bytes 393224 | tf_op jit(solution)/shard_map/ppermute | solution.py:258
  105.7 2.3 %collective-permute-start.7 = (bf16[2,32,1024]{2,1,0:T(8,128)(2,1)S(1)}, bf16[2,32,1024]{2,1,0:T(8,128)(2,1)S(1)}, u32[]{:S(2)}, u32[]{:S(2)}) collective-permute-start(bf16[2,32,1024]{2,1,0:T(8,128)(2,1)S(1)} %get-tuple-element.58), channel_id=1, source_target_pairs={{64,128},{65,129},{66,130},{67,131},{68,132},{69,133},{70,134},{71... | collective-permute-start | bytes 393224 | tf_op jit(solution)/shard_map/ppermute | solution.py:258
  106.5 2.3 %collective-permute-start.6 = (bf16[2,32,1024]{2,1,0:T(8,128)(2,1)S(1)}, bf16[2,32,1024]{2,1,0:T(8,128)(2,1)S(1)}, u32[]{:S(2)}, u32[]{:S(2)}) collective-permute-start(bf16[2,32,1024]{2,1,0:T(8,128)(2,1)S(1)} %get-tuple-element.57), channel_id=1, source_target_pairs={{64,128},{65,129},{66,130},{67,131},{68,132},{69,133},{70,134},{71... | collective-permute-start | bytes 393224 | tf_op jit(solution)/shard_map/ppermute | solution.py:258
  107.4 2.3 %collective-permute-start.11 = (bf16[2,32,1024]{2,1,0:T(8,128)(2,1)S(1)}, bf16[2,32,1024]{2,1,0:T(8,128)(2,1)S(1)}, u32[]{:S(2)}, u32[]{:S(2)}) collective-permute-start(bf16[2,32,1024]{2,1,0:T(8,128)(2,1)S(1)} %get-tuple-element.65), channel_id=1, source_target_pairs={{128,192},{129,193},{130,194},{131,195},{132,196},{133,197},{134,1... | collective-permute-start | bytes 393224 | tf_op jit(solution)/shard_map/ppermute | solution.py:258
  108.2 2.3 %collective-permute-start.10 = (bf16[2,32,1024]{2,1,0:T(8,128)(2,1)S(1)}, bf16[2,32,1024]{2,1,0:T(8,128)(2,1)S(1)}, u32[]{:S(2)}, u32[]{:S(2)}) collective-permute-start(bf16[2,32,1024]{2,1,0:T(8,128)(2,1)S(1)} %get-tuple-element.64), channel_id=1, source_target_pairs={{128,192},{129,193},{130,194},{131,195},{132,196},{133,197},{134,1... | collective-permute-start | bytes 393224 | tf_op jit(solution)/shard_map/ppermute | solution.py:258
  109.0 2.3 %collective-permute-start.9 = (bf16[2,32,1024]{2,1,0:T(8,128)(2,1)S(1)}, bf16[2,32,1024]{2,1,0:T(8,128)(2,1)S(1)}, u32[]{:S(2)}, u32[]{:S(2)}) collective-permute-start(bf16[2,32,1024]{2,1,0:T(8,128)(2,1)S(1)} %get-tuple-element.63), channel_id=1, source_target_pairs={{128,192},{129,193},{130,194},{131,195},{132,196},{133,197},{134,1... | collective-permute-start | bytes 393224 | tf_op jit(solution)/shard_map/ppermute | solution.py:258
  109.9 2.3 %collective-permute-start.14 = (bf16[2,32,1024]{2,1,0:T(8,128)(2,1)S(1)}, bf16[2,32,1024]{2,1,0:T(8,128)(2,1)S(1)}, u32[]{:S(2)}, u32[]{:S(2)}) collective-permute-start(bf16[2,32,1024]{2,1,0:T(8,128)(2,1)S(1)} %get-tuple-element.71), channel_id=1, source_target_pairs={{192,256},{193,257},{194,258},{195,259},{196,260},{197,261},{198,2... | collective-permute-start | bytes 393224 | tf_op jit(solution)/shard_map/ppermute | solution.py:258
  110.7 2.3 %collective-permute-start.13 = (bf16[2,32,1024]{2,1,0:T(8,128)(2,1)S(1)}, bf16[2,32,1024]{2,1,0:T(8,128)(2,1)S(1)}, u32[]{:S(2)}, u32[]{:S(2)}) collective-permute-start(bf16[2,32,1024]{2,1,0:T(8,128)(2,1)S(1)} %get-tuple-element.70), channel_id=1, source_target_pairs={{192,256},{193,257},{194,258},{195,259},{196,260},{197,261},{198,2... | collective-permute-start | bytes 393224 | tf_op jit(solution)/shard_map/ppermute | solution.py:258
  111.5 2.3 %collective-permute-start.12 = (bf16[2,32,1024]{2,1,0:T(8,128)(2,1)S(1)}, bf16[2,32,1024]{2,1,0:T(8,128)(2,1)S(1)}, u32[]{:S(2)}, u32[]{:S(2)}) collective-permute-start(bf16[2,32,1024]{2,1,0:T(8,128)(2,1)S(1)} %get-tuple-element.69), channel_id=1, source_target_pairs={{192,256},{193,257},{194,258},{195,259},{196,260},{197,261},{198,2... | collective-permute-start | bytes 393224 | tf_op jit(solution)/shard_map/ppermute | solution.py:258
  112.3 2.3 %collective-permute-start.17 = (bf16[2,32,1024]{2,1,0:T(8,128)(2,1)S(1)}, bf16[2,32,1024]{2,1,0:T(8,128)(2,1)S(1)}, u32[]{:S(2)}, u32[]{:S(2)}) collective-permute-start(bf16[2,32,1024]{2,1,0:T(8,128)(2,1)S(1)} %get-tuple-element.77), channel_id=1, source_target_pairs={{256,320},{257,321},{258,322},{259,323},{260,324},{261,325},{262,3... | collective-permute-start | bytes 393224 | tf_op jit(solution)/shard_map/ppermute | solution.py:258
  113.2 2.3 %collective-permute-start.16 = (bf16[2,32,1024]{2,1,0:T(8,128)(2,1)S(1)}, bf16[2,32,1024]{2,1,0:T(8,128)(2,1)S(1)}, u32[]{:S(2)}, u32[]{:S(2)}) collective-permute-start(bf16[2,32,1024]{2,1,0:T(8,128)(2,1)S(1)} %get-tuple-element.76), channel_id=1, source_target_pairs={{256,320},{257,321},{258,322},{259,323},{260,324},{261,325},{262,3... | collective-permute-start | bytes 393224 | tf_op jit(solution)/shard_map/ppermute | solution.py:258
  114.0 2.3 %collective-permute-start.15 = (bf16[2,32,1024]{2,1,0:T(8,128)(2,1)S(1)}, bf16[2,32,1024]{2,1,0:T(8,128)(2,1)S(1)}, u32[]{:S(2)}, u32[]{:S(2)}) collective-permute-start(bf16[2,32,1024]{2,1,0:T(8,128)(2,1)S(1)} %get-tuple-element.75), channel_id=1, source_target_pairs={{256,320},{257,321},{258,322},{259,323},{260,324},{261,325},{262,3... | collective-permute-start | bytes 393224 | tf_op jit(solution)/shard_map/ppermute | solution.py:258
  114.8 2.3 %collective-permute-start.20 = (bf16[2,32,1024]{2,1,0:T(8,128)(2,1)S(1)}, bf16[2,32,1024]{2,1,0:T(8,128)(2,1)S(1)}, u32[]{:S(2)}, u32[]{:S(2)}) collective-permute-start(bf16[2,32,1024]{2,1,0:T(8,128)(2,1)S(1)} %get-tuple-element.83), channel_id=1, source_target_pairs={{320,384},{321,385},{322,386},{323,387},{324,388},{325,389},{326,3... | collective-permute-start | bytes 393224 | tf_op jit(solution)/shard_map/ppermute | solution.py:258
  115.7 1.7 collective-permute-start.19
  116.5 3.8 %collective-permute-start.18 = (bf16[2,32,1024]{2,1,0:T(8,128)(2,1)S(1)}, bf16[2,32,1024]{2,1,0:T(8,128)(2,1)S(1)}, u32[]{:S(2)}, u32[]{:S(2)}) collective-permute-start(bf16[2,32,1024]{2,1,0:T(8,128)(2,1)S(1)} %get-tuple-element.81), channel_id=1, source_target_pairs={{320,384},{321,385},{322,386},{323,387},{324,388},{325,389},{326,3... | collective-permute-start | bytes 393224 | tf_op jit(solution)/shard_map/ppermute | solution.py:258
  117.5 40.2 %collective-permute-start.22 = (bf16[2,32,1024]{2,1,0:T(8,128)(2,1)S(1)}, bf16[2,32,1024]{2,1,0:T(8,128)(2,1)S(1)}, u32[]{:S(2)}, u32[]{:S(2)}) collective-permute-start(bf16[2,32,1024]{2,1,0:T(8,128)(2,1)S(1)} %get-tuple-element.88), channel_id=1, source_target_pairs={{384,448},{385,449},{386,450},{387,451},{388,452},{389,453},{390,4... | collective-permute-start | bytes 393224 | tf_op jit(solution)/shard_map/ppermute | solution.py:258
  118.8 36.5 %collective-permute-start.23 = (bf16[2,32,1024]{2,1,0:T(8,128)(2,1)S(1)}, bf16[2,32,1024]{2,1,0:T(8,128)(2,1)S(1)}, u32[]{:S(2)}, u32[]{:S(2)}) collective-permute-start(bf16[2,32,1024]{2,1,0:T(8,128)(2,1)S(1)} %get-tuple-element.89), channel_id=1, source_target_pairs={{384,448},{385,449},{386,450},{387,451},{388,452},{389,453},{390,4... | collective-permute-start | bytes 393224 | tf_op jit(solution)/shard_map/ppermute | solution.py:258
  120.4 40.4 %collective-permute-start.21 = (bf16[2,32,1024]{2,1,0:T(8,128)(2,1)S(1)}, bf16[2,32,1024]{2,1,0:T(8,128)(2,1)S(1)}, u32[]{:S(2)}, u32[]{:S(2)}) collective-permute-start(bf16[2,32,1024]{2,1,0:T(8,128)(2,1)S(1)} %get-tuple-element.87), channel_id=1, source_target_pairs={{384,448},{385,449},{386,450},{387,451},{388,452},{389,453},{390,4... | collective-permute-start | bytes 393224 | tf_op jit(solution)/shard_map/ppermute | solution.py:258
Sparse Core Ops, SparseCore 0:
  17.5 76.1 all-gather.2

commit v9 on v8

--- a/solution.py
+++ b/solution.py
@@ -89,6 +89,7 @@
         out_specs=pl.BlockSpec((1, channels, groups * share), lambda s: (s, 0, 0)),
         out_shape=jax.ShapeDtypeStruct((sectors, channels, groups * share), basis.dtype),
         compiler_params=pltpu.CompilerParams(vmem_limit_bytes=40 * MIB),
+        cost_estimate=pl.CostEstimate(flops=0, bytes_accessed=2 * basis.size, transcendentals=0),
         name="turn",
     )(basis, basis, basis, basis)
 
@@ -188,6 +189,11 @@
         + [jax.ShapeDtypeStruct((sectors + 1, 16, PARTS, own, 128), state.dtype)],
         input_output_aliases={} if first else {4: handed},
         compiler_params=pltpu.CompilerParams(vmem_limit_bytes=(48 if first else 16) * MIB),
+        cost_estimate=pl.CostEstimate(
+            flops=4 * sectors * rows * channels * channels,
+            bytes_accessed=2 * sectors * channels * (channels + 2 * rows),
+            transcendentals=0,
+        ),
         name="stage",
     )(y_index, state, *[basis] * pieces, coefs, *([] if first else [kept]))
     return list(outs[:-1]), outs[-1]
@@ -217,16 +223,6 @@
     )(pieces)
 
 
-def around_x(values):
-    size = lax.axis_size("x")
-    moved = [values] + [
-        lax.ppermute(values, "x", [(k, (k + shift) % size) for k in range(size)])
-        for shift in range(size - 1, 0, -1)
-    ]
-    start = lax.rem(size - lax.axis_index("x"), size)
-    return lax.dynamic_slice_in_dim(jnp.concatenate(moved + moved), start, size)
-
-
 def per_device(start_amps, energies, thresholds, intersection):
     planes = lax.axis_size("y")
     y_index = lax.axis_index("y").astype(jnp.int32).reshape(1)
@@ -234,10 +230,10 @@
     count = energies.shape[0]
     channels = intersection.shape[2]
     share = intersection.shape[1]
-    ring = lax.all_gather(intersection[0], "x")
-    basis = lax.all_gather(ring, CH_AXES)
-    limits = around_x(lax.optimization_barrier((thresholds, ring))[0])
-    limits = jnp.pad(limits.reshape(2, 2 * share), ((0, 14), (0, 0)))
+    extra = jnp.pad(thresholds, ((0, 7), (0, channels - share)))
+    ring = lax.all_gather(jnp.concatenate([intersection[0], extra]), "x")
+    basis = lax.all_gather(ring[:, :share], CH_AXES)
+    limits = jnp.pad(ring[:, share, :share].reshape(2, 2 * share), ((0, 14), (0, 0)))
 
     blocks = spread(x_index, start_amps, limits)
     per, lanes = blocks.shape[2:]

time: 226 us -> 221 us (0.978)
  starting transfers between devices: 39.3 us -> 30.7 us
  waiting for transfers between devices: 79.6 us -> 85 us
  blocking collectives: 63.3 us -> 60.4 us
    all_gather x1, waiting for transfers between devices: 21.4 us -> 33.4 us  [per_device(): basis = lax.all_gather(ring[:, :share], CH_AXES)]
    ppermute x3 -> x0, starting transfers between devices: 7.83 us -> none  [around_x(): lax.ppermute(values, 'x', [(k, (k + shift) % size) for k in range(size)])]
    ppermute x3 -> x0, waiting for transfers between devices: 3.68 us -> none  [around_x(): lax.ppermute(values, 'x', [(k, (k + shift) % size) for k in range(size)])]
  transfers between devices with their start and end apart: 26 -> 23, of which waited for: 6 -> 5; matrix products, arithmetic and copies ran while one was open for 2% -> 1% of each run, Pallas kernels for 7% -> 8%
where the time goes in v9:
time: 221 us; the launch traced here: 220 us
  waiting for transfers between devices  85 us (38%)
  blocking collectives  60.4 us (27%)
  starting transfers between devices  30.7 us (14%)
  Pallas kernels  24.9 us (11%)
  between operations  13.9 us (6%)
  other arithmetic  2.74 us (1%)
    all_to_all x1, blocking collectives, per_device(): back = lax.all_to_all(kept[:4].reshape(64, rows, lanes), PLANE, 0, 0)  50.4 us
    all_gather x1, waiting for transfers between devices, per_device(): basis = lax.all_gather(ring[:, :share], CH_AXES)  33.4 us
    ppermute x21, waiting for transfers between devices, per_device(): state = lax.ppermute(states[part], 'y', [(step - 1, step)])  32.2 us
    all_to_all x1, waiting for transfers between devices, per_device(): lax.all_to_all(blocks.reshape(16, rows + per, lanes), CH_AXES, 0, 0)  19.4 us
    ppermute x21, starting transfers between devices, per_device(): state = lax.ppermute(states[part], 'y', [(step - 1, step)])  16.1 us
    all_to_all x1, starting transfers between devices, per_device(): lax.all_to_all(blocks.reshape(16, rows + per, lanes), CH_AXES, 0, 0)  14.6 us
    pallas_call x22, Pallas kernels, stage(): pl.pallas_call(functools.partial(stage_kernel, step, pieces, parts, hande...  13.4 us
    all_gather x1, blocking collectives, per_device(): ring = lax.all_gather(jnp.concatenate([intersection[0], extra]), 'x')  10 us
  transfers between devices with their start and end apart: 23, of which 5 were waited for; matrix products, arithmetic and copies ran while one was open for 1% of the time, Pallas kernels for 8%

profile of v9, /device:TPU:63, one launch (start us, length us, event | category | flops | bytes accessed | tf_op | source)
XLA Modules:
  0.0 219.8 jit_solution(9534254669925475952)
XLA Ops:
  6.5 0.9 fusion.1
  7.5 10.0 %all-gather = bf16[288,1024]{1,0:T(8,128)(2,1)S(1)} all-gather(bf16[72,1024]{1,0:T(8,128)(2,1)S(1)} %fusion.1), channel_id=2, replica_groups=mesh['y'=8,'x'=4,'z'=8,'core'=2] {'x'}, dimensions={0}, use_global_device_ids=true | all-gather | bytes 737280 | tf_op jit(solution)/shard_map/all_gather | solution.py:234
  17.5 0.8 slice.18
  19.1 4.1 %spread.1 = bf16[16,7,16,128]{3,2,1,0:T(8,128)(2,1)} custom-call(s32[1]{0:T(128)} %bitcast.1.x_ref, bf16[6,64,2048]{2,1,0:T(8,128)(2,1)} %p_ref.1, bf16[6,64,2048]{2,1,0:T(8,128)(2,1)} %p_ref.1, bf16[16,128]{1,0:T(8,128)(2,1)} %pad.9.limit_ref), custom_call_target="tpu_custom_call" | custom-call | tf_op jit(solution)/shard_map/spread/pallas_call | solution.py:36
  23.2 14.6 %all-to-all-start = ((bf16[16,112,128]{2,1,0:T(8,128)(2,1)}), bf16[16,112,128]{2,1,0:T(8,128)(2,1)S(1)}, u32[]{:S(2)}, u32[]{:S(2)}) async-start(bf16[16,112,128]{2,1,0:T(8,128)(2,1)} %bitcast.24), calls=%async_computation | async-start | bytes 917504 | tf_op jit(solution)/shard_map/all_to_all | solution.py:241
  37.9 19.4 %all-to-all-done.in_ref = bf16[16,112,128]{2,1,0:T(8,128)(2,1)S(1)} async-done(((bf16[16,112,128]{2,1,0:T(8,128)(2,1)}), bf16[16,112,128]{2,1,0:T(8,128)(2,1)S(1)}, u32[]{:S(2)}, u32[]{:S(2)}) %all-to-all-start) | async-done | bytes 458784 | tf_op jit(solution)/shard_map/all_to_all | solution.py:241
  57.4 1.7 fusion.5
  59.4 33.4 %all-gather.4.cloned.1.call-done = bf16[64,64,1024]{2,1,0:T(8,128)(2,1)} async-done(((bf16[4,64,1024]{2,1,0:T(8,128)(2,1)}), bf16[64,64,1024]{2,1,0:T(8,128)(2,1)}) %all-gather.4.cloned.1.call-update) | async-done | bytes 8388624 | tf_op jit(solution)/shard_map/all_gather | solution.py:235
  92.8 3.8 %stage.22 = (bf16[2,32,1024]{2,1,0:T(8,128)(2,1)S(1)}, bf16[2,32,1024]{2,1,0:T(8,128)(2,1)S(1)}, bf16[2,32,1024]{2,1,0:T(8,128)(2,1)S(1)}, bf16[5,16,3,32,128]{4,3,2,1,0:T(8,128)(2,1)S(1)}) custom-call(s32[1]{0:T(128)} %bitcast.y_ref, bf16[2,96,1024]{2,1,0:T(8,128)(2,1)S(1)} %join.1.state_ref, bf16[16,4,64,1024]{3,2,1,0:T(8,128)(2,1)} %bitcast.13, ...), custom_call_target="tpu_custom_call" | custom-call | flops 1610612736 | bytes 9961472 | tf_op jit(solution)/shard_map/stage/pallas_call | solution.py:167
  97.3 0.7 collective-permute-start.1
  98.0 0.7 collective-permute-start
  98.6 5.2 %turn.1.refs_0_ = bf16[4,1024,1024]{2,1,0:T(8,128)(2,1)S(1)} custom-call(bf16[16,4,64,1024]{3,2,1,0:T(8,128)(2,1)} %bitcast.17, bf16[16,4,64,1024]{3,2,1,0:T(8,128)(2,1)} %bitcast.18, bf16[16,4,64,1024]{3,2,1,0:T(8,128)(2,1)} %bitcast.19, bf16[16,4,64,1024]{3,2,1,0:T(8,128)(2,1)} %bitcast.20), custom_call_target="tpu_custom_call" | custom-call | bytes 8388608 | tf_op jit(solution)/shard_map/turn/pallas_call | solution.py:85
  104.0 0.7 collective-permute-start.5
  104.8 0.7 collective-permute-start.4
  105.7 0.7 collective-permute-start.3
  106.5 0.7 collective-permute-start.8
  107.3 0.7 collective-permute-start.7
  109.0 0.7 collective-permute-start.11
  111.5 0.7 collective-permute-start.14
  113.1 0.7 collective-permute-start.12
  115.6 0.7 collective-permute-start.15
  116.4 1.3 collective-permute-start.20
  117.9 1.5 collective-permute-start.19
  119.5 1.3 collective-permute-start.18
  120.8 26.9 %collective-permute-done.20.state_ref = bf16[2,32,1024]{2,1,0:T(8,128)(2,1)S(1)} collective-permute-done((bf16[2,32,1024]{2,1,0:T(8,128)(2,1)S(1)}, bf16[2,32,1024]{2,1,0:T(8,128)(2,1)S(1)}, u32[]{:S(2)}, u32[]{:S(2)}) %collective-permute-start.20) | collective-permute-done | bytes 131104 | tf_op jit(solution)/shard_map/ppermute | solution.py:254
  147.8 2.4 %stage.41.refs_2_ = bf16[5,16,3,32,128]{4,3,2,1,0:T(8,128)(2,1)S(1)} custom-call(s32[1]{0:T(128)} %bitcast.y_ref, bf16[2,32,1024]{2,1,0:T(8,128)(2,1)S(1)} %collective-permute-done.20.state_ref, bf16[4,1024,1024]{2,1,0:T(8,128)(2,1)S(1)} %turn.1.refs_0_, ...), custom_call_target="tpu_custom_call", output_to_operand_aliasing={{}: (4, {})} | custom-call | flops 536870912 | bytes 8912896 | tf_op jit(solution)/shard_map/stage/pallas_call | solution.py:167
  150.2 3.6 %collective-permute-done.19.state_ref = bf16[2,32,1024]{2,1,0:T(8,128)(2,1)S(1)} collective-permute-done((bf16[2,32,1024]{2,1,0:T(8,128)(2,1)S(1)}, bf16[2,32,1024]{2,1,0:T(8,128)(2,1)S(1)}, u32[]{:S(2)}, u32[]{:S(2)}) %collective-permute-start.19) | collective-permute-done | bytes 131104 | tf_op jit(solution)/shard_map/ppermute | solution.py:254
  153.8 2.4 %stage.42.refs_2_ = bf16[5,16,3,32,128]{4,3,2,1,0:T(8,128)(2,1)S(1)} custom-call(s32[1]{0:T(128)} %bitcast.y_ref, bf16[2,32,1024]{2,1,0:T(8,128)(2,1)S(1)} %collective-permute-done.19.state_ref, bf16[4,1024,1024]{2,1,0:T(8,128)(2,1)S(1)} %turn.1.refs_0_, ...), custom_call_target="tpu_custom_call", output_to_operand_aliasing={{}: (4, {})} | custom-call | flops 536870912 | bytes 8912896 | tf_op jit(solution)/shard_map/stage/pallas_call | solution.py:167
  156.2 1.6 collective-permute-done.18.state_ref
  157.8 2.4 %stage.43 = bf16[5,16,3,32,128]{4,3,2,1,0:T(8,128)(2,1)S(1)} custom-call(s32[1]{0:T(128)} %bitcast.y_ref, bf16[2,32,1024]{2,1,0:T(8,128)(2,1)S(1)} %collective-permute-done.18.state_ref, bf16[4,1024,1024]{2,1,0:T(8,128)(2,1)S(1)} %turn.1.refs_0_, f32[3,4,3,2,1024]{4,3,2,1,0:T(2,128)S(1)} %maximum_bitcast_fusion.refs_4_.refs_1_, ...), custom_call_target="tpu_custom_call", output_to_operand_aliasing={{}: (4, {})} | custom-call | flops 536870912 | bytes 8912896 | tf_op jit(solution)/shard_map/stage/pallas_call | solution.py:167
  160.5 50.4 %all_to_all.10 = bf16[64,96,128]{2,1,0:T(8,128)(2,1)S(1)} all-to-all(bf16[64,96,128]{2,1,0:T(8,128)(2,1)S(1)} %bitcast.21), channel_id=1, replica_groups=mesh['y'=8,'x'=4,'z'=8,'core'=2] {'x','z','core'}, dimensions={0} | all-to-all | bytes 3145728 | tf_op jit(solution)/shard_map/all_to_all | solution.py:257
  210.9 2.1 finish.1
  (58 shorter events, 8.8 us)
Async XLA Ops:
  6.5 86.3 %all-gather.4.cloned.1.call-start = ((), (), s32[]{:S(2)}) async-start(), calls=%async_computation.2 | async-start | bytes 8912896 | tf_op jit(solution)/shard_map/all_gather | solution.py:235
  19.1 18.7 %copy-start = (f32[6]{0:T(128)S(1)}, f32[6]{0:T(128)}, u32[]{:S(2)}) copy-start(f32[6]{0:T(128)} %param.5) | copy-start | bytes 76
  23.2 34.0 %all-to-all-start = ((bf16[16,112,128]{2,1,0:T(8,128)(2,1)}), bf16[16,112,128]{2,1,0:T(8,128)(2,1)S(1)}, u32[]{:S(2)}, u32[]{:S(2)}) async-start(bf16[16,112,128]{2,1,0:T(8,128)(2,1)} %bitcast.24), calls=%async_computation | async-start | bytes 917504 | tf_op jit(solution)/shard_map/all_to_all | solution.py:241
  96.6 7.2 %collective-permute-start.2 = (bf16[2,32,1024]{2,1,0:T(8,128)(2,1)S(1)}, bf16[2,32,1024]{2,1,0:T(8,128)(2,1)S(1)}, u32[]{:S(2)}, u32[]{:S(2)}) collective-permute-start(bf16[2,32,1024]{2,1,0:T(8,128)(2,1)S(1)} %get-tuple-element.51), channel_id=1, source_target_pairs={{0,64},{1,65},{2,66},{3,67},{4,68},{5,69},{6,70},{7,71},{8,72},{9,... | collective-permute-start | bytes 393224 | tf_op jit(solution)/shard_map/ppermute | solution.py:254
  97.3 7.4 %collective-permute-start.1 = (bf16[2,32,1024]{2,1,0:T(8,128)(2,1)S(1)}, bf16[2,32,1024]{2,1,0:T(8,128)(2,1)S(1)}, u32[]{:S(2)}, u32[]{:S(2)}) collective-permute-start(bf16[2,32,1024]{2,1,0:T(8,128)(2,1)S(1)} %get-tuple-element.50), channel_id=1, source_target_pairs={{0,64},{1,65},{2,66},{3,67},{4,68},{5,69},{6,70},{7,71},{8,72},{9,... | collective-permute-start | bytes 393224 | tf_op jit(solution)/shard_map/ppermute | solution.py:254
  98.0 7.5 %collective-permute-start = (bf16[2,32,1024]{2,1,0:T(8,128)(2,1)S(1)}, bf16[2,32,1024]{2,1,0:T(8,128)(2,1)S(1)}, u32[]{:S(2)}, u32[]{:S(2)}) collective-permute-start(bf16[2,32,1024]{2,1,0:T(8,128)(2,1)S(1)} %get-tuple-element.49), channel_id=1, source_target_pairs={{0,64},{1,65},{2,66},{3,67},{4,68},{5,69},{6,70},{7,71},{8,72},{9,... | collective-permute-start | bytes 393224 | tf_op jit(solution)/shard_map/ppermute | solution.py:254
  104.0 2.3 %collective-permute-start.5 = (bf16[2,32,1024]{2,1,0:T(8,128)(2,1)S(1)}, bf16[2,32,1024]{2,1,0:T(8,128)(2,1)S(1)}, u32[]{:S(2)}, u32[]{:S(2)}) collective-permute-start(bf16[2,32,1024]{2,1,0:T(8,128)(2,1)S(1)} %get-tuple-element.57), channel_id=1, source_target_pairs={{64,128},{65,129},{66,130},{67,131},{68,132},{69,133},{70,134},{71... | collective-permute-start | bytes 393224 | tf_op jit(solution)/shard_map/ppermute | solution.py:254
  104.8 2.3 %collective-permute-start.4 = (bf16[2,32,1024]{2,1,0:T(8,128)(2,1)S(1)}, bf16[2,32,1024]{2,1,0:T(8,128)(2,1)S(1)}, u32[]{:S(2)}, u32[]{:S(2)}) collective-permute-start(bf16[2,32,1024]{2,1,0:T(8,128)(2,1)S(1)} %get-tuple-element.56), channel_id=1, source_target_pairs={{64,128},{65,129},{66,130},{67,131},{68,132},{69,133},{70,134},{71... | collective-permute-start | bytes 393224 | tf_op jit(solution)/shard_map/ppermute | solution.py:254
  105.7 2.3 %collective-permute-start.3 = (bf16[2,32,1024]{2,1,0:T(8,128)(2,1)S(1)}, bf16[2,32,1024]{2,1,0:T(8,128)(2,1)S(1)}, u32[]{:S(2)}, u32[]{:S(2)}) collective-permute-start(bf16[2,32,1024]{2,1,0:T(8,128)(2,1)S(1)} %get-tuple-element.55), channel_id=1, source_target_pairs={{64,128},{65,129},{66,130},{67,131},{68,132},{69,133},{70,134},{71... | collective-permute-start | bytes 393224 | tf_op jit(solution)/shard_map/ppermute | solution.py:254
  106.5 2.3 %collective-permute-start.8 = (bf16[2,32,1024]{2,1,0:T(8,128)(2,1)S(1)}, bf16[2,32,1024]{2,1,0:T(8,128)(2,1)S(1)}, u32[]{:S(2)}, u32[]{:S(2)}) collective-permute-start(bf16[2,32,1024]{2,1,0:T(8,128)(2,1)S(1)} %get-tuple-element.63), channel_id=1, source_target_pairs={{128,192},{129,193},{130,194},{131,195},{132,196},{133,197},{134,1... | collective-permute-start | bytes 393224 | tf_op jit(solution)/shard_map/ppermute | solution.py:254
  107.3 2.3 %collective-permute-start.7 = (bf16[2,32,1024]{2,1,0:T(8,128)(2,1)S(1)}, bf16[2,32,1024]{2,1,0:T(8,128)(2,1)S(1)}, u32[]{:S(2)}, u32[]{:S(2)}) collective-permute-start(bf16[2,32,1024]{2,1,0:T(8,128)(2,1)S(1)} %get-tuple-element.62), channel_id=1, source_target_pairs={{128,192},{129,193},{130,194},{131,195},{132,196},{133,197},{134,1... | collective-permute-start | bytes 393224 | tf_op jit(solution)/shard_map/ppermute | solution.py:254
  108.1 2.3 %collective-permute-start.6 = (bf16[2,32,1024]{2,1,0:T(8,128)(2,1)S(1)}, bf16[2,32,1024]{2,1,0:T(8,128)(2,1)S(1)}, u32[]{:S(2)}, u32[]{:S(2)}) collective-permute-start(bf16[2,32,1024]{2,1,0:T(8,128)(2,1)S(1)} %get-tuple-element.61), channel_id=1, source_target_pairs={{128,192},{129,193},{130,194},{131,195},{132,196},{133,197},{134,1... | collective-permute-start | bytes 393224 | tf_op jit(solution)/shard_map/ppermute | solution.py:254
  109.0 2.3 %collective-permute-start.11 = (bf16[2,32,1024]{2,1,0:T(8,128)(2,1)S(1)}, bf16[2,32,1024]{2,1,0:T(8,128)(2,1)S(1)}, u32[]{:S(2)}, u32[]{:S(2)}) collective-permute-start(bf16[2,32,1024]{2,1,0:T(8,128)(2,1)S(1)} %get-tuple-element.69), channel_id=1, source_target_pairs={{192,256},{193,257},{194,258},{195,259},{196,260},{197,261},{198,2... | collective-permute-start | bytes 393224 | tf_op jit(solution)/shard_map/ppermute | solution.py:254
  109.8 2.3 %collective-permute-start.10 = (bf16[2,32,1024]{2,1,0:T(8,128)(2,1)S(1)}, bf16[2,32,1024]{2,1,0:T(8,128)(2,1)S(1)}, u32[]{:S(2)}, u32[]{:S(2)}) collective-permute-start(bf16[2,32,1024]{2,1,0:T(8,128)(2,1)S(1)} %get-tuple-element.68), channel_id=1, source_target_pairs={{192,256},{193,257},{194,258},{195,259},{196,260},{197,261},{198,2... | collective-permute-start | bytes 393224 | tf_op jit(solution)/shard_map/ppermute | solution.py:254
  110.6 2.3 %collective-permute-start.9 = (bf16[2,32,1024]{2,1,0:T(8,128)(2,1)S(1)}, bf16[2,32,1024]{2,1,0:T(8,128)(2,1)S(1)}, u32[]{:S(2)}, u32[]{:S(2)}) collective-permute-start(bf16[2,32,1024]{2,1,0:T(8,128)(2,1)S(1)} %get-tuple-element.67), channel_id=1, source_target_pairs={{192,256},{193,257},{194,258},{195,259},{196,260},{197,261},{198,2... | collective-permute-start | bytes 393224 | tf_op jit(solution)/shard_map/ppermute | solution.py:254
  111.5 2.3 %collective-permute-start.14 = (bf16[2,32,1024]{2,1,0:T(8,128)(2,1)S(1)}, bf16[2,32,1024]{2,1,0:T(8,128)(2,1)S(1)}, u32[]{:S(2)}, u32[]{:S(2)}) collective-permute-start(bf16[2,32,1024]{2,1,0:T(8,128)(2,1)S(1)} %get-tuple-element.75), channel_id=1, source_target_pairs={{256,320},{257,321},{258,322},{259,323},{260,324},{261,325},{262,3... | collective-permute-start | bytes 393224 | tf_op jit(solution)/shard_map/ppermute | solution.py:254
  112.3 2.3 %collective-permute-start.13 = (bf16[2,32,1024]{2,1,0:T(8,128)(2,1)S(1)}, bf16[2,32,1024]{2,1,0:T(8,128)(2,1)S(1)}, u32[]{:S(2)}, u32[]{:S(2)}) collective-permute-start(bf16[2,32,1024]{2,1,0:T(8,128)(2,1)S(1)} %get-tuple-element.74), channel_id=1, source_target_pairs={{256,320},{257,321},{258,322},{259,323},{260,324},{261,325},{262,3... | collective-permute-start | bytes 393224 | tf_op jit(solution)/shard_map/ppermute | solution.py:254
  113.1 2.3 %collective-permute-start.12 = (bf16[2,32,1024]{2,1,0:T(8,128)(2,1)S(1)}, bf16[2,32,1024]{2,1,0:T(8,128)(2,1)S(1)}, u32[]{:S(2)}, u32[]{:S(2)}) collective-permute-start(bf16[2,32,1024]{2,1,0:T(8,128)(2,1)S(1)} %get-tuple-element.73), channel_id=1, source_target_pairs={{256,320},{257,321},{258,322},{259,323},{260,324},{261,325},{262,3... | collective-permute-start | bytes 393224 | tf_op jit(solution)/shard_map/ppermute | solution.py:254
  113.9 2.3 %collective-permute-start.17 = (bf16[2,32,1024]{2,1,0:T(8,128)(2,1)S(1)}, bf16[2,32,1024]{2,1,0:T(8,128)(2,1)S(1)}, u32[]{:S(2)}, u32[]{:S(2)}) collective-permute-start(bf16[2,32,1024]{2,1,0:T(8,128)(2,1)S(1)} %get-tuple-element.81), channel_id=1, source_target_pairs={{320,384},{321,385},{322,386},{323,387},{324,388},{325,389},{326,3... | collective-permute-start | bytes 393224 | tf_op jit(solution)/shard_map/ppermute | solution.py:254
  114.8 3.0 %collective-permute-start.16 = (bf16[2,32,1024]{2,1,0:T(8,128)(2,1)S(1)}, bf16[2,32,1024]{2,1,0:T(8,128)(2,1)S(1)}, u32[]{:S(2)}, u32[]{:S(2)}) collective-permute-start(bf16[2,32,1024]{2,1,0:T(8,128)(2,1)S(1)} %get-tuple-element.80), channel_id=1, source_target_pairs={{320,384},{321,385},{322,386},{323,387},{324,388},{325,389},{326,3... | collective-permute-start | bytes 393224 | tf_op jit(solution)/shard_map/ppermute | solution.py:254
  115.6 3.8 %collective-permute-start.15 = (bf16[2,32,1024]{2,1,0:T(8,128)(2,1)S(1)}, bf16[2,32,1024]{2,1,0:T(8,128)(2,1)S(1)}, u32[]{:S(2)}, u32[]{:S(2)}) collective-permute-start(bf16[2,32,1024]{2,1,0:T(8,128)(2,1)S(1)} %get-tuple-element.79), channel_id=1, source_target_pairs={{320,384},{321,385},{322,386},{323,387},{324,388},{325,389},{326,3... | collective-permute-start | bytes 393224 | tf_op jit(solution)/shard_map/ppermute | solution.py:254
  116.4 31.3 %collective-permute-start.20 = (bf16[2,32,1024]{2,1,0:T(8,128)(2,1)S(1)}, bf16[2,32,1024]{2,1,0:T(8,128)(2,1)S(1)}, u32[]{:S(2)}, u32[]{:S(2)}) collective-permute-start(bf16[2,32,1024]{2,1,0:T(8,128)(2,1)S(1)} %get-tuple-element.87), channel_id=1, source_target_pairs={{384,448},{385,449},{386,450},{387,451},{388,452},{389,453},{390,4... | collective-permute-start | bytes 393224 | tf_op jit(solution)/shard_map/ppermute | solution.py:254
  117.9 35.9 %collective-permute-start.19 = (bf16[2,32,1024]{2,1,0:T(8,128)(2,1)S(1)}, bf16[2,32,1024]{2,1,0:T(8,128)(2,1)S(1)}, u32[]{:S(2)}, u32[]{:S(2)}) collective-permute-start(bf16[2,32,1024]{2,1,0:T(8,128)(2,1)S(1)} %get-tuple-element.86), channel_id=1, source_target_pairs={{384,448},{385,449},{386,450},{387,451},{388,452},{389,453},{390,4... | collective-permute-start | bytes 393224 | tf_op jit(solution)/shard_map/ppermute | solution.py:254
  119.5 38.3 %collective-permute-start.18 = (bf16[2,32,1024]{2,1,0:T(8,128)(2,1)S(1)}, bf16[2,32,1024]{2,1,0:T(8,128)(2,1)S(1)}, u32[]{:S(2)}, u32[]{:S(2)}) collective-permute-start(bf16[2,32,1024]{2,1,0:T(8,128)(2,1)S(1)} %get-tuple-element.85), channel_id=1, source_target_pairs={{384,448},{385,449},{386,450},{387,451},{388,452},{389,453},{390,4... | collective-permute-start | bytes 393224 | tf_op jit(solution)/shard_map/ppermute | solution.py:254
Sparse Core Ops, SparseCore 0:
  18.5 74.2 all-gather.3

commit v10 on v9

--- a/solution.py
+++ b/solution.py
@@ -94,51 +94,58 @@
     )(basis, basis, basis, basis)
 
 
-def stage_kernel(step, pieces, parts, handed, y_ref, state_ref, *refs):
+def rotate(now, rot, coef_ref, part, sector, first_row, rows, per):
+    for e in range(coef_ref.shape[3]):
+        cosine = coef_ref[part, sector, 0, pl.ds(e, 1), :]
+        ratio = coef_ref[part, sector, 1, pl.ds(e, 1), :]
+        product = coef_ref[part, sector, 2, pl.ds(e, 1), :]
+        upper = pl.ds(first_row + per * e, per)
+        lower = pl.ds(rows + first_row + per * e, per)
+        values = now[upper, :].astype(jnp.float32)
+        slopes = now[lower, :].astype(jnp.float32)
+        rot[upper, :] = (cosine * values + ratio * slopes).astype(rot.dtype)
+        rot[lower, :] = (cosine * slopes - product * values).astype(rot.dtype)
+
+
+def pair_up(fresh, rows, z):
+    low = lax.broadcasted_iota(jnp.int32, (rows, 128), 1) < 64
+    lanes = slice(128 * z, 128 * z + 128)
+    values = fresh[:rows, lanes]
+    slopes = fresh[rows:, lanes]
+    one = jnp.where(low, values, pltpu.roll(slopes, 64, 1)).astype(jnp.bfloat16)
+    two = jnp.where(low, pltpu.roll(values, 64, 1), slopes).astype(jnp.bfloat16)
+    return one, two
+
+
+def first_kernel(pieces, y_ref, state_ref, *refs):
     basis_refs, coef_ref = refs[:pieces], refs[pieces]
-    next_refs, (out_ref, now, rot) = refs[-3 - handed : -3], refs[-3:]
+    next_refs, (kept_ref, now, rot) = refs[pieces + 1 : -3], refs[-3:]
     s = pl.program_id(0)
-    energies = coef_ref.shape[3]
     rows, channels = state_ref.shape[1:]
-    own = rows // parts
-    per = own // energies
-
-    @pl.when(y_ref[0] == step)
+    own = rows // PARTS
+    per = own // coef_ref.shape[3]
+
+    @pl.when(y_ref[0] == 0)
     def _():
         @pl.when(s == 0)
         def _():
             now[pl.ds(0, rows)] = state_ref[0]
             now[pl.ds(rows, rows)] = state_ref[1]
 
-        for k in range(parts * energies):
-            part, e = divmod(k, energies)
-            cosine = coef_ref[part, 0, 0, pl.ds(e, 1), :]
-            ratio = coef_ref[part, 0, 1, pl.ds(e, 1), :]
-            product = coef_ref[part, 0, 2, pl.ds(e, 1), :]
-            values = now[pl.ds(per * k, per), :].astype(jnp.float32)
-            slopes = now[pl.ds(rows + per * k, per), :].astype(jnp.float32)
-            rot[pl.ds(per * k, per), :] = (cosine * values + ratio * slopes).astype(rot.dtype)
-            rot[pl.ds(rows + per * k, per), :] = (cosine * slopes - product * values).astype(rot.dtype)
-        low = lax.broadcasted_iota(jnp.int32, (rows, 128), 1) < 64
+        for part in range(PARTS):
+            rotate(now, rot, coef_ref, part, 0, own * part, rows, per)
         width = channels // pieces
         for q, basis_ref in enumerate(basis_refs):
-            if pieces == 1:
-                fresh = jnp.dot(rot[...], basis_ref[0], preferred_element_type=jnp.float32)
-            else:
-                block = basis_ref[...].reshape(width, channels)
-                fresh = lax.dot_general(
-                    rot[...], block, (((1,), (1,)), ((), ())), preferred_element_type=jnp.float32
-                )
+            block = basis_ref[...].reshape(width, channels)
+            fresh = lax.dot_general(
+                rot[...], block, (((1,), (1,)), ((), ())), preferred_element_type=jnp.float32
+            )
             now[:, pl.ds(width * q, width)] = fresh.astype(now.dtype)
             for k in range(width // 128):
                 z = width // 128 * q + k
-                lanes = slice(128 * k, 128 * k + 128)
-                values = fresh[:rows, lanes]
-                slopes = fresh[rows:, lanes]
-                one = jnp.where(low, values, pltpu.roll(slopes, 64, 1)).astype(out_ref.dtype)
-                two = jnp.where(low, pltpu.roll(values, 64, 1), slopes).astype(out_ref.dtype)
-                out_ref[0, 2 * z] = one.reshape(parts, own, 128)
-                out_ref[0, 2 * z + 1] = two.reshape(parts, own, 128)
+                one, two = pair_up(fresh, rows, k)
+                kept_ref[0, 2 * z] = one.reshape(PARTS, own, 128)
+                kept_ref[0, 2 * z + 1] = two.reshape(PARTS, own, 128)
 
         @pl.when(s == pl.num_programs(0) - 1)
         def _():
@@ -147,56 +154,81 @@
                 next_ref[1] = now[pl.ds(rows + own * part, own)]
 
 
-def stage(step, part, last, y_index, state, basis, coefs, kept):
+def first_stage(y_index, state, basis, coefs):
     sectors = coefs.shape[1]
     _, rows, channels = state.shape
-    first = step == 0
-    pieces, parts = (4, PARTS) if first else (1, 1)
-    own = rows // parts
-    handed = 0 if last else parts
-    if first:
-        groups, _, share, _ = basis.shape
-        block = (groups // pieces, 1, share, channels)
-        basis_specs = [pl.BlockSpec(block, lambda s, y, q=q: (q, s, 0, 0)) for q in range(pieces)]
-    else:
-        basis_specs = [
-            pl.BlockSpec(
-                (1, channels, channels), lambda s, y: (jnp.where(y[0] == step, s, 0), 0, 0)
-            )
-        ]
+    pieces = 4
+    own = rows // PARTS
+    groups, _, share, _ = basis.shape
+    block = (groups // pieces, 1, share, channels)
     outs = pl.pallas_call(
-        functools.partial(stage_kernel, step, pieces, parts, handed),
+        functools.partial(first_kernel, pieces),
         grid_spec=pltpu.PrefetchScalarGridSpec(
             num_scalar_prefetch=1,
             grid=(sectors,),
             in_specs=[pl.BlockSpec(state.shape, lambda s, y: (0, 0, 0))]
-            + basis_specs
-            + [pl.BlockSpec((parts, 1) + coefs.shape[2:], lambda s, y: (part, s, 0, 0, 0))]
-            + ([] if first else [pl.BlockSpec(memory_space=pl.ANY)]),
-            out_specs=[pl.BlockSpec((2, own, channels), lambda s, y: (0, 0, 0))] * handed
-            + [
-                pl.BlockSpec(
-                    (1, 16, parts, own, 128),
-                    lambda s, y: (jnp.where(y[0] == step, s, sectors), 0, part, 0, 0),
-                ),
-            ],
-            scratch_shapes=[
-                pltpu.VMEM((2 * rows, channels), state.dtype),
-                pltpu.VMEM((2 * rows, channels), state.dtype),
-            ],
+            + [pl.BlockSpec(block, lambda s, y, q=q: (q, s, 0, 0)) for q in range(pieces)]
+            + [pl.BlockSpec((PARTS, 1) + coefs.shape[2:], lambda s, y: (0, s, 0, 0, 0))],
+            out_specs=[pl.BlockSpec((2, own, channels), lambda s, y: (0, 0, 0))] * PARTS
+            + [pl.BlockSpec((1, groups, PARTS, own, 128), lambda s, y: (s, 0, 0, 0, 0))],
+            scratch_shapes=[pltpu.VMEM((2 * rows, channels), state.dtype)] * 2,
         ),
-        out_shape=[jax.ShapeDtypeStruct((2, own, channels), state.dtype)] * handed
-        + [jax.ShapeDtypeStruct((sectors + 1, 16, PARTS, own, 128), state.dtype)],
-        input_output_aliases={} if first else {4: handed},
-        compiler_params=pltpu.CompilerParams(vmem_limit_bytes=(48 if first else 16) * MIB),
+        out_shape=[jax.ShapeDtypeStruct((2, own, channels), state.dtype)] * PARTS
+        + [jax.ShapeDtypeStruct((sectors, groups, PARTS, own, 128), state.dtype)],
+        compiler_params=pltpu.CompilerParams(vmem_limit_bytes=48 * MIB),
+        cost_estimate=pl.CostEstimate(
+            flops=4 * sectors * rows * channels * channels,
+            bytes_accessed=2 * sectors * channels * (channels + 2 * rows),
+            transcendentals=0,
+        ),
+        name="first_stage",
+    )(y_index, state, *[basis] * pieces, coefs)
+    return list(outs[:-1]), outs[-1]
+
+
+def stage_kernel(step, part, y_ref, state_ref, basis_ref, coef_ref, *refs):
+    next_refs, (kept_ref, now, rot) = refs[1:-3], refs[-3:]
+    rows, channels = state_ref.shape[1:]
+    sectors = basis_ref.shape[0]
+    per = rows // coef_ref.shape[3]
+
+    @pl.when(y_ref[0] == step)
+    def _():
+        now[pl.ds(0, rows)] = state_ref[0]
+        now[pl.ds(rows, rows)] = state_ref[1]
+        for s in range(sectors):
+            rotate(now, rot, coef_ref, part, s, 0, rows, per)
+            fresh = jnp.dot(rot[...], basis_ref[s], preferred_element_type=jnp.float32)
+            if s < sectors - 1 or next_refs:
+                now[...] = fresh.astype(now.dtype)
+            for z in range(channels // 128):
+                kept_ref[s, 2 * z, part], kept_ref[s, 2 * z + 1, part] = pair_up(fresh, rows, z)
+        for next_ref in next_refs:
+            next_ref[0] = now[pl.ds(0, rows)]
+            next_ref[1] = now[pl.ds(rows, rows)]
+
+
+def stage(step, part, last, y_index, state, basis, coefs, kept):
+    sectors = coefs.shape[1]
+    _, rows, channels = state.shape
+    handed = 0 if last else 1
+    whole = pl.BlockSpec(memory_space=pltpu.VMEM)
+    return pl.pallas_call(
+        functools.partial(stage_kernel, step, part),
+        in_specs=[pl.BlockSpec(memory_space=pltpu.SMEM)] + [whole] * 4,
+        out_specs=[whole] * (handed + 1),
+        out_shape=[jax.ShapeDtypeStruct(state.shape, state.dtype)] * handed
+        + [jax.ShapeDtypeStruct(kept.shape, kept.dtype)],
+        scratch_shapes=[pltpu.VMEM((2 * rows, channels), state.dtype)] * 2,
+        input_output_aliases={4: handed},
+        compiler_params=pltpu.CompilerParams(vmem_limit_bytes=24 * MIB),
         cost_estimate=pl.CostEstimate(
             flops=4 * sectors * rows * channels * channels,
             bytes_accessed=2 * sectors * channels * (channels + 2 * rows),
             transcendentals=0,
         ),
         name="stage",
-    )(y_index, state, *[basis] * pieces, coefs, *([] if first else [kept]))
-    return list(outs[:-1]), outs[-1]
+    )(y_index, state, basis, coefs, kept)
 
 
 def finish_kernel(in_ref, out_ref):
@@ -246,15 +278,15 @@
     coefs = coefs.reshape(4, 3, PARTS, count // PARTS, channels).transpose(2, 0, 1, 3, 4)
     blocks, coefs = lax.optimization_barrier((blocks, coefs))
     state = join(blocks, rows)
-    states, kept = stage(0, 0, False, y_index, state, basis, coefs, None)
+    states, kept = first_stage(y_index, state, basis, coefs)
     basis = turn(basis)
     for step in range(1, planes):
         last = step == planes - 1
         for part in range(PARTS):
             state = lax.ppermute(states[part], "y", [(step - 1, step)])
-            fresh, kept = stage(step, part, last, y_index, state, basis, coefs, kept)
+            *fresh, kept = stage(step, part, last, y_index, state, basis, coefs, kept)
             states[part] = None if last else fresh[0]
-    back = lax.all_to_all(kept[:4].reshape(64, rows, lanes), PLANE, 0, 0)
+    back = lax.all_to_all(kept.reshape(64, rows, lanes), PLANE, 0, 0)
     return finish(back.reshape(64, count, per, lanes))[None]
 
 

time: 221 us -> 216 us (0.977)
  Pallas kernels: 24.9 us -> 21.2 us
    pallas_call x22, Pallas kernels: 13.4 us -> 9.63 us  [the longest x21 5.83 us: stage(): pl.pallas_call(functools.partial(stage_kernel, step, part), in_specs=[pl....]
  transfers between devices with their start and end apart: 23 -> 23, of which waited for: 5 -> 5; matrix products, arithmetic and copies ran while one was open for 1% -> 1% of each run, Pallas kernels for 8% -> 6%
where the time goes in v10:
time: 216 us; the launch traced here: 215 us
  waiting for transfers between devices  84.3 us (39%)
  blocking collectives  60.2 us (28%)
  starting transfers between devices  30.5 us (14%)
  Pallas kernels  21.2 us (10%)
  between operations  13.9 us (6%)
  other arithmetic  2.74 us (1%)
    all_to_all x1, blocking collectives, per_device(): back = lax.all_to_all(kept.reshape(64, rows, lanes), PLANE, 0, 0)  50.2 us
    all_gather x1, waiting for transfers between devices, per_device(): basis = lax.all_gather(ring[:, :share], CH_AXES)  33.4 us
    ppermute x21, waiting for transfers between devices, per_device(): state = lax.ppermute(states[part], 'y', [(step - 1, step)])  31.5 us
    all_to_all x1, waiting for transfers between devices, per_device(): lax.all_to_all(blocks.reshape(16, rows + per, lanes), CH_AXES, 0, 0)  19.4 us
    ppermute x21, starting transfers between devices, per_device(): state = lax.ppermute(states[part], 'y', [(step - 1, step)])  15.9 us
    all_to_all x1, starting transfers between devices, per_device(): lax.all_to_all(blocks.reshape(16, rows + per, lanes), CH_AXES, 0, 0)  14.6 us
    all_gather x1, blocking collectives, per_device(): ring = lax.all_gather(jnp.concatenate([intersection[0], extra]), 'x')  10 us
    pallas_call x21, Pallas kernels, stage(): pl.pallas_call(functools.partial(stage_kernel, step, part), in_specs=[pl....  5.83 us
  transfers between devices with their start and end apart: 23, of which 5 were waited for; matrix products, arithmetic and copies ran while one was open for 1% of the time, Pallas kernels for 6%

profile of v10, /device:TPU:63, one launch (start us, length us, event | category | flops | bytes accessed | tf_op | source)
XLA Modules:
  0.0 214.7 jit_solution(16763307750835360627)
XLA Ops:
  6.5 0.9 fusion.1
  7.5 10.0 %all-gather = bf16[288,1024]{1,0:T(8,128)(2,1)S(1)} all-gather(bf16[72,1024]{1,0:T(8,128)(2,1)S(1)} %fusion.1), channel_id=2, replica_groups=mesh['y'=8,'x'=4,'z'=8,'core'=2] {'x'}, dimensions={0}, use_global_device_ids=true | all-gather | bytes 737280 | tf_op jit(solution)/shard_map/all_gather | solution.py:266
  17.5 0.8 slice.14
  19.1 4.1 %spread.1 = bf16[16,7,16,128]{3,2,1,0:T(8,128)(2,1)} custom-call(s32[1]{0:T(128)} %bitcast.1.x_ref, bf16[6,64,2048]{2,1,0:T(8,128)(2,1)} %p_ref.1, bf16[6,64,2048]{2,1,0:T(8,128)(2,1)} %p_ref.1, bf16[16,128]{1,0:T(8,128)(2,1)} %pad.9.limit_ref), custom_call_target="tpu_custom_call" | custom-call | tf_op jit(solution)/shard_map/spread/pallas_call | solution.py:36
  23.2 14.6 %all-to-all-start = ((bf16[16,112,128]{2,1,0:T(8,128)(2,1)}), bf16[16,112,128]{2,1,0:T(8,128)(2,1)S(1)}, u32[]{:S(2)}, u32[]{:S(2)}) async-start(bf16[16,112,128]{2,1,0:T(8,128)(2,1)} %bitcast.24), calls=%async_computation | async-start | bytes 917504 | tf_op jit(solution)/shard_map/all_to_all | solution.py:273
  37.9 19.4 %all-to-all-done.in_ref = bf16[16,112,128]{2,1,0:T(8,128)(2,1)S(1)} async-done(((bf16[16,112,128]{2,1,0:T(8,128)(2,1)}), bf16[16,112,128]{2,1,0:T(8,128)(2,1)S(1)}, u32[]{:S(2)}, u32[]{:S(2)}) %all-to-all-start) | async-done | bytes 458784 | tf_op jit(solution)/shard_map/all_to_all | solution.py:273
  57.4 1.7 fusion.5
  59.4 33.4 %all-gather.4.cloned.1.call-done = bf16[64,64,1024]{2,1,0:T(8,128)(2,1)} async-done(((bf16[4,64,1024]{2,1,0:T(8,128)(2,1)}), bf16[64,64,1024]{2,1,0:T(8,128)(2,1)}) %all-gather.4.cloned.1.call-update) | async-done | bytes 8388624 | tf_op jit(solution)/shard_map/all_gather | solution.py:267
  92.8 3.8 %first_stage.1 = (bf16[2,32,1024]{2,1,0:T(8,128)(2,1)S(1)}, bf16[2,32,1024]{2,1,0:T(8,128)(2,1)S(1)}, bf16[2,32,1024]{2,1,0:T(8,128)(2,1)S(1)}, bf16[4,16,3,32,128]{4,3,2,1,0:T(8,128)(2,1)S(1)}) custom-call(s32[1]{0:T(128)} %bitcast.y_ref, bf16[2,96,1024]{2,1,0:T(8,128)(2,1)S(1)} %join.1.state_ref, bf16[16,4,64,1024]{3,2,1,0:T(8,128)(2,1)} %bitcast.14, ...), custom_call_target="tpu_custom_call" | custom-call | flops 1610612736 | bytes 9961472 | tf_op jit(solution)/shard_map/first_stage/pallas_call | solution.py:164
  97.3 0.7 collective-permute-start.1
  98.0 0.7 collective-permute-start
  98.6 5.2 %turn.1.basis_ref = bf16[4,1024,1024]{2,1,0:T(8,128)(2,1)S(1)} custom-call(bf16[16,4,64,1024]{3,2,1,0:T(8,128)(2,1)} %bitcast.18, bf16[16,4,64,1024]{3,2,1,0:T(8,128)(2,1)} %bitcast.19, bf16[16,4,64,1024]{3,2,1,0:T(8,128)(2,1)} %bitcast.20, bf16[16,4,64,1024]{3,2,1,0:T(8,128)(2,1)} %bitcast.21), custom_call_target="tpu_custom_call" | custom-call | bytes 8388608 | tf_op jit(solution)/shard_map/turn/pallas_call | solution.py:85
  103.9 0.7 collective-permute-start.5
  104.6 0.7 collective-permute-start.4
  105.3 0.7 collective-permute-start.3
  106.0 0.7 collective-permute-start.8
  106.7 0.7 collective-permute-start.7
  107.4 0.7 collective-permute-start.6
  110.4 0.7 collective-permute-start.14
  111.8 0.7 collective-permute-start.12
  113.2 0.7 collective-permute-start.16
  114.9 1.3 collective-permute-start.20
  116.2 1.3 collective-permute-start.19
  117.5 1.3 collective-permute-start.18
  118.8 25.1 %collective-permute-done.20.state_ref = bf16[2,32,1024]{2,1,0:T(8,128)(2,1)S(1)} collective-permute-done((bf16[2,32,1024]{2,1,0:T(8,128)(2,1)S(1)}, bf16[2,32,1024]{2,1,0:T(8,128)(2,1)S(1)}, u32[]{:S(2)}, u32[]{:S(2)}) %collective-permute-start.20) | collective-permute-done | bytes 131104 | tf_op jit(solution)/shard_map/ppermute | solution.py:286
  143.9 1.7 stage.39.refs_0_
  145.7 4.5 %collective-permute-done.19.state_ref = bf16[2,32,1024]{2,1,0:T(8,128)(2,1)S(1)} collective-permute-done((bf16[2,32,1024]{2,1,0:T(8,128)(2,1)S(1)}, bf16[2,32,1024]{2,1,0:T(8,128)(2,1)S(1)}, u32[]{:S(2)}, u32[]{:S(2)}) %collective-permute-start.19) | collective-permute-done | bytes 131104 | tf_op jit(solution)/shard_map/ppermute | solution.py:286
  150.1 1.8 stage.40.refs_0_
  151.9 1.9 collective-permute-done.18.state_ref
  153.8 1.7 stage.41
  155.6 50.2 %all_to_all.10 = bf16[64,96,128]{2,1,0:T(8,128)(2,1)S(1)} all-to-all(bf16[64,96,128]{2,1,0:T(8,128)(2,1)S(1)} %bitcast.12), channel_id=1, replica_groups=mesh['y'=8,'x'=4,'z'=8,'core'=2] {'x','z','core'}, dimensions={0} | all-to-all | bytes 3145728 | tf_op jit(solution)/shard_map/all_to_all | solution.py:289
  205.8 2.1 finish.1
  (57 shorter events, 6.6 us)
Async XLA Ops:
  6.5 86.3 %all-gather.4.cloned.1.call-start = ((), (), s32[]{:S(2)}) async-start(), calls=%async_computation.2 | async-start | bytes 8912896 | tf_op jit(solution)/shard_map/all_gather | solution.py:267
  19.1 18.7 %copy-start = (f32[6]{0:T(128)S(1)}, f32[6]{0:T(128)}, u32[]{:S(2)}) copy-start(f32[6]{0:T(128)} %param.5) | copy-start | bytes 76
  23.2 34.0 %all-to-all-start = ((bf16[16,112,128]{2,1,0:T(8,128)(2,1)}), bf16[16,112,128]{2,1,0:T(8,128)(2,1)S(1)}, u32[]{:S(2)}, u32[]{:S(2)}) async-start(bf16[16,112,128]{2,1,0:T(8,128)(2,1)} %bitcast.24), calls=%async_computation | async-start | bytes 917504 | tf_op jit(solution)/shard_map/all_to_all | solution.py:273
  96.6 7.2 %collective-permute-start.2 = (bf16[2,32,1024]{2,1,0:T(8,128)(2,1)S(1)}, bf16[2,32,1024]{2,1,0:T(8,128)(2,1)S(1)}, u32[]{:S(2)}, u32[]{:S(2)}) collective-permute-start(bf16[2,32,1024]{2,1,0:T(8,128)(2,1)S(1)} %get-tuple-element.51), channel_id=1, source_target_pairs={{0,64},{1,65},{2,66},{3,67},{4,68},{5,69},{6,70},{7,71},{8,72},{9,... | collective-permute-start | bytes 393224 | tf_op jit(solution)/shard_map/ppermute | solution.py:286
  97.3 7.3 %collective-permute-start.1 = (bf16[2,32,1024]{2,1,0:T(8,128)(2,1)S(1)}, bf16[2,32,1024]{2,1,0:T(8,128)(2,1)S(1)}, u32[]{:S(2)}, u32[]{:S(2)}) collective-permute-start(bf16[2,32,1024]{2,1,0:T(8,128)(2,1)S(1)} %get-tuple-element.50), channel_id=1, source_target_pairs={{0,64},{1,65},{2,66},{3,67},{4,68},{5,69},{6,70},{7,71},{8,72},{9,... | collective-permute-start | bytes 393224 | tf_op jit(solution)/shard_map/ppermute | solution.py:286
  98.0 7.3 %collective-permute-start = (bf16[2,32,1024]{2,1,0:T(8,128)(2,1)S(1)}, bf16[2,32,1024]{2,1,0:T(8,128)(2,1)S(1)}, u32[]{:S(2)}, u32[]{:S(2)}) collective-permute-start(bf16[2,32,1024]{2,1,0:T(8,128)(2,1)S(1)} %get-tuple-element.49), channel_id=1, source_target_pairs={{0,64},{1,65},{2,66},{3,67},{4,68},{5,69},{6,70},{7,71},{8,72},{9,... | collective-permute-start | bytes 393224 | tf_op jit(solution)/shard_map/ppermute | solution.py:286
  103.9 2.1 collective-permute-start.5
  104.6 2.1 collective-permute-start.4
  105.3 2.1 collective-permute-start.3
  106.0 2.1 collective-permute-start.8
  106.7 2.3 %collective-permute-start.7 = (bf16[2,32,1024]{2,1,0:T(8,128)(2,1)S(1)}, bf16[2,32,1024]{2,1,0:T(8,128)(2,1)S(1)}, u32[]{:S(2)}, u32[]{:S(2)}) collective-permute-start(bf16[2,32,1024]{2,1,0:T(8,128)(2,1)S(1)} %get-tuple-element.62), channel_id=1, source_target_pairs={{128,192},{129,193},{130,194},{131,195},{132,196},{133,197},{134,1... | collective-permute-start | bytes 393224 | tf_op jit(solution)/shard_map/ppermute | solution.py:286
  107.4 2.3 %collective-permute-start.6 = (bf16[2,32,1024]{2,1,0:T(8,128)(2,1)S(1)}, bf16[2,32,1024]{2,1,0:T(8,128)(2,1)S(1)}, u32[]{:S(2)}, u32[]{:S(2)}) collective-permute-start(bf16[2,32,1024]{2,1,0:T(8,128)(2,1)S(1)} %get-tuple-element.61), channel_id=1, source_target_pairs={{128,192},{129,193},{130,194},{131,195},{132,196},{133,197},{134,1... | collective-permute-start | bytes 393224 | tf_op jit(solution)/shard_map/ppermute | solution.py:286
  108.3 2.1 collective-permute-start.11
  109.0 2.1 collective-permute-start.10
  109.7 2.1 collective-permute-start.9
  110.4 2.1 collective-permute-start.14
  111.1 2.1 collective-permute-start.13
  111.8 2.1 collective-permute-start.12
  112.5 2.3 %collective-permute-start.17 = (bf16[2,32,1024]{2,1,0:T(8,128)(2,1)S(1)}, bf16[2,32,1024]{2,1,0:T(8,128)(2,1)S(1)}, u32[]{:S(2)}, u32[]{:S(2)}) collective-permute-start(bf16[2,32,1024]{2,1,0:T(8,128)(2,1)S(1)} %get-tuple-element.81), channel_id=1, source_target_pairs={{320,384},{321,385},{322,386},{323,387},{324,388},{325,389},{326,3... | collective-permute-start | bytes 393224 | tf_op jit(solution)/shard_map/ppermute | solution.py:286
  113.2 2.9 %collective-permute-start.16 = (bf16[2,32,1024]{2,1,0:T(8,128)(2,1)S(1)}, bf16[2,32,1024]{2,1,0:T(8,128)(2,1)S(1)}, u32[]{:S(2)}, u32[]{:S(2)}) collective-permute-start(bf16[2,32,1024]{2,1,0:T(8,128)(2,1)S(1)} %get-tuple-element.80), channel_id=1, source_target_pairs={{320,384},{321,385},{322,386},{323,387},{324,388},{325,389},{326,3... | collective-permute-start | bytes 393224 | tf_op jit(solution)/shard_map/ppermute | solution.py:286
  114.2 3.3 %collective-permute-start.15 = (bf16[2,32,1024]{2,1,0:T(8,128)(2,1)S(1)}, bf16[2,32,1024]{2,1,0:T(8,128)(2,1)S(1)}, u32[]{:S(2)}, u32[]{:S(2)}) collective-permute-start(bf16[2,32,1024]{2,1,0:T(8,128)(2,1)S(1)} %get-tuple-element.79), channel_id=1, source_target_pairs={{320,384},{321,385},{322,386},{323,387},{324,388},{325,389},{326,3... | collective-permute-start | bytes 393224 | tf_op jit(solution)/shard_map/ppermute | solution.py:286
  114.9 29.0 %collective-permute-start.20 = (bf16[2,32,1024]{2,1,0:T(8,128)(2,1)S(1)}, bf16[2,32,1024]{2,1,0:T(8,128)(2,1)S(1)}, u32[]{:S(2)}, u32[]{:S(2)}) collective-permute-start(bf16[2,32,1024]{2,1,0:T(8,128)(2,1)S(1)} %get-tuple-element.87), channel_id=1, source_target_pairs={{384,448},{385,449},{386,450},{387,451},{388,452},{389,453},{390,4... | collective-permute-start | bytes 393224 | tf_op jit(solution)/shard_map/ppermute | solution.py:286
  116.2 34.0 %collective-permute-start.19 = (bf16[2,32,1024]{2,1,0:T(8,128)(2,1)S(1)}, bf16[2,32,1024]{2,1,0:T(8,128)(2,1)S(1)}, u32[]{:S(2)}, u32[]{:S(2)}) collective-permute-start(bf16[2,32,1024]{2,1,0:T(8,128)(2,1)S(1)} %get-tuple-element.86), channel_id=1, source_target_pairs={{384,448},{385,449},{386,450},{387,451},{388,452},{389,453},{390,4... | collective-permute-start | bytes 393224 | tf_op jit(solution)/shard_map/ppermute | solution.py:286
  117.5 36.3 %collective-permute-start.18 = (bf16[2,32,1024]{2,1,0:T(8,128)(2,1)S(1)}, bf16[2,32,1024]{2,1,0:T(8,128)(2,1)S(1)}, u32[]{:S(2)}, u32[]{:S(2)}) collective-permute-start(bf16[2,32,1024]{2,1,0:T(8,128)(2,1)S(1)} %get-tuple-element.85), channel_id=1, source_target_pairs={{384,448},{385,449},{386,450},{387,451},{388,452},{389,453},{390,4... | collective-permute-start | bytes 393224 | tf_op jit(solution)/shard_map/ppermute | solution.py:286
Sparse Core Ops, SparseCore 0:
  18.5 74.3 all-gather.3

commit v11 on v10

--- a/solution.py
+++ b/solution.py
@@ -232,23 +232,21 @@
 
 
 def finish_kernel(in_ref, out_ref):
-    groups, energies, per, lanes = in_ref.shape
+    groups, _, per, lanes = in_ref.shape
     half = lanes // 2
     cols = groups * per
-    for e in range(energies):
-        turned = in_ref[:, e].reshape(cols, lanes).T
-        out_ref[e, :, pl.ds(0, cols)] = turned[:half]
-        out_ref[e, :, pl.ds(cols, cols)] = turned[half:]
+    turned = in_ref[:, pl.program_id(0)].reshape(cols, lanes).T
+    out_ref[0, :, pl.ds(0, cols)] = turned[:half]
+    out_ref[0, :, pl.ds(cols, cols)] = turned[half:]
 
 
 def finish(pieces):
     groups, energies, per, lanes = pieces.shape
-    batch = 2
     return pl.pallas_call(
         finish_kernel,
-        grid=(energies // batch,),
-        in_specs=[pl.BlockSpec((groups, batch, per, lanes), lambda e: (0, e, 0, 0))],
-        out_specs=pl.BlockSpec((batch, lanes // 2, 2 * groups * per), lambda e: (e, 0, 0)),
+        grid=(energies,),
+        in_specs=[pl.BlockSpec(memory_space=pltpu.VMEM)],
+        out_specs=pl.BlockSpec((1, lanes // 2, 2 * groups * per), lambda e: (e, 0, 0)),
         out_shape=jax.ShapeDtypeStruct((energies, lanes // 2, 2 * groups * per), pieces.dtype),
         compiler_params=pltpu.CompilerParams(vmem_limit_bytes=16 * MIB),
         name="finish",

time: 216 us -> 216 us (level)
  no operation moved by 1% of the time
where the time goes in v11:
time: 216 us; the launch traced here: 215 us
  waiting for transfers between devices  84.3 us (39%)
  blocking collectives  60.2 us (28%)
  starting transfers between devices  30.5 us (14%)
  Pallas kernels  21.7 us (10%)
  between operations  13.9 us (6%)
  other arithmetic  2.74 us (1%)
    all_to_all x1, blocking collectives, per_device(): back = lax.all_to_all(kept.reshape(64, rows, lanes), PLANE, 0, 0)  50.2 us
    all_gather x1, waiting for transfers between devices, per_device(): basis = lax.all_gather(ring[:, :share], CH_AXES)  33.4 us
    ppermute x21, waiting for transfers between devices, per_device(): state = lax.ppermute(states[part], 'y', [(step - 1, step)])  31.5 us
    all_to_all x1, waiting for transfers between devices, per_device(): lax.all_to_all(blocks.reshape(16, rows + per, lanes), CH_AXES, 0, 0)  19.4 us
    ppermute x21, starting transfers between devices, per_device(): state = lax.ppermute(states[part], 'y', [(step - 1, step)])  15.9 us
    all_to_all x1, starting transfers between devices, per_device(): lax.all_to_all(blocks.reshape(16, rows + per, lanes), CH_AXES, 0, 0)  14.6 us
    all_gather x1, blocking collectives, per_device(): ring = lax.all_gather(jnp.concatenate([intersection[0], extra]), 'x')  10 us
    pallas_call x21, Pallas kernels, stage(): pl.pallas_call(functools.partial(stage_kernel, step, part), in_specs=[pl....  5.83 us
  transfers between devices with their start and end apart: 23, of which 5 were waited for; matrix products, arithmetic and copies ran while one was open for 1% of the time, Pallas kernels for 6%

profile of v11, /device:TPU:63, one launch (start us, length us, event | category | flops | bytes accessed | tf_op | source)
XLA Modules:
  0.0 215.2 jit_solution(14658122692517337162)
XLA Ops:
  6.5 0.9 fusion.1
  7.5 10.0 %all-gather = bf16[288,1024]{1,0:T(8,128)(2,1)S(1)} all-gather(bf16[72,1024]{1,0:T(8,128)(2,1)S(1)} %fusion.1), channel_id=2, replica_groups=mesh['y'=8,'x'=4,'z'=8,'core'=2] {'x'}, dimensions={0}, use_global_device_ids=true | all-gather | bytes 737280 | tf_op jit(solution)/shard_map/all_gather | solution.py:264
  17.5 0.8 slice.14
  19.1 4.1 %spread.1 = bf16[16,7,16,128]{3,2,1,0:T(8,128)(2,1)} custom-call(s32[1]{0:T(128)} %bitcast.1.x_ref, bf16[6,64,2048]{2,1,0:T(8,128)(2,1)} %p_ref.1, bf16[6,64,2048]{2,1,0:T(8,128)(2,1)} %p_ref.1, bf16[16,128]{1,0:T(8,128)(2,1)} %pad.9.limit_ref), custom_call_target="tpu_custom_call" | custom-call | tf_op jit(solution)/shard_map/spread/pallas_call | solution.py:36
  23.2 14.6 %all-to-all-start = ((bf16[16,112,128]{2,1,0:T(8,128)(2,1)}), bf16[16,112,128]{2,1,0:T(8,128)(2,1)S(1)}, u32[]{:S(2)}, u32[]{:S(2)}) async-start(bf16[16,112,128]{2,1,0:T(8,128)(2,1)} %bitcast.24), calls=%async_computation | async-start | bytes 917504 | tf_op jit(solution)/shard_map/all_to_all | solution.py:271
  37.9 19.4 %all-to-all-done.in_ref = bf16[16,112,128]{2,1,0:T(8,128)(2,1)S(1)} async-done(((bf16[16,112,128]{2,1,0:T(8,128)(2,1)}), bf16[16,112,128]{2,1,0:T(8,128)(2,1)S(1)}, u32[]{:S(2)}, u32[]{:S(2)}) %all-to-all-start) | async-done | bytes 458784 | tf_op jit(solution)/shard_map/all_to_all | solution.py:271
  57.4 1.7 fusion.5
  59.4 33.4 %all-gather.4.cloned.1.call-done = bf16[64,64,1024]{2,1,0:T(8,128)(2,1)} async-done(((bf16[4,64,1024]{2,1,0:T(8,128)(2,1)}), bf16[64,64,1024]{2,1,0:T(8,128)(2,1)}) %all-gather.4.cloned.1.call-update) | async-done | bytes 8388624 | tf_op jit(solution)/shard_map/all_gather | solution.py:265
  92.8 3.8 %first_stage.1 = (bf16[2,32,1024]{2,1,0:T(8,128)(2,1)S(1)}, bf16[2,32,1024]{2,1,0:T(8,128)(2,1)S(1)}, bf16[2,32,1024]{2,1,0:T(8,128)(2,1)S(1)}, bf16[4,16,3,32,128]{4,3,2,1,0:T(8,128)(2,1)S(1)}) custom-call(s32[1]{0:T(128)} %bitcast.y_ref, bf16[2,96,1024]{2,1,0:T(8,128)(2,1)S(1)} %join.1.state_ref, bf16[16,4,64,1024]{3,2,1,0:T(8,128)(2,1)} %bitcast.14, ...), custom_call_target="tpu_custom_call" | custom-call | flops 1610612736 | bytes 9961472 | tf_op jit(solution)/shard_map/first_stage/pallas_call | solution.py:164
  97.3 0.7 collective-permute-start.1
  98.0 0.7 collective-permute-start
  98.6 5.2 %turn.1.basis_ref = bf16[4,1024,1024]{2,1,0:T(8,128)(2,1)S(1)} custom-call(bf16[16,4,64,1024]{3,2,1,0:T(8,128)(2,1)} %bitcast.18, bf16[16,4,64,1024]{3,2,1,0:T(8,128)(2,1)} %bitcast.19, bf16[16,4,64,1024]{3,2,1,0:T(8,128)(2,1)} %bitcast.20, bf16[16,4,64,1024]{3,2,1,0:T(8,128)(2,1)} %bitcast.21), custom_call_target="tpu_custom_call" | custom-call | bytes 8388608 | tf_op jit(solution)/shard_map/turn/pallas_call | solution.py:85
  103.9 0.7 collective-permute-start.5
  104.6 0.7 collective-permute-start.4
  105.3 0.7 collective-permute-start.3
  106.0 0.7 collective-permute-start.8
  107.4 0.7 collective-permute-start.6
  109.0 0.7 collective-permute-start.10
  110.4 0.7 collective-permute-start.14
  111.8 0.7 collective-permute-start.12
  113.2 0.7 collective-permute-start.16
  114.9 1.3 collective-permute-start.20
  116.2 1.3 collective-permute-start.19
  117.5 1.3 collective-permute-start.18
  118.8 25.1 %collective-permute-done.20.state_ref = bf16[2,32,1024]{2,1,0:T(8,128)(2,1)S(1)} collective-permute-done((bf16[2,32,1024]{2,1,0:T(8,128)(2,1)S(1)}, bf16[2,32,1024]{2,1,0:T(8,128)(2,1)S(1)}, u32[]{:S(2)}, u32[]{:S(2)}) %collective-permute-start.20) | collective-permute-done | bytes 131104 | tf_op jit(solution)/shard_map/ppermute | solution.py:284
  143.9 1.7 stage.39.refs_0_
  145.7 4.5 %collective-permute-done.19.state_ref = bf16[2,32,1024]{2,1,0:T(8,128)(2,1)S(1)} collective-permute-done((bf16[2,32,1024]{2,1,0:T(8,128)(2,1)S(1)}, bf16[2,32,1024]{2,1,0:T(8,128)(2,1)S(1)}, u32[]{:S(2)}, u32[]{:S(2)}) %collective-permute-start.19) | collective-permute-done | bytes 131104 | tf_op jit(solution)/shard_map/ppermute | solution.py:284
  150.1 1.8 stage.40.refs_0_
  151.9 1.9 collective-permute-done.18.state_ref
  153.8 1.7 stage.41
  155.6 50.2 %all_to_all.10 = bf16[64,96,128]{2,1,0:T(8,128)(2,1)S(1)} all-to-all(bf16[64,96,128]{2,1,0:T(8,128)(2,1)S(1)} %bitcast.12), channel_id=1, replica_groups=mesh['y'=8,'x'=4,'z'=8,'core'=2] {'x','z','core'}, dimensions={0} | all-to-all | bytes 3145728 | tf_op jit(solution)/shard_map/all_to_all | solution.py:287
  205.8 2.6 %finish.1 = bf16[6,64,2048]{2,1,0:T(8,128)(2,1)} custom-call(bf16[64,6,16,128]{3,2,1,0:T(8,128)(2,1)S(1)} %bitcast.13), custom_call_target="tpu_custom_call" | custom-call | tf_op jit(solution)/shard_map/finish/pallas_call | solution.py:245
  (57 shorter events, 6.6 us)
Async XLA Ops:
  6.5 86.3 %all-gather.4.cloned.1.call-start = ((), (), s32[]{:S(2)}) async-start(), calls=%async_computation.2 | async-start | bytes 8912896 | tf_op jit(solution)/shard_map/all_gather | solution.py:265
  19.1 18.7 %copy-start = (f32[6]{0:T(128)S(1)}, f32[6]{0:T(128)}, u32[]{:S(2)}) copy-start(f32[6]{0:T(128)} %param.5) | copy-start | bytes 76
  23.2 34.0 %all-to-all-start = ((bf16[16,112,128]{2,1,0:T(8,128)(2,1)}), bf16[16,112,128]{2,1,0:T(8,128)(2,1)S(1)}, u32[]{:S(2)}, u32[]{:S(2)}) async-start(bf16[16,112,128]{2,1,0:T(8,128)(2,1)} %bitcast.24), calls=%async_computation | async-start | bytes 917504 | tf_op jit(solution)/shard_map/all_to_all | solution.py:271
  96.6 7.2 %collective-permute-start.2 = (bf16[2,32,1024]{2,1,0:T(8,128)(2,1)S(1)}, bf16[2,32,1024]{2,1,0:T(8,128)(2,1)S(1)}, u32[]{:S(2)}, u32[]{:S(2)}) collective-permute-start(bf16[2,32,1024]{2,1,0:T(8,128)(2,1)S(1)} %get-tuple-element.51), channel_id=1, source_target_pairs={{0,64},{1,65},{2,66},{3,67},{4,68},{5,69},{6,70},{7,71},{8,72},{9,... | collective-permute-start | bytes 393224 | tf_op jit(solution)/shard_map/ppermute | solution.py:284
  97.3 7.3 %collective-permute-start.1 = (bf16[2,32,1024]{2,1,0:T(8,128)(2,1)S(1)}, bf16[2,32,1024]{2,1,0:T(8,128)(2,1)S(1)}, u32[]{:S(2)}, u32[]{:S(2)}) collective-permute-start(bf16[2,32,1024]{2,1,0:T(8,128)(2,1)S(1)} %get-tuple-element.50), channel_id=1, source_target_pairs={{0,64},{1,65},{2,66},{3,67},{4,68},{5,69},{6,70},{7,71},{8,72},{9,... | collective-permute-start | bytes 393224 | tf_op jit(solution)/shard_map/ppermute | solution.py:284
  98.0 7.3 %collective-permute-start = (bf16[2,32,1024]{2,1,0:T(8,128)(2,1)S(1)}, bf16[2,32,1024]{2,1,0:T(8,128)(2,1)S(1)}, u32[]{:S(2)}, u32[]{:S(2)}) collective-permute-start(bf16[2,32,1024]{2,1,0:T(8,128)(2,1)S(1)} %get-tuple-element.49), channel_id=1, source_target_pairs={{0,64},{1,65},{2,66},{3,67},{4,68},{5,69},{6,70},{7,71},{8,72},{9,... | collective-permute-start | bytes 393224 | tf_op jit(solution)/shard_map/ppermute | solution.py:284
  103.9 2.1 collective-permute-start.5
  104.6 2.1 collective-permute-start.4
  105.3 2.1 collective-permute-start.3
  106.0 2.1 collective-permute-start.8
  106.7 2.3 %collective-permute-start.7 = (bf16[2,32,1024]{2,1,0:T(8,128)(2,1)S(1)}, bf16[2,32,1024]{2,1,0:T(8,128)(2,1)S(1)}, u32[]{:S(2)}, u32[]{:S(2)}) collective-permute-start(bf16[2,32,1024]{2,1,0:T(8,128)(2,1)S(1)} %get-tuple-element.62), channel_id=1, source_target_pairs={{128,192},{129,193},{130,194},{131,195},{132,196},{133,197},{134,1... | collective-permute-start | bytes 393224 | tf_op jit(solution)/shard_map/ppermute | solution.py:284
  107.4 2.3 %collective-permute-start.6 = (bf16[2,32,1024]{2,1,0:T(8,128)(2,1)S(1)}, bf16[2,32,1024]{2,1,0:T(8,128)(2,1)S(1)}, u32[]{:S(2)}, u32[]{:S(2)}) collective-permute-start(bf16[2,32,1024]{2,1,0:T(8,128)(2,1)S(1)} %get-tuple-element.61), channel_id=1, source_target_pairs={{128,192},{129,193},{130,194},{131,195},{132,196},{133,197},{134,1... | collective-permute-start | bytes 393224 | tf_op jit(solution)/shard_map/ppermute | solution.py:284
  108.3 2.1 collective-permute-start.11
  109.0 2.1 collective-permute-start.10
  109.7 2.1 collective-permute-start.9
  110.4 2.1 collective-permute-start.14
  111.1 2.1 collective-permute-start.13
  111.8 2.1 collective-permute-start.12
  112.5 2.3 %collective-permute-start.17 = (bf16[2,32,1024]{2,1,0:T(8,128)(2,1)S(1)}, bf16[2,32,1024]{2,1,0:T(8,128)(2,1)S(1)}, u32[]{:S(2)}, u32[]{:S(2)}) collective-permute-start(bf16[2,32,1024]{2,1,0:T(8,128)(2,1)S(1)} %get-tuple-element.81), channel_id=1, source_target_pairs={{320,384},{321,385},{322,386},{323,387},{324,388},{325,389},{326,3... | collective-permute-start | bytes 393224 | tf_op jit(solution)/shard_map/ppermute | solution.py:284
  113.2 2.9 %collective-permute-start.16 = (bf16[2,32,1024]{2,1,0:T(8,128)(2,1)S(1)}, bf16[2,32,1024]{2,1,0:T(8,128)(2,1)S(1)}, u32[]{:S(2)}, u32[]{:S(2)}) collective-permute-start(bf16[2,32,1024]{2,1,0:T(8,128)(2,1)S(1)} %get-tuple-element.80), channel_id=1, source_target_pairs={{320,384},{321,385},{322,386},{323,387},{324,388},{325,389},{326,3... | collective-permute-start | bytes 393224 | tf_op jit(solution)/shard_map/ppermute | solution.py:284
  114.2 3.3 %collective-permute-start.15 = (bf16[2,32,1024]{2,1,0:T(8,128)(2,1)S(1)}, bf16[2,32,1024]{2,1,0:T(8,128)(2,1)S(1)}, u32[]{:S(2)}, u32[]{:S(2)}) collective-permute-start(bf16[2,32,1024]{2,1,0:T(8,128)(2,1)S(1)} %get-tuple-element.79), channel_id=1, source_target_pairs={{320,384},{321,385},{322,386},{323,387},{324,388},{325,389},{326,3... | collective-permute-start | bytes 393224 | tf_op jit(solution)/shard_map/ppermute | solution.py:284
  114.9 29.0 %collective-permute-start.20 = (bf16[2,32,1024]{2,1,0:T(8,128)(2,1)S(1)}, bf16[2,32,1024]{2,1,0:T(8,128)(2,1)S(1)}, u32[]{:S(2)}, u32[]{:S(2)}) collective-permute-start(bf16[2,32,1024]{2,1,0:T(8,128)(2,1)S(1)} %get-tuple-element.87), channel_id=1, source_target_pairs={{384,448},{385,449},{386,450},{387,451},{388,452},{389,453},{390,4... | collective-permute-start | bytes 393224 | tf_op jit(solution)/shard_map/ppermute | solution.py:284
  116.2 34.0 %collective-permute-start.19 = (bf16[2,32,1024]{2,1,0:T(8,128)(2,1)S(1)}, bf16[2,32,1024]{2,1,0:T(8,128)(2,1)S(1)}, u32[]{:S(2)}, u32[]{:S(2)}) collective-permute-start(bf16[2,32,1024]{2,1,0:T(8,128)(2,1)S(1)} %get-tuple-element.86), channel_id=1, source_target_pairs={{384,448},{385,449},{386,450},{387,451},{388,452},{389,453},{390,4... | collective-permute-start | bytes 393224 | tf_op jit(solution)/shard_map/ppermute | solution.py:284
  117.5 36.3 %collective-permute-start.18 = (bf16[2,32,1024]{2,1,0:T(8,128)(2,1)S(1)}, bf16[2,32,1024]{2,1,0:T(8,128)(2,1)S(1)}, u32[]{:S(2)}, u32[]{:S(2)}) collective-permute-start(bf16[2,32,1024]{2,1,0:T(8,128)(2,1)S(1)} %get-tuple-element.85), channel_id=1, source_target_pairs={{384,448},{385,449},{386,450},{387,451},{388,452},{389,453},{390,4... | collective-permute-start | bytes 393224 | tf_op jit(solution)/shard_map/ppermute | solution.py:284
Sparse Core Ops, SparseCore 0:
  18.5 74.3 all-gather.3

commit v12 on v10

--- a/solution.py
+++ b/solution.py
@@ -135,17 +135,18 @@
         for part in range(PARTS):
             rotate(now, rot, coef_ref, part, 0, own * part, rows, per)
         width = channels // pieces
-        for q, basis_ref in enumerate(basis_refs):
-            block = basis_ref[...].reshape(width, channels)
-            fresh = lax.dot_general(
-                rot[...], block, (((1,), (1,)), ((), ())), preferred_element_type=jnp.float32
-            )
-            now[:, pl.ds(width * q, width)] = fresh.astype(now.dtype)
-            for k in range(width // 128):
-                z = width // 128 * q + k
-                one, two = pair_up(fresh, rows, k)
-                kept_ref[0, 2 * z] = one.reshape(PARTS, own, 128)
-                kept_ref[0, 2 * z + 1] = two.reshape(PARTS, own, 128)
+        blocks = [ref[...].reshape(width, channels) for ref in basis_refs]
+        fresh = lax.dot_general(
+            rot[...],
+            jnp.concatenate(blocks, axis=0),
+            (((1,), (1,)), ((), ())),
+            preferred_element_type=jnp.float32,
+        )
+        now[...] = fresh.astype(now.dtype)
+        for z in range(channels // 128):
+            one, two = pair_up(fresh, rows, z)
+            kept_ref[0, 2 * z] = one.reshape(PARTS, own, 128)
+            kept_ref[0, 2 * z + 1] = two.reshape(PARTS, own, 128)
 
         @pl.when(s == pl.num_programs(0) - 1)
         def _():
@@ -232,11 +233,13 @@
 
 
 def finish_kernel(in_ref, out_ref):
-    groups, energies, per, lanes = in_ref.shape
+    groups, _, per, lanes = in_ref.shape
+    batch = out_ref.shape[0]
     half = lanes // 2
     cols = groups * per
-    for e in range(energies):
-        turned = in_ref[:, e].reshape(cols, lanes).T
+    for e in range(batch):
+        block = in_ref[:, batch * pl.program_id(0) + e]
+        turned = block.reshape(cols, lanes).T
         out_ref[e, :, pl.ds(0, cols)] = turned[:half]
         out_ref[e, :, pl.ds(cols, cols)] = turned[half:]
 
@@ -247,7 +250,7 @@
     return pl.pallas_call(
         finish_kernel,
         grid=(energies // batch,),
-        in_specs=[pl.BlockSpec((groups, batch, per, lanes), lambda e: (0, e, 0, 0))],
+        in_specs=[pl.BlockSpec(memory_space=pltpu.VMEM)],
         out_specs=pl.BlockSpec((batch, lanes // 2, 2 * groups * per), lambda e: (e, 0, 0)),
         out_shape=jax.ShapeDtypeStruct((energies, lanes // 2, 2 * groups * per), pieces.dtype),
         compiler_params=pltpu.CompilerParams(vmem_limit_bytes=16 * MIB),

time: 216 us -> 216 us (level)
  no operation moved by 1% of the time
where the time goes in v12:
time: 216 us; the launch traced here: 215 us
  waiting for transfers between devices  84.3 us (39%)
  blocking collectives  60.2 us (28%)
  starting transfers between devices  30.5 us (14%)
  Pallas kernels  21.1 us (10%)
  between operations  13.9 us (6%)
  other arithmetic  2.74 us (1%)
    all_to_all x1, blocking collectives, per_device(): back = lax.all_to_all(kept.reshape(64, rows, lanes), PLANE, 0, 0)  50.2 us
    all_gather x1, waiting for transfers between devices, per_device(): basis = lax.all_gather(ring[:, :share], CH_AXES)  33.4 us
    ppermute x21, waiting for transfers between devices, per_device(): state = lax.ppermute(states[part], 'y', [(step - 1, step)])  31.5 us
    all_to_all x1, waiting for transfers between devices, per_device(): lax.all_to_all(blocks.reshape(16, rows + per, lanes), CH_AXES, 0, 0)  19.4 us
    ppermute x21, starting transfers between devices, per_device(): state = lax.ppermute(states[part], 'y', [(step - 1, step)])  15.9 us
    all_to_all x1, starting transfers between devices, per_device(): lax.all_to_all(blocks.reshape(16, rows + per, lanes), CH_AXES, 0, 0)  14.6 us
    all_gather x1, blocking collectives, per_device(): ring = lax.all_gather(jnp.concatenate([intersection[0], extra]), 'x')  10 us
    pallas_call x21, Pallas kernels, stage(): pl.pallas_call(functools.partial(stage_kernel, step, part), in_specs=[pl....  5.83 us
  transfers between devices with their start and end apart: 23, of which 5 were waited for; matrix products, arithmetic and copies ran while one was open for 1% of the time, Pallas kernels for 6%

profile of v12, /device:TPU:63, one launch (start us, length us, event | category | flops | bytes accessed | tf_op | source)
XLA Modules:
  0.0 214.6 jit_solution(12197023492598307164)
XLA Ops:
  6.5 0.9 fusion.1
  7.5 10.0 %all-gather = bf16[288,1024]{1,0:T(8,128)(2,1)S(1)} all-gather(bf16[72,1024]{1,0:T(8,128)(2,1)S(1)} %fusion.1), channel_id=2, replica_groups=mesh['y'=8,'x'=4,'z'=8,'core'=2] {'x'}, dimensions={0}, use_global_device_ids=true | all-gather | bytes 737280 | tf_op jit(solution)/shard_map/all_gather | solution.py:269
  17.5 0.8 slice.14
  19.1 4.1 %spread.1 = bf16[16,7,16,128]{3,2,1,0:T(8,128)(2,1)} custom-call(s32[1]{0:T(128)} %bitcast.1.x_ref, bf16[6,64,2048]{2,1,0:T(8,128)(2,1)} %p_ref.1, bf16[6,64,2048]{2,1,0:T(8,128)(2,1)} %p_ref.1, bf16[16,128]{1,0:T(8,128)(2,1)} %pad.9.limit_ref), custom_call_target="tpu_custom_call" | custom-call | tf_op jit(solution)/shard_map/spread/pallas_call | solution.py:36
  23.2 14.6 %all-to-all-start = ((bf16[16,112,128]{2,1,0:T(8,128)(2,1)}), bf16[16,112,128]{2,1,0:T(8,128)(2,1)S(1)}, u32[]{:S(2)}, u32[]{:S(2)}) async-start(bf16[16,112,128]{2,1,0:T(8,128)(2,1)} %bitcast.24), calls=%async_computation | async-start | bytes 917504 | tf_op jit(solution)/shard_map/all_to_all | solution.py:276
  37.9 19.4 %all-to-all-done.in_ref = bf16[16,112,128]{2,1,0:T(8,128)(2,1)S(1)} async-done(((bf16[16,112,128]{2,1,0:T(8,128)(2,1)}), bf16[16,112,128]{2,1,0:T(8,128)(2,1)S(1)}, u32[]{:S(2)}, u32[]{:S(2)}) %all-to-all-start) | async-done | bytes 458784 | tf_op jit(solution)/shard_map/all_to_all | solution.py:276
  57.4 1.7 fusion.5
  59.4 33.4 %all-gather.4.cloned.1.call-done = bf16[64,64,1024]{2,1,0:T(8,128)(2,1)} async-done(((bf16[4,64,1024]{2,1,0:T(8,128)(2,1)}), bf16[64,64,1024]{2,1,0:T(8,128)(2,1)}) %all-gather.4.cloned.1.call-update) | async-done | bytes 8388624 | tf_op jit(solution)/shard_map/all_gather | solution.py:270
  92.8 3.8 %first_stage.1 = (bf16[2,32,1024]{2,1,0:T(8,128)(2,1)S(1)}, bf16[2,32,1024]{2,1,0:T(8,128)(2,1)S(1)}, bf16[2,32,1024]{2,1,0:T(8,128)(2,1)S(1)}, bf16[4,16,3,32,128]{4,3,2,1,0:T(8,128)(2,1)S(1)}) custom-call(s32[1]{0:T(128)} %bitcast.y_ref, bf16[2,96,1024]{2,1,0:T(8,128)(2,1)S(1)} %join.1.state_ref, bf16[16,4,64,1024]{3,2,1,0:T(8,128)(2,1)} %bitcast.14, ...), custom_call_target="tpu_custom_call" | custom-call | flops 1610612736 | bytes 9961472 | tf_op jit(solution)/shard_map/first_stage/pallas_call | solution.py:165
  97.3 0.7 collective-permute-start.1
  98.0 0.7 collective-permute-start
  98.6 5.2 %turn.1.basis_ref = bf16[4,1024,1024]{2,1,0:T(8,128)(2,1)S(1)} custom-call(bf16[16,4,64,1024]{3,2,1,0:T(8,128)(2,1)} %bitcast.18, bf16[16,4,64,1024]{3,2,1,0:T(8,128)(2,1)} %bitcast.19, bf16[16,4,64,1024]{3,2,1,0:T(8,128)(2,1)} %bitcast.20, bf16[16,4,64,1024]{3,2,1,0:T(8,128)(2,1)} %bitcast.21), custom_call_target="tpu_custom_call" | custom-call | bytes 8388608 | tf_op jit(solution)/shard_map/turn/pallas_call | solution.py:85
  103.9 0.7 collective-permute-start.5
  104.6 0.7 collective-permute-start.4
  105.3 0.7 collective-permute-start.3
  106.0 0.7 collective-permute-start.8
  106.7 0.7 collective-permute-start.7
  107.4 0.7 collective-permute-start.6
  110.4 0.7 collective-permute-start.14
  111.8 0.7 collective-permute-start.12
  113.2 0.7 collective-permute-start.16
  114.9 1.3 collective-permute-start.20
  116.2 1.3 collective-permute-start.19
  117.5 1.3 collective-permute-start.18
  118.8 25.1 %collective-permute-done.20.state_ref = bf16[2,32,1024]{2,1,0:T(8,128)(2,1)S(1)} collective-permute-done((bf16[2,32,1024]{2,1,0:T(8,128)(2,1)S(1)}, bf16[2,32,1024]{2,1,0:T(8,128)(2,1)S(1)}, u32[]{:S(2)}, u32[]{:S(2)}) %collective-permute-start.20) | collective-permute-done | bytes 131104 | tf_op jit(solution)/shard_map/ppermute | solution.py:289
  143.9 1.7 stage.39.refs_0_
  145.7 4.5 %collective-permute-done.19.state_ref = bf16[2,32,1024]{2,1,0:T(8,128)(2,1)S(1)} collective-permute-done((bf16[2,32,1024]{2,1,0:T(8,128)(2,1)S(1)}, bf16[2,32,1024]{2,1,0:T(8,128)(2,1)S(1)}, u32[]{:S(2)}, u32[]{:S(2)}) %collective-permute-start.19) | collective-permute-done | bytes 131104 | tf_op jit(solution)/shard_map/ppermute | solution.py:289
  150.1 1.8 stage.40.refs_0_
  151.9 1.9 collective-permute-done.18.state_ref
  153.8 1.7 stage.41
  155.6 50.2 %all_to_all.10 = bf16[64,96,128]{2,1,0:T(8,128)(2,1)S(1)} all-to-all(bf16[64,96,128]{2,1,0:T(8,128)(2,1)S(1)} %bitcast.12), channel_id=1, replica_groups=mesh['y'=8,'x'=4,'z'=8,'core'=2] {'x','z','core'}, dimensions={0} | all-to-all | bytes 3145728 | tf_op jit(solution)/shard_map/all_to_all | solution.py:292
  205.8 2.0 finish.1
  (57 shorter events, 6.6 us)
Async XLA Ops:
  6.5 86.3 %all-gather.4.cloned.1.call-start = ((), (), s32[]{:S(2)}) async-start(), calls=%async_computation.2 | async-start | bytes 8912896 | tf_op jit(solution)/shard_map/all_gather | solution.py:270
  19.1 18.7 %copy-start = (f32[6]{0:T(128)S(1)}, f32[6]{0:T(128)}, u32[]{:S(2)}) copy-start(f32[6]{0:T(128)} %param.5) | copy-start | bytes 76
  23.2 34.0 %all-to-all-start = ((bf16[16,112,128]{2,1,0:T(8,128)(2,1)}), bf16[16,112,128]{2,1,0:T(8,128)(2,1)S(1)}, u32[]{:S(2)}, u32[]{:S(2)}) async-start(bf16[16,112,128]{2,1,0:T(8,128)(2,1)} %bitcast.24), calls=%async_computation | async-start | bytes 917504 | tf_op jit(solution)/shard_map/all_to_all | solution.py:276
  96.6 7.2 %collective-permute-start.2 = (bf16[2,32,1024]{2,1,0:T(8,128)(2,1)S(1)}, bf16[2,32,1024]{2,1,0:T(8,128)(2,1)S(1)}, u32[]{:S(2)}, u32[]{:S(2)}) collective-permute-start(bf16[2,32,1024]{2,1,0:T(8,128)(2,1)S(1)} %get-tuple-element.51), channel_id=1, source_target_pairs={{0,64},{1,65},{2,66},{3,67},{4,68},{5,69},{6,70},{7,71},{8,72},{9,... | collective-permute-start | bytes 393224 | tf_op jit(solution)/shard_map/ppermute | solution.py:289
  97.3 7.3 %collective-permute-start.1 = (bf16[2,32,1024]{2,1,0:T(8,128)(2,1)S(1)}, bf16[2,32,1024]{2,1,0:T(8,128)(2,1)S(1)}, u32[]{:S(2)}, u32[]{:S(2)}) collective-permute-start(bf16[2,32,1024]{2,1,0:T(8,128)(2,1)S(1)} %get-tuple-element.50), channel_id=1, source_target_pairs={{0,64},{1,65},{2,66},{3,67},{4,68},{5,69},{6,70},{7,71},{8,72},{9,... | collective-permute-start | bytes 393224 | tf_op jit(solution)/shard_map/ppermute | solution.py:289
  98.0 7.3 %collective-permute-start = (bf16[2,32,1024]{2,1,0:T(8,128)(2,1)S(1)}, bf16[2,32,1024]{2,1,0:T(8,128)(2,1)S(1)}, u32[]{:S(2)}, u32[]{:S(2)}) collective-permute-start(bf16[2,32,1024]{2,1,0:T(8,128)(2,1)S(1)} %get-tuple-element.49), channel_id=1, source_target_pairs={{0,64},{1,65},{2,66},{3,67},{4,68},{5,69},{6,70},{7,71},{8,72},{9,... | collective-permute-start | bytes 393224 | tf_op jit(solution)/shard_map/ppermute | solution.py:289
  103.9 2.1 collective-permute-start.5
  104.6 2.1 collective-permute-start.4
  105.3 2.1 collective-permute-start.3
  106.0 2.1 collective-permute-start.8
  106.7 2.3 %collective-permute-start.7 = (bf16[2,32,1024]{2,1,0:T(8,128)(2,1)S(1)}, bf16[2,32,1024]{2,1,0:T(8,128)(2,1)S(1)}, u32[]{:S(2)}, u32[]{:S(2)}) collective-permute-start(bf16[2,32,1024]{2,1,0:T(8,128)(2,1)S(1)} %get-tuple-element.62), channel_id=1, source_target_pairs={{128,192},{129,193},{130,194},{131,195},{132,196},{133,197},{134,1... | collective-permute-start | bytes 393224 | tf_op jit(solution)/shard_map/ppermute | solution.py:289
  107.4 2.3 %collective-permute-start.6 = (bf16[2,32,1024]{2,1,0:T(8,128)(2,1)S(1)}, bf16[2,32,1024]{2,1,0:T(8,128)(2,1)S(1)}, u32[]{:S(2)}, u32[]{:S(2)}) collective-permute-start(bf16[2,32,1024]{2,1,0:T(8,128)(2,1)S(1)} %get-tuple-element.61), channel_id=1, source_target_pairs={{128,192},{129,193},{130,194},{131,195},{132,196},{133,197},{134,1... | collective-permute-start | bytes 393224 | tf_op jit(solution)/shard_map/ppermute | solution.py:289
  108.3 2.1 collective-permute-start.11
  109.0 2.1 collective-permute-start.10
  109.7 2.1 collective-permute-start.9
  110.4 2.1 collective-permute-start.14
  111.1 2.1 collective-permute-start.13
  111.8 2.1 collective-permute-start.12
  112.5 2.3 %collective-permute-start.17 = (bf16[2,32,1024]{2,1,0:T(8,128)(2,1)S(1)}, bf16[2,32,1024]{2,1,0:T(8,128)(2,1)S(1)}, u32[]{:S(2)}, u32[]{:S(2)}) collective-permute-start(bf16[2,32,1024]{2,1,0:T(8,128)(2,1)S(1)} %get-tuple-element.81), channel_id=1, source_target_pairs={{320,384},{321,385},{322,386},{323,387},{324,388},{325,389},{326,3... | collective-permute-start | bytes 393224 | tf_op jit(solution)/shard_map/ppermute | solution.py:289
  113.2 2.9 %collective-permute-start.16 = (bf16[2,32,1024]{2,1,0:T(8,128)(2,1)S(1)}, bf16[2,32,1024]{2,1,0:T(8,128)(2,1)S(1)}, u32[]{:S(2)}, u32[]{:S(2)}) collective-permute-start(bf16[2,32,1024]{2,1,0:T(8,128)(2,1)S(1)} %get-tuple-element.80), channel_id=1, source_target_pairs={{320,384},{321,385},{322,386},{323,387},{324,388},{325,389},{326,3... | collective-permute-start | bytes 393224 | tf_op jit(solution)/shard_map/ppermute | solution.py:289
  114.2 3.3 %collective-permute-start.15 = (bf16[2,32,1024]{2,1,0:T(8,128)(2,1)S(1)}, bf16[2,32,1024]{2,1,0:T(8,128)(2,1)S(1)}, u32[]{:S(2)}, u32[]{:S(2)}) collective-permute-start(bf16[2,32,1024]{2,1,0:T(8,128)(2,1)S(1)} %get-tuple-element.79), channel_id=1, source_target_pairs={{320,384},{321,385},{322,386},{323,387},{324,388},{325,389},{326,3... | collective-permute-start | bytes 393224 | tf_op jit(solution)/shard_map/ppermute | solution.py:289
  114.9 29.0 %collective-permute-start.20 = (bf16[2,32,1024]{2,1,0:T(8,128)(2,1)S(1)}, bf16[2,32,1024]{2,1,0:T(8,128)(2,1)S(1)}, u32[]{:S(2)}, u32[]{:S(2)}) collective-permute-start(bf16[2,32,1024]{2,1,0:T(8,128)(2,1)S(1)} %get-tuple-element.87), channel_id=1, source_target_pairs={{384,448},{385,449},{386,450},{387,451},{388,452},{389,453},{390,4... | collective-permute-start | bytes 393224 | tf_op jit(solution)/shard_map/ppermute | solution.py:289
  116.2 34.0 %collective-permute-start.19 = (bf16[2,32,1024]{2,1,0:T(8,128)(2,1)S(1)}, bf16[2,32,1024]{2,1,0:T(8,128)(2,1)S(1)}, u32[]{:S(2)}, u32[]{:S(2)}) collective-permute-start(bf16[2,32,1024]{2,1,0:T(8,128)(2,1)S(1)} %get-tuple-element.86), channel_id=1, source_target_pairs={{384,448},{385,449},{386,450},{387,451},{388,452},{389,453},{390,4... | collective-permute-start | bytes 393224 | tf_op jit(solution)/shard_map/ppermute | solution.py:289
  117.5 36.3 %collective-permute-start.18 = (bf16[2,32,1024]{2,1,0:T(8,128)(2,1)S(1)}, bf16[2,32,1024]{2,1,0:T(8,128)(2,1)S(1)}, u32[]{:S(2)}, u32[]{:S(2)}) collective-permute-start(bf16[2,32,1024]{2,1,0:T(8,128)(2,1)S(1)} %get-tuple-element.85), channel_id=1, source_target_pairs={{384,448},{385,449},{386,450},{387,451},{388,452},{389,453},{390,4... | collective-permute-start | bytes 393224 | tf_op jit(solution)/shard_map/ppermute | solution.py:289
Sparse Core Ops, SparseCore 0:
  18.5 74.3 all-gather.3
